TPU v7x, 32 devices: a whole 2x2x4 slice. The times are simulated.
32 devices in a mesh: clip: 4 (over y, x), space: 8 (over z, core).
Axes of the slice: x: 2, y: 2, z: 4, core: 2. Of those that a mesh axis runs over, the one named last changes fastest.
Arguments:
- clip_input: bfloat16 [16, 16, 14, 14, 1024], P('clip', 'space'), may hold values from -6 to 6
- frame_counts: int32 [16], P('clip'), may hold values from 2 to 16, as said below
- third_down: bfloat16 [1024, 256], replicated, may hold values from -0.1875 to 0.1875
- third_depth: float32 [256, 27], replicated, may hold values from -1.25 to 1.25
- third_up: bfloat16 [256, 1024], replicated, may hold values from -0.375 to 0.375
- third_gain: float32 [1024], replicated, may hold values from 0.25 to 1.75
- third_shift: float32 [1024], replicated, may hold values from -3 to 3
- fourth_down: bfloat16 [1024, 512], replicated, may hold values from -0.1875 to 0.1875
- fourth_skip: bfloat16 [1024, 2048], replicated, may hold values from -0.1875 to 0.1875
- fourth_depth: float32 [512, 27], replicated, may hold values from -1.25 to 1.25
- fourth_up: bfloat16 [512, 2048], replicated, may hold values from -0.25 to 0.25
- fourth_gain: float32 [2048], replicated, may hold values from 0.25 to 1.75
- fourth_shift: float32 [2048], replicated, may hold values from -3 to 3
- classifier: bfloat16 [2048, 400], replicated, may hold values from -0.125 to 0.125
- class_bias: float32 [400], replicated, may hold values from -3 to 3
- logit_grad: float32 [16, 400], replicated, may hold values from -6 to 6
Outputs:
- logits: float32 [16, 400], P('clip')
- clip_grad: bfloat16 [16, 16, 14, 14, 1024], P('clip', 'space')
- third_down_grad: float32 [1024, 256], P(('clip', 'space'))
- third_depth_grad: float32 [256, 27], P(('clip', 'space'))
- third_up_grad: float32 [256, 1024], P(('clip', 'space'))
- third_gain_grad: float32 [1024], P(('clip', 'space'))
- third_shift_grad: float32 [1024], P(('clip', 'space'))
- fourth_down_grad: float32 [1024, 512], P(('clip', 'space'))
- fourth_skip_grad: float32 [1024, 2048], P(('clip', 'space'))
- fourth_depth_grad: float32 [512, 27], P(('clip', 'space'))
- fourth_up_grad: float32 [512, 2048], P(('clip', 'space'))
- fourth_gain_grad: float32 [2048], P(('clip', 'space'))
- fourth_shift_grad: float32 [2048], P(('clip', 'space'))
- classifier_grad: float32 [2048, 400], P(('clip', 'space'))
- class_bias_grad: float32 [400], replicated
Inputs may be any that keep to these rules, and one draw needn't show every extreme that they name: `frame_counts`: in each group of 4 clips one clip has exactly 16 frames.
All inputs are finite; a program needn't handle non-finite values.
Results may differ from a plain program's by a relative error of at most 0.014.
Values may be sent and summed in bfloat16 or wider, within the bound.
No kernel may reach another device: no remote copies, remote signals or barrier semaphores. Data moves between devices by JAX's collectives and lax.ppermute only.
A program may use at most 128 MiB of HBM per device.

v0:
```python
import functools
import math

import jax
import jax.numpy as jnp
from jax import lax
from jax.experimental import pallas as pl
from jax.experimental.pallas import tpu as pltpu
from jax.sharding import PartitionSpec as P

eps = 1e-05
f32 = jnp.float32
bf16 = jnp.bfloat16
mib = 1 << 20


def gelu_terms(x):
    c = math.sqrt(2.0 / math.pi)
    x2 = x * x
    t = jnp.tanh(x * (c + (c * 0.044715) * x2))
    return x2, t


def gelu(x):
    _, t = gelu_terms(x)
    return x * (0.5 + 0.5 * t)


def gelu_slope(x):
    c = math.sqrt(2.0 / math.pi)
    x2, t = gelu_terms(x)
    return 0.5 + 0.5 * t + (0.5 * x) * ((1.0 - t * t) * (c + (3.0 * c * 0.044715) * x2))


def gelu_both(x):
    c = math.sqrt(2.0 / math.pi)
    x2, t = gelu_terms(x)
    cdf = 0.5 + 0.5 * t
    return x * cdf, cdf + (0.5 * x) * ((1.0 - t * t) * (c + (3.0 * c * 0.044715) * x2))


def valid_rows(shape, group, used):
    return lax.broadcasted_iota(jnp.int32, shape, 0) % group < used


def row_sums(values):
    rows, width = values.shape
    return jnp.sum(values.reshape(rows // 8, 8, width), axis=0)


def dot(left, right):
    return jnp.dot(left, right, preferred_element_type=f32)


def dot_t(left, right):
    return lax.dot_general(left, right, (((1,), (1,)), ((), ())), preferred_element_type=f32)


def t_dot(left, right):
    return lax.dot_general(left, right, (((0,), (0,)), ((), ())), preferred_element_type=f32)


def put_lanes(ref, start, values):
    rows, channels = values.shape
    for j in range(channels // 128):
        ref[j, pl.ds(start, rows), :] = values[:, 128 * j : 128 * (j + 1)]


def get_lanes(ref, start, rows):
    return jnp.concatenate([ref[j, pl.ds(start, rows), :] for j in range(ref.shape[0])], axis=1)


def get_even(ref, start, count):
    return jnp.concatenate(
        [ref[j, pl.ds(start, count, stride=2), :] for j in range(ref.shape[0])], axis=1
    )


def put_even(ref, start, values):
    rows, channels = values.shape
    for j in range(channels // 128):
        ref[j, pl.ds(start, rows, stride=2), :] = values[:, 128 * j : 128 * (j + 1)]


def conv_rows(taps, load, rows):
    sums = [None, None, None]
    for a in range(3):
        for b in range(3):
            block = load(a, b)
            for e in range(3):
                i = 9 * a + 3 * b + e
                term = block * taps(i)
                sums[e] = term if sums[e] is None else sums[e] + term
    return pltpu.roll(sums[0], 1, 0) + sums[1] + pltpu.roll(sums[2], rows - 1, 0)


def first_kernel(par_ref, scal_ref, x_ref, w_ref, first_ref, actz_ref, actc_ref, even_ref, xpad, xe):
    k = pl.program_id(0)
    _, _, height, width, _ = x_ref.shape
    pitch = xe.shape[1]

    @pl.when(k == 0)
    def _():
        xpad[...] = jnp.zeros_like(xpad)
        xe[...] = jnp.zeros_like(xe)

    for slot, act_ref in ((0, actz_ref), (1, actc_ref)):
        frame = par_ref[0] if slot == 0 else 1 - par_ref[0]
        for h in range(height):
            xpad[pl.ds(h * pitch, width), :] = x_ref[0, frame, h]
        first = dot(xpad[...], w_ref[...])
        first_ref[0, slot] = first
        act_ref[0] = (gelu(first) * scal_ref[slot, k]).astype(bf16)
    for h in range(0, height, 2):
        put_lanes(xe, 0, x_ref[0, 0, h].astype(f32))
        even_ref[0, pl.ds(h // 2 * (pitch // 2), pitch // 2), :] = get_even(xe, 0, pitch // 2)


def fill_frames(frames, sources, pad, rows):
    for s, source in enumerate(sources):
        frames[s, pl.ds(pad, rows), :] = source[0].astype(f32)


def clear_edges(frames, pad, rows):
    edge = jnp.zeros((pad, frames.shape[-1]), f32)
    for s in range(frames.shape[0]):
        frames[s, pl.ds(0, pad), :] = edge
        frames[s, pl.ds(pad + rows, pad), :] = edge


def mid_kernel(
    width, par_ref, scal_ref, rz_ref, oz_ref, oc_ref, rc_ref, taps_ref, up_ref,
    mid_ref, act_ref, even_ref, moment_ref, frames, sums, total,
):
    k = pl.program_id(0)
    rows = oz_ref.shape[1]
    pitch = 16
    chunk = 2 * pitch

    @pl.when(k == 0)
    def _():
        clear_edges(frames, pitch, rows)
        total[...] = jnp.zeros_like(total)

    fill_frames(frames, (rz_ref, oz_ref, oc_ref, rc_ref), pitch, rows)

    for slot in range(2):
        def step(c, _):
            start = pl.multiple_of(c * chunk, chunk)
            mid = conv_rows(
                lambda i: taps_ref[pl.ds(i, 1), :],
                lambda a, b: frames[slot + a, pl.ds(pl.multiple_of(start + pitch * b, pitch), chunk), :],
                chunk,
            )
            mid_ref[0, slot, pl.ds(start, chunk), :] = mid
            act = jnp.where(valid_rows(mid.shape, pitch, width), gelu(mid), 0.0)
            act_ref[0, slot, pl.ds(start, chunk), :] = act.astype(bf16)
            return 0

        lax.fori_loop(0, rows // chunk, step, 0)
        third = dot(act_ref[0, slot], up_ref[...])
        put_lanes(sums, slot * rows, third)
        scale = scal_ref[slot, k]
        total[0] += row_sums(third) * scale
        total[1] += row_sums(third * third) * scale
    half = pitch // 2
    for j in range(rows // chunk):
        even_ref[0, pl.ds(half * j, half), :] = get_even(
            sums, par_ref[0] * rows + chunk * j, half
        )

    @pl.when(k == pl.num_programs(0) - 1)
    def _():
        moment_ref[...] = jnp.sum(total[...], axis=1)


def norm_stats(received_ref, inverse):
    totals = received_ref[0]
    for i in range(1, received_ref.shape[0]):
        totals = totals + received_ref[i]
    center = totals[0:1] * inverse
    return center, lax.rsqrt(totals[1:2] * inverse - center * center + eps)


def entry_kernel(
    width, scal_ref, moments_ref, even_x_ref, even_ref, gain_ref, shift_ref, down_ref,
    stats_ref, hat_ref, entry_ref, first_ref, act_ref,
):
    center, scale = norm_stats(moments_ref, scal_ref[4, 0])
    stats_ref[0:1] = center
    stats_ref[1:2] = scale
    clips, rows, channels = even_ref.shape
    for k in range(clips):
        hat = (even_ref[k] - center) * scale
        hat_ref[k] = hat
        entry = even_x_ref[k] + hat * gain_ref[...] + shift_ref[...]
        entry = jnp.where(valid_rows(entry.shape, 8, width), entry, 0.0)
        entry_ref[pl.ds(k * rows, rows), :] = entry.astype(bf16)
    late = dot(entry_ref[...], down_ref[...])
    first_ref[...] = late
    for k in range(clips):
        act_ref[k] = (gelu(late[k * rows : (k + 1) * rows]) * scal_ref[2, k]).astype(bf16)


def late_kernel(
    width, scal_ref, rz_ref, own_ref, rc_ref, taps_ref, up_ref,
    mid_ref, act_ref, sum_ref, moment_ref, frames,
):
    clips, rows, channels = own_ref.shape
    pitch = 8
    edge = jnp.zeros((pitch, channels), f32)
    lanes = 128

    def clip_step(k, _):
        for s, source in enumerate((rz_ref, own_ref, rc_ref)):
            frames[s, pl.ds(0, pitch), :] = edge
            frames[s, pl.ds(pitch + rows, pitch), :] = edge
            frames[s, pl.ds(pitch, rows), :] = source[k].astype(f32)
        for l in range(channels // lanes):
            cols = pl.ds(l * lanes, lanes)
            mid = conv_rows(
                lambda i: taps_ref[pl.ds(i, 1), cols],
                lambda a, b: frames[a, pl.ds(pitch * b, rows), cols],
                rows,
            )
            mid_ref[k, :, cols] = mid
            act = jnp.where(valid_rows(mid.shape, pitch, width), gelu(mid), 0.0)
            act_ref[k, :, cols] = act
        return 0

    lax.fori_loop(0, clips, clip_step, 0)


def late_sum_kernel(scal_ref, act_in_ref, up_ref, act_ref, sum_ref, moment_ref):
    clips, rows, channels = act_in_ref.shape
    for k in range(clips):
        act_ref[pl.ds(k * rows, rows), :] = act_in_ref[k].astype(bf16)
    late = dot(act_ref[...], up_ref[...]).astype(bf16)
    sum_ref[...] = late
    wide = late.astype(f32)
    one = two = None
    for k in range(clips):
        block = wide[k * rows : (k + 1) * rows]
        a = row_sums(block) * scal_ref[2, k]
        b = row_sums(block * block) * scal_ref[2, k]
        one, two = (a, b) if one is None else (one + a, two + b)
    moment_ref[0:1] = jnp.sum(one, axis=0, keepdims=True)
    moment_ref[1:2] = jnp.sum(two, axis=0, keepdims=True)


def post_kernel(
    width, scal_ref, moments_ref, sum_ref, skip_ref, gain_ref, shift_ref, pooled_grad_ref,
    stats_ref, back_ref, pooled_ref, pre_ref, skip_grad_ref,
):
    center, scale = norm_stats(moments_ref, scal_ref[4, 1])
    stats_ref[0:1] = center
    stats_ref[1:2] = scale
    clips, rows, channels = sum_ref.shape
    one = two = None
    for k in range(clips):
        hat = (sum_ref[k].astype(f32) - center) * scale
        post, slope = gelu_both(hat * gain_ref[...] + shift_ref[...] + skip_ref[k].astype(f32))
        keep = valid_rows(post.shape, 8, width)
        weight = scal_ref[3, k]
        pooled_ref[pl.ds(k, 1)] = jnp.sum(jnp.where(keep, post, 0.0), axis=0, keepdims=True) * weight
        pre = jnp.where(keep, pooled_grad_ref[pl.ds(k, 1)] * weight * slope, 0.0)
        pre_ref[k] = pre
        skip_grad_ref[k] = pre.astype(bf16)
        a, b = row_sums(pre), row_sums(pre * hat)
        one, two = (a, b) if one is None else (one + a, two + b)
    back_ref[0:1] = jnp.sum(one, axis=0, keepdims=True)
    back_ref[1:2] = jnp.sum(two, axis=0, keepdims=True)


def sum_grad_kernel(
    width, scal_ref, back_ref, stats_ref, sum_ref, pre_ref, gain_ref, up_ref, mid_ref,
    sum_grad_ref, mid_grad_ref,
):
    totals = back_ref[0]
    for i in range(1, back_ref.shape[0]):
        totals = totals + back_ref[i]
    inverse = scal_ref[4, 1]
    center, scale = stats_ref[0:1], stats_ref[1:2]
    lead = gain_ref[...] * scale
    clips, rows, channels = sum_ref.shape
    for k in range(clips):
        hat = (sum_ref[k].astype(f32) - center) * scale
        weight = scal_ref[2, k] * inverse
        grad = lead * (pre_ref[k] - weight * (totals[0:1] + hat * totals[1:2]))
        grad = jnp.where(valid_rows(grad.shape, 8, width), grad, 0.0)
        sum_grad_ref[pl.ds(k * rows, rows), :] = grad.astype(bf16)
    back = dot_t(sum_grad_ref[...], up_ref[...])
    for k in range(clips):
        mid_grad_ref[k] = (back[k * rows : (k + 1) * rows] * gelu_slope(mid_ref[k])).astype(bf16)


def late_back_kernel(
    width, scal_ref, rz_ref, own_ref, rc_ref, taps_ref, first_ref, down_ref, skip_back_ref, hat_ref,
    first_grad_ref, entry_grad_ref, back_ref, frames, grads,
):
    clips, rows, channels = own_ref.shape
    pitch = 8
    edge = jnp.zeros((pitch, channels), f32)
    lanes = 128

    def clip_step(k, _):
        for s, source in enumerate((rz_ref, own_ref, rc_ref)):
            frames[s, pl.ds(0, pitch), :] = edge
            frames[s, pl.ds(pitch + rows, pitch), :] = edge
            frames[s, pl.ds(pitch, rows), :] = source[k].astype(f32)
        for l in range(channels // lanes):
            cols = pl.ds(l * lanes, lanes)
            grad = conv_rows(
                lambda i: taps_ref[pl.ds(26 - i, 1), cols],
                lambda a, b: frames[a, pl.ds(pitch * b, rows), cols],
                rows,
            )
            grad = grad * scal_ref[2, k] * gelu_slope(first_ref[k, :, cols])
            grads[k, :, cols] = jnp.where(valid_rows(grad.shape, pitch, width), grad, 0.0)
        return 0

    lax.fori_loop(0, clips, clip_step, 0)
    for k in range(clips):
        first_grad_ref[pl.ds(k * rows, rows), :] = grads[k].astype(bf16)
    entry = dot_t(first_grad_ref[...], down_ref[...]) + skip_back_ref[...]
    one = two = None
    for k in range(clips):
        block = entry[k * rows : (k + 1) * rows]
        entry_grad_ref[k] = block
        masked = block * scal_ref[2, k]
        a, b = row_sums(masked), row_sums(masked * hat_ref[k])
        one, two = (a, b) if one is None else (one + a, two + b)
    back_ref[0:1] = jnp.sum(one, axis=0, keepdims=True)
    back_ref[1:2] = jnp.sum(two, axis=0, keepdims=True)


def tap_grads(load, grad_of, steps, rows):
    def step(c, totals):
        grad = grad_of(c)
        sides = (pltpu.roll(grad, rows - 1, 0), grad, pltpu.roll(grad, 1, 0))
        new = []
        for a in range(3):
            for b in range(3):
                block = load(c, a, b)
                for e in range(3):
                    new.append(totals[9 * a + 3 * b + e] + row_sums(block * sides[e]))
        return tuple(new)

    return steps, step


def late_taps_kernel(rz_ref, own_ref, rc_ref, grad_ref, out_ref, frames):
    clips, rows, channels = own_ref.shape
    pitch = 8
    edge = jnp.zeros((pitch, channels), f32)
    lanes = 128
    for s, source in enumerate((rz_ref, own_ref, rc_ref)):
        for k in range(clips):
            frames[s, k, pl.ds(0, pitch), :] = edge
            frames[s, k, pl.ds(pitch + rows, pitch), :] = edge
            frames[s, k, pl.ds(pitch, rows), :] = source[k].astype(f32)
    for l in range(channels // lanes):
        cols = pl.ds(l * lanes, lanes)
        steps, step = tap_grads(
            lambda k, a, b: frames[a, k, pl.ds(pitch * b, rows), cols],
            lambda k: grad_ref[k, :, cols].astype(f32),
            clips,
            rows,
        )
        zero = jnp.zeros((8, lanes), f32)
        totals = lax.fori_loop(0, steps, step, (zero,) * 27)
        for i in range(27):
            out_ref[pl.ds(i, 1), cols] = jnp.sum(totals[i], axis=0, keepdims=True)


def third_taps_kernel(rz_ref, oz_ref, oc_ref, rc_ref, gz_ref, gc_ref, out_ref, frames, grads, total):
    k = pl.program_id(0)
    rows, channels = oz_ref.shape[1], oz_ref.shape[2]
    pitch = 16
    chunk = 2 * pitch
    lanes = 128

    @pl.when(k == 0)
    def _():
        clear_edges(frames, pitch, rows)
        total[...] = jnp.zeros_like(total)

    fill_frames(frames, (rz_ref, oz_ref, oc_ref, rc_ref), pitch, rows)
    grads[0] = gz_ref[0].astype(f32)
    grads[1] = gc_ref[0].astype(f32)
    count = rows // chunk
    for l in range(channels // lanes):
        cols = pl.ds(l * lanes, lanes)
        totals = tuple(total[i, :, cols] for i in range(27))
        for slot in range(2):
            steps, step = tap_grads(
                lambda c, a, b: frames[
                    slot + a, pl.ds(pl.multiple_of(c * chunk + pitch * b, pitch), chunk), cols
                ],
                lambda c: grads[slot, pl.ds(pl.multiple_of(c * chunk, chunk), chunk), cols],
                count,
                chunk,
            )
            totals = lax.fori_loop(0, steps, step, totals)
        for i in range(27):
            total[i, :, cols] = totals[i]

    @pl.when(k == pl.num_programs(0) - 1)
    def _():
        out_ref[...] = jnp.sum(total[...], axis=1)


def third_grad_kernel(
    width, par_ref, scal_ref, back_ref, stats_ref, act_ref, mid_ref, entry_grad_ref, gain_ref, up_ref,
    sum_grad_ref, gz_ref, gc_ref, placed,
):
    k = pl.program_id(0)
    totals = back_ref[0]
    for i in range(1, back_ref.shape[0]):
        totals = totals + back_ref[i]
    rows = act_ref.shape[2]
    pitch = 16
    chunk = 2 * pitch
    half = pitch // 2
    center, scale = stats_ref[0:1], stats_ref[1:2]
    lead = gain_ref[...] * scale
    inverse = scal_ref[4, 0]

    @pl.when(k == 0)
    def _():
        placed[...] = jnp.zeros_like(placed)

    for j in range(rows // chunk):
        put_even(
            placed, par_ref[0] * rows + chunk * j, lead * entry_grad_ref[0, pl.ds(half * j, half), :]
        )
    for slot, out in ((0, gz_ref), (1, gc_ref)):
        weight = scal_ref[slot, k] * inverse
        slope_hat = -(lead * scale * totals[1:2]) * weight
        offset = -(lead * (totals[0:1] - center * scale * totals[1:2])) * weight
        third = dot(act_ref[0, slot], up_ref[...])
        grad = get_lanes(placed, slot * rows, rows) + (offset + third * slope_hat)
        sum_grad_ref[0, slot] = grad.astype(bf16)
        back = dot_t(sum_grad_ref[0, slot], up_ref[...]) * gelu_slope(mid_ref[0, slot])
        out[0] = jnp.where(valid_rows(back.shape, pitch, width), back, 0.0).astype(bf16)


def first_grad_kernel(
    width, par_ref, scal_ref, rz_ref, gz_ref, gc_ref, rc_ref, taps_ref, first_ref, x_ref,
    grad_ref, down_grad_ref, frames, xpad,
):
    k = pl.program_id(0)
    rows = gz_ref.shape[1]
    height, width = x_ref.shape[2], x_ref.shape[3]
    pitch = 16
    chunk = 2 * pitch

    @pl.when(k == 0)
    def _():
        clear_edges(frames, pitch, rows)
        xpad[...] = jnp.zeros_like(xpad)
        down_grad_ref[...] = jnp.zeros_like(down_grad_ref)

    fill_frames(frames, (rz_ref, gz_ref, gc_ref, rc_ref), pitch, rows)
    for slot in range(2):
        frame = par_ref[0] if slot == 0 else 1 - par_ref[0]
        for h in range(height):
            xpad[pl.ds(slot * rows + h * pitch, width), :] = x_ref[0, frame, h]
        scale = scal_ref[slot, k]

        def step(c, _):
            start = pl.multiple_of(c * chunk, chunk)
            grad = conv_rows(
                lambda i: taps_ref[pl.ds(26 - i, 1), :],
                lambda a, b: frames[slot + a, pl.ds(pl.multiple_of(start + pitch * b, pitch), chunk), :],
                chunk,
            )
            grad = grad * scale * gelu_slope(first_ref[0, slot, pl.ds(start, chunk), :])
            grad = jnp.where(valid_rows(grad.shape, pitch, width), grad, 0.0)
            grad_ref[0, pl.ds(pl.multiple_of(slot * rows + start, chunk), chunk), :] = grad.astype(bf16)
            return 0

        lax.fori_loop(0, rows // chunk, step, 0)
    down_grad_ref[...] += t_dot(xpad[...], grad_ref[0])


def clip_grad_kernel(par_ref, grad_ref, down_ref, entry_grad_ref, out_ref, wide):
    _, _, height, width, _ = out_ref.shape
    pitch = 16
    half = pitch // 2
    rows = height * pitch
    for slot in range(2):
        frame = par_ref[0] if slot == 0 else 1 - par_ref[0]
        put_lanes(wide, slot * rows, dot_t(grad_ref[0, pl.ds(slot * rows, rows), :], down_ref[...]))
    for j in range(height // 2):
        at = par_ref[0] * rows + 2 * pitch * j
        put_even(wide, at, get_even(wide, at, half) + entry_grad_ref[0, pl.ds(half * j, half), :])
    for slot in range(2):
        frame = par_ref[0] if slot == 0 else 1 - par_ref[0]
        for h in range(height):
            out_ref[0, frame, h] = get_lanes(wide, slot * rows + h * pitch, width).astype(bf16)


smem = pl.BlockSpec(memory_space=pltpu.SMEM)


def whole(shape):
    return pl.BlockSpec(shape, lambda k: (0,) * len(shape))


def by_clip(shape):
    return pl.BlockSpec((1,) + shape[1:], lambda k: (k,) + (0,) * (len(shape) - 1))


def call(kernel, name, inputs, outputs, scratch, clips=None, limit=60, flops=0):
    if clips is None:
        def spec(kind, shape):
            return smem if kind == "s" else pl.BlockSpec(memory_space=pltpu.VMEM)
    else:
        def spec(kind, shape):
            return smem if kind == "s" else whole(shape) if kind == "w" else by_clip(shape)
    size = sum(math.prod(a.shape) * a.dtype.itemsize for a, _ in inputs)
    size += sum(math.prod(s) * jnp.dtype(d).itemsize for s, d, _ in outputs)
    options = {} if clips is None else {"grid": (clips,)}
    return pl.pallas_call(
        kernel,
        name=name,
        out_shape=[jax.ShapeDtypeStruct(s, d) for s, d, _ in outputs],
        in_specs=[spec(kind, a.shape) for a, kind in inputs],
        out_specs=[spec(kind, s) for s, _, kind in outputs],
        scratch_shapes=scratch,
        compiler_params=pltpu.CompilerParams(vmem_limit_bytes=limit * mib),
        cost_estimate=pl.CostEstimate(flops=flops, bytes_accessed=size, transcendentals=0),
        **options,
    )(*[a for a, _ in inputs])


def copies_exchange(values):
    size = lax.axis_size("space")
    copies = jnp.broadcast_to(values[None], (size,) + values.shape)
    return lax.all_to_all(copies, "space", split_axis=0, concat_axis=0, tiled=True)


def swap_neighbours(to_z, to_core):
    size = lax.axis_size("space")
    core = [(i, i ^ 1) for i in range(size)]
    z = [(i, j) for m in range(1, size - 1, 2) for i, j in ((m, m + 1), (m + 1, m))]
    return lax.ppermute(to_z, "space", z), lax.ppermute(to_core, "space", core)


def reduce_rows(term, axes=("clip", "space")):
    parts = 1
    for axis in axes:
        parts *= lax.axis_size(axis)
    pieces = term.astype(bf16).reshape((parts, term.shape[0] // parts) + term.shape[1:])
    received = lax.all_to_all(pieces, axes, split_axis=0, concat_axis=0, tiled=True)
    return jnp.sum(received.astype(f32), axis=0)


def per_device(
    clip_input, frame_counts, third_down, third_depth, third_up, third_gain, third_shift,
    fourth_down, fourth_skip, fourth_depth, fourth_up, fourth_gain, fourth_shift,
    classifier, class_bias, logit_grad,
):
    clips, frames, height, width, channels = clip_input.shape
    inner = third_down.shape[1]
    late_inner = fourth_down.shape[1]
    late_wide = fourth_up.shape[1]
    half_width = width // 2
    rows = height * 16
    late_rows = height // 2 * 8
    late_all = clips * late_rows
    slab = lax.axis_index("space")
    parity = slab & 1
    par = parity.reshape(1)
    flip = (parity == 1)

    frame_ids = 2 * slab + jnp.stack((parity, 1 - parity))
    masks = (frame_ids[:, None] < frame_counts[None, :]).astype(f32)
    late_mask = (2 * slab < frame_counts).astype(f32)
    late_counts = ((frame_counts + 1) // 2).astype(f32)
    cells = (height // 2) * half_width
    third_total = jnp.sum(frame_counts).astype(f32) * (height * width)
    late_total = jnp.sum(late_counts) * cells
    inverses = jnp.stack((1.0 / third_total, 1.0 / late_total))
    scal = jnp.concatenate(
        (
            masks,
            late_mask[None],
            (late_mask / (late_counts * cells))[None],
            jnp.pad(inverses, (0, clips - 2))[None],
        )
    )

    def tap_rows(kernel):
        taps = jnp.transpose(kernel).reshape(3, 9, -1)
        return jnp.where(flip, taps[::-1], taps).reshape(27, -1)

    def tap_columns(rows_out):
        taps = rows_out.reshape(3, 9, -1)
        return jnp.transpose(jnp.where(flip, taps[::-1], taps).reshape(27, -1))

    third_taps = tap_rows(third_depth)
    late_taps = tap_rows(fourth_depth)
    third_gain, third_shift = third_gain[None], third_shift[None]
    fourth_gain, fourth_shift = fourth_gain[None], fourth_shift[None]

    own_start = lax.axis_index("clip") * clips
    grad_rows = lax.dynamic_slice_in_dim(logit_grad, own_start, clips, 0)
    pooled_grad = lax.dot_general(
        grad_rows, classifier.astype(f32), (((1,), (1,)), ((), ())), precision=lax.Precision.HIGHEST
    ).astype(bf16).astype(f32)

    first, act_z, act_c, even_x = call(
        first_kernel, "first",
        [(par, "s"), (scal, "s"), (clip_input, "c"), (third_down, "w")],
        [
            ((clips, 2, rows, inner), f32, "c"),
            ((clips, rows, inner), bf16, "c"),
            ((clips, rows, inner), bf16, "c"),
            ((clips, late_rows, channels), f32, "c"),
        ],
        [pltpu.VMEM((rows, channels), bf16), pltpu.VMEM((channels // 128, 16, 128), f32)],
        clips=clips,
    )
    got_z, got_c = swap_neighbours(act_z, act_c)
    mid, mid_act, even_sum, moments = call(
        functools.partial(mid_kernel, width), "mid",
        [(par, "s"), (scal, "s"), (got_z, "c"), (act_z, "c"), (act_c, "c"), (got_c, "c"),
         (third_taps, "w"), (third_up, "w")],
        [
            ((clips, 2, rows, inner), f32, "c"),
            ((clips, 2, rows, inner), bf16, "c"),
            ((clips, late_rows, channels), f32, "c"),
            ((2, channels), f32, "w"),
        ],
        [
            pltpu.VMEM((4, rows + 32, inner), f32),
            pltpu.VMEM((channels // 128, 2 * rows, 128), f32),
            pltpu.VMEM((2, 8, channels), f32),
        ],
        clips=clips,
    )
    stats, even_hat, entry, late_first, late_act = call(
        functools.partial(entry_kernel, half_width), "entry",
        [(scal, "s"), (copies_exchange(moments), "w"), (even_x, "w"), (even_sum, "w"),
         (third_gain, "w"), (third_shift, "w"), (fourth_down, "w")],
        [
            ((2, channels), f32, "w"),
            ((clips, late_rows, channels), f32, "w"),
            ((late_all, channels), bf16, "w"),
            ((late_all, late_inner), f32, "w"),
            ((clips, late_rows, late_inner), bf16, "w"),
        ],
        [],
    )
    late_first = late_first.reshape(clips, late_rows, late_inner)
    late_z, late_c = swap_neighbours(late_act, late_act)
    skipped = dot(entry, fourth_skip).astype(bf16).reshape(clips, late_rows, late_wide)
    late_mid, late_mid_wide = call(
        lambda scal_ref, z, o, c, t, m, a, fr: late_kernel(
            half_width, scal_ref, z, o, c, t, None, m, a, None, None, fr
        ),
        "late_mid",
        [(scal, "s"), (late_z, "w"), (late_act, "w"), (late_c, "w"), (late_taps, "w")],
        [((clips, late_rows, late_inner), f32, "w"), ((clips, late_rows, late_inner), f32, "w")],
        [pltpu.VMEM((3, late_rows + 16, late_inner), f32)],
    )
    late_mid_act, late_sum, late_moments = call(
        late_sum_kernel, "late_sum",
        [(scal, "s"), (late_mid_wide, "w"), (fourth_up, "w")],
        [
            ((late_all, late_inner), bf16, "w"),
            ((late_all, late_wide), bf16, "w"),
            ((2, late_wide), f32, "w"),
        ],
        [],
    )
    late_sum = late_sum.reshape(clips, late_rows, late_wide)
    late_stats, late_back, pooled_term, pre_grad, skip_grad = call(
        functools.partial(post_kernel, half_width), "post",
        [(scal, "s"), (copies_exchange(late_moments), "w"), (late_sum, "w"), (skipped, "w"),
         (fourth_gain, "w"), (fourth_shift, "w"), (pooled_grad, "w")],
        [
            ((2, late_wide), f32, "w"),
            ((2, late_wide), f32, "w"),
            ((clips, late_wide), f32, "w"),
            ((clips, late_rows, late_wide), f32, "w"),
            ((clips, late_rows, late_wide), bf16, "w"),
        ],
        [],
    )
    received = copies_exchange(jnp.concatenate((late_back, pooled_term)))
    pooled = jnp.sum(received[:, 2:], axis=0).astype(bf16)
    logits = dot(pooled, classifier) + class_bias
    skip_rows = skip_grad.reshape(late_all, late_wide)
    skip_back = dot_t(skip_rows, fourth_skip)
    fourth_skip_term = t_dot(entry, skip_rows)
    late_sum_grad, late_mid_grad = call(
        functools.partial(sum_grad_kernel, half_width), "sum_grad",
        [(scal, "s"), (received, "w"), (late_stats, "w"), (late_sum, "w"), (pre_grad, "w"),
         (fourth_gain, "w"), (fourth_up, "w"), (late_mid, "w")],
        [((late_all, late_wide), bf16, "w"), ((clips, late_rows, late_inner), bf16, "w")],
        [],
    )
    late_gz, late_gc = swap_neighbours(late_mid_grad, late_mid_grad)
    fourth_up_term = t_dot(late_mid_act, late_sum_grad)
    (fourth_depth_term,) = call(
        late_taps_kernel, "late_taps",
        [(late_z, "w"), (late_act, "w"), (late_c, "w"), (late_mid_grad, "w")],
        [((27, late_inner), f32, "w")],
        [pltpu.VMEM((3, clips, late_rows + 16, late_inner), f32)],
    )
    late_first_grad, entry_grad, third_back = call(
        functools.partial(late_back_kernel, half_width), "late_back",
        [(scal, "s"), (late_gz, "w"), (late_mid_grad, "w"), (late_gc, "w"), (late_taps, "w"),
         (late_first, "w"), (fourth_down, "w"), (skip_back, "w"), (even_hat, "w")],
        [
            ((late_all, late_inner), bf16, "w"),
            ((clips, late_rows, channels), f32, "w"),
            ((2, channels), f32, "w"),
        ],
        [
            pltpu.VMEM((3, late_rows + 16, late_inner), f32),
            pltpu.VMEM((clips, late_rows, late_inner), f32),
        ],
    )
    fourth_down_term = t_dot(entry, late_first_grad)
    third_sum_grad, grad_z, grad_c = call(
        functools.partial(third_grad_kernel, width), "third_grad",
        [(par, "s"), (scal, "s"), (copies_exchange(third_back), "w"), (stats, "w"), (mid_act, "c"), (mid, "c"),
         (entry_grad, "c"), (third_gain, "w"), (third_up, "w")],
        [
            ((clips, 2, rows, channels), bf16, "c"),
            ((clips, rows, inner), bf16, "c"),
            ((clips, rows, inner), bf16, "c"),
        ],
        [pltpu.VMEM((channels // 128, 2 * rows, 128), f32)],
        clips=clips,
    )
    third_gz, third_gc = swap_neighbours(grad_z, grad_c)
    third_up_term = t_dot(
        mid_act.reshape(clips * 2 * rows, inner), third_sum_grad.reshape(clips * 2 * rows, channels)
    )
    (third_depth_term,) = call(
        third_taps_kernel, "third_taps",
        [(got_z, "c"), (act_z, "c"), (act_c, "c"), (got_c, "c"), (grad_z, "c"), (grad_c, "c")],
        [((27, inner), f32, "w")],
        [
            pltpu.VMEM((4, rows + 32, inner), f32),
            pltpu.VMEM((2, rows, inner), f32),
            pltpu.VMEM((27, 8, inner), f32),
        ],
        clips=clips,
    )
    first_grad, third_down_term = call(
        functools.partial(first_grad_kernel, width), "first_grad",
        [(par, "s"), (scal, "s"), (third_gz, "c"), (grad_z, "c"), (grad_c, "c"), (third_gc, "c"),
         (third_taps, "w"), (first, "c"), (clip_input, "c")],
        [((clips, 2 * rows, inner), bf16, "c"), ((channels, inner), f32, "w")],
        [pltpu.VMEM((4, rows + 32, inner), f32), pltpu.VMEM((2 * rows, channels), bf16)],
        clips=clips,
    )
    (clip_grad,) = call(
        clip_grad_kernel, "clip_grad",
        [(par, "s"), (first_grad, "c"), (third_down, "w"), (entry_grad, "c")],
        [(clip_input.shape, bf16, "c")],
        [pltpu.VMEM((channels // 128, 2 * rows, 128), f32)],
        clips=clips,
    )

    parts = lax.axis_size("clip") * lax.axis_size("space")
    small_terms = [
        term.reshape(parts, -1)
        for term in (
            third_back[1], third_back[0], late_back[1], late_back[0],
            tap_columns(third_depth_term), tap_columns(fourth_depth_term),
        )
    ]
    widths = [term.shape[1] for term in small_terms]
    pooled_pieces = jnp.moveaxis(pooled.astype(f32).reshape(clips, parts, -1), 1, 0)
    own_width = pooled_pieces.shape[2]
    packed = jnp.concatenate(small_terms + [pooled_pieces.reshape(parts, -1)], axis=1)
    length = packed.shape[1]
    packed = jnp.pad(packed, ((0, 0), (0, -length % 1024))).reshape(parts, -1, 128)
    received = lax.all_to_all(packed, ("clip", "space"), split_axis=0, concat_axis=0, tiled=True)
    received = received.reshape(parts, -1)
    totals = jnp.sum(received[:, : sum(widths)], axis=0)
    ends = [sum(widths[: i + 1]) for i in range(len(widths))]
    pieces = [totals[end - size : end] for size, end in zip(widths, ends)]
    gathered = received[:, sum(widths) : length].reshape(
        lax.axis_size("clip"), lax.axis_size("space"), clips, own_width
    )[:, 0]
    classifier_grad = lax.dot_general(
        gathered.reshape(-1, own_width), logit_grad, (((0,), (0,)), ((), ())),
        precision=lax.Precision.HIGHEST,
    )
    return (
        logits,
        clip_grad,
        reduce_rows(third_down_term),
        pieces[4].reshape(-1, 27),
        reduce_rows(third_up_term),
        pieces[0],
        pieces[1],
        reduce_rows(fourth_down_term),
        reduce_rows(fourth_skip_term),
        pieces[5].reshape(-1, 27),
        reduce_rows(fourth_up_term),
        pieces[2],
        pieces[3],
        classifier_grad,
        jnp.sum(logit_grad, axis=0),
    )


def solution(mesh):
    both = ("clip", "space")
    return jax.shard_map(
        per_device,
        mesh=mesh,
        in_specs=(P("clip", "space", None, None, None), P("clip")) + (P(),) * 14,
        out_specs=(
            P("clip", None),
            P("clip", "space", None, None, None),
            P(both, None),
            P(both, None),
            P(both, None),
            P(both),
            P(both),
            P(both, None),
            P(both, None),
            P(both, None),
            P(both, None),
            P(both),
            P(both),
            P(both, None),
            P(),
        ),
        check_vma=False,
    )
```

profile of v0, /device:TPU:0, one launch (start us, length us, event | category | flops | bytes accessed | tf_op | source)
XLA Modules:
  0.0 408.2 jit_solution(12220004094511855156)
XLA Ops:
  6.2 4.8 %copy.39.x_ref = bf16[4,2,14,14,1024]{4,3,2,1,0:T(8,128)(2,1)} copy(bf16[4,2,14,14,1024]{4,1,3,2,0:T(2,128)(2,1)} %param.16) | data formatting | bytes 6422528 | tf_op args[0]
  11.7 5.4 %first.1 = (f32[4,2,224,256]{3,2,1,0:T(8,128)}, bf16[4,224,256]{2,1,0:T(8,128)(2,1)}, bf16[4,224,256]{2,1,0:T(8,128)(2,1)}, f32[4,56,1024]{2,1,0:T(8,128)}) custom-call(s32[1]{0:T(128)} %bitcast.par_ref, f32[5,4]{1,0:T(8,128)} %pad_maximum_fusion.1.scal_ref, bf16[4,2,14,14,1024]{4,3,2,1,0:T(8,128)(2,1)} %copy.39.x_ref, bf16[1024,256]{1,0:T(8,128)(2,1)} %down_ref.5), custom_call_target="tpu_custom_call" | custom-call | bytes 7405652 | tf_op jit(solution)/shard_map/first/pallas_call | solution.py:525
  24.7 10.1 %mid.1 = (f32[4,2,224,256]{3,2,1,0:T(8,128)}, bf16[4,2,224,256]{3,2,1,0:T(8,128)(2,1)}, f32[4,56,1024]{2,1,0:T(8,128)}, f32[2,1024]{1,0:T(2,128)}) custom-call(s32[1]{0:T(128)} %bitcast.par_ref, f32[5,4]{1,0:T(8,128)} %pad_maximum_fusion.1.scal_ref, bf16[4,224,256]{2,1,0:T(8,128)(2,1)} %copy-done.8, bf16[4,224,256]{2,1,0:T(8,128)(2,1)} %get-tuple-element.48.oz_ref, ...), custom_call_target="tpu_custom_call" | custom-call | bytes 6065236 | tf_op jit(solution)/shard_map/mid/pallas_call | solution.py:525
  36.2 10.3 %all-to-all-start = ((f32[8,2,1024]{2,1,0:T(2,128)}), f32[8,2,1024]{2,1,0:T(2,128)S(1)}, u32[]{:S(2)}, u32[]{:S(2)}) async-start(f32[8,2,1024]{2,1,0:T(2,128)} %broadcast_in_dim.25), calls=%async_computation | async-start | bytes 131072 | tf_op jit(solution)/shard_map/all_to_all | solution.py:541
  47.2 5.3 %all-to-all-done.moments_ref = f32[8,2,1024]{2,1,0:T(2,128)S(1)} async-done(((f32[8,2,1024]{2,1,0:T(2,128)}), f32[8,2,1024]{2,1,0:T(2,128)S(1)}, u32[]{:S(2)}, u32[]{:S(2)}) %all-to-all-start) | async-done | bytes 65568 | tf_op jit(solution)/shard_map/all_to_all | solution.py:541
  68.2 6.9 %all-to-all-start.1 = ((f32[8,2,2048]{2,1,0:T(2,128)}), f32[8,2,2048]{2,1,0:T(2,128)S(1)}, u32[]{:S(2)}, u32[]{:S(2)}) async-start(f32[8,2,2048]{2,1,0:T(2,128)} %broadcast_in_dim.54), calls=%async_computation.1 | async-start | bytes 262144 | tf_op jit(solution)/shard_map/all_to_all | solution.py:541
  82.5 5.0 %post.1 = (f32[2,2048]{1,0:T(2,128)}, f32[2,2048]{1,0:T(2,128)}, f32[4,2048]{1,0:T(4,128)}, f32[4,56,2048]{2,1,0:T(8,128)}, bf16[4,56,2048]{2,1,0:T(8,128)(2,1)}) custom-call(f32[5,4]{1,0:T(8,128)} %pad_maximum_fusion.1.scal_ref, f32[8,2,2048]{2,1,0:T(2,128)} %copy-done.12, bf16[4,56,2048]{2,1,0:T(8,128)(2,1)} %bitcast.65, bf16[4,56,2048]{2,1,0:T(8,128)(2,1)} %bitcast.69, ...), custom_call_target="tpu_custom_call" | custom-call | bytes 4833360 | tf_op jit(solution)/shard_map/post/pallas_call | solution.py:525
  93.4 4.9 %fusion.12.skip_back_ref = f32[224,1024]{1,0:T(8,128)} fusion(bf16[224,2048]{1,0:T(8,128)(2,1)} %bitcast.70, bf16[1024,2048]{1,0:T(8,128)(2,1)} %param.24), kind=kOutput, calls=%fused_computation.50 | convolution fusion | flops 939524096 | bytes 6029312 | tf_op jit(solution)/shard_map/dot_general | solution.py:56
  98.3 9.6 %all-to-all-done.2.back_ref = f32[8,6,2048]{2,1,0:T(8,128)S(1)} async-done(((f32[8,6,2048]{2,1,0:T(8,128)}), f32[8,6,2048]{2,1,0:T(8,128)S(1)}, u32[]{:S(2)}, u32[]{:S(2)}) %all-to-all-start.2) | async-done | bytes 393248 | tf_op jit(solution)/shard_map/all_to_all | solution.py:541
  108.7 4.5 %sum_grad.1 = (bf16[224,2048]{1,0:T(8,128)(2,1)}, bf16[4,56,512]{2,1,0:T(8,128)(2,1)}) custom-call(f32[5,4]{1,0:T(8,128)} %pad_maximum_fusion.1.scal_ref, f32[8,6,2048]{2,1,0:T(8,128)} %copy-done.2, f32[2,2048]{1,0:T(2,128)} %get-tuple-element.60.stats_ref, bf16[4,56,2048]{2,1,0:T(8,128)(2,1)} %bitcast.66, f32[4,56,2048]{2,1,0:T(8,128)} %get-tuple-element.61.pre_ref, ...), custom_call_target="tpu_custom_call" | custom-call | bytes 6873168 | tf_op jit(solution)/shard_map/sum_grad/pallas_call | solution.py:525
  119.1 4.9 %late_back.1 = (bf16[224,512]{1,0:T(8,128)(2,1)}, f32[4,56,1024]{2,1,0:T(8,128)}, f32[2,1024]{1,0:T(2,128)}) custom-call(f32[5,4]{1,0:T(8,128)} %pad_maximum_fusion.1.scal_ref, bf16[4,56,512]{2,1,0:T(8,128)(2,1)} %copy-done.18, bf16[4,56,512]{2,1,0:T(8,128)(2,1)} %get-tuple-element.63.own_ref.grad_ref, bf16[4,56,512]{2,1,0:T(8,128)(2,1)} %copy-done.17, ...), custom_call_target="tpu_custom_call" | custom-call | bytes 5240912 | tf_op jit(solution)/shard_map/late_back/pallas_call | solution.py:525
  125.3 5.0 %all-to-all-start.3 = ((f32[8,2,1024]{2,1,0:T(2,128)}), f32[8,2,1024]{2,1,0:T(2,128)S(1)}, u32[]{:S(2)}, u32[]{:S(2)}) async-start(f32[8,2,1024]{2,1,0:T(2,128)} %broadcast_in_dim.58), calls=%async_computation.3 | async-start | bytes 131072 | tf_op jit(solution)/shard_map/all_to_all | solution.py:541
  136.9 6.7 %third_grad.1 = (bf16[4,2,224,1024]{3,2,1,0:T(8,128)(2,1)}, bf16[4,224,256]{2,1,0:T(8,128)(2,1)}, bf16[4,224,256]{2,1,0:T(8,128)(2,1)}) custom-call(s32[1]{0:T(128)} %bitcast.par_ref, f32[5,4]{1,0:T(8,128)} %pad_maximum_fusion.1.scal_ref, f32[8,2,1024]{2,1,0:T(2,128)} %copy-done.15, f32[2,1024]{1,0:T(2,128)} %get-tuple-element.68.stats_ref, ...), custom_call_target="tpu_custom_call" | custom-call | bytes 8859732 | tf_op jit(solution)/shard_map/third_grad/pallas_call | solution.py:525
  143.6 6.9 %third_taps.1 = f32[27,256]{1,0:T(8,128)} custom-call(bf16[4,224,256]{2,1,0:T(8,128)(2,1)} %copy-done.8, bf16[4,224,256]{2,1,0:T(8,128)(2,1)} %get-tuple-element.48.oz_ref, bf16[4,224,256]{2,1,0:T(8,128)(2,1)} %get-tuple-element.49.oc_ref, bf16[4,224,256]{2,1,0:T(8,128)(2,1)} %copy-done.9, bf16[4,224,256]{2,1,0:T(8,128)(2,1)} %get-tuple-element.72.gz_ref, ...), custom_call_target="tpu_custom_call" | custom-call | bytes 2780160 | tf_op jit(solution)/shard_map/third_taps/pallas_call | solution.py:525
  159.7 6.4 %all-to-all-done.5 = f32[32,16,128]{2,1,0:T(8,128)S(1)} async-done(((f32[32,16,128]{2,1,0:T(8,128)}), f32[32,16,128]{2,1,0:T(8,128)S(1)}, u32[]{:S(2)}, u32[]{:S(2)}) %all-to-all-start.5) | async-done | bytes 262176 | tf_op jit(solution)/shard_map/all_to_all | solution.py:786
  174.9 10.5 %first_grad.1 = (bf16[4,448,256]{2,1,0:T(8,128)(2,1)}, f32[1024,256]{1,0:T(8,128)}) custom-call(s32[1]{0:T(128)} %bitcast.par_ref, f32[5,4]{1,0:T(8,128)} %pad_maximum_fusion.1.scal_ref, bf16[4,224,256]{2,1,0:T(8,128)(2,1)} %copy-done.13, bf16[4,224,256]{2,1,0:T(8,128)(2,1)} %get-tuple-element.72.gz_ref, bf16[4,224,256]{2,1,0:T(8,128)(2,1)} %get-tuple-element.73.gc_ref, ...), custom_call_target="tpu_custom_call" | custom-call | bytes 8875092 | tf_op jit(solution)/shard_map/first_grad/pallas_call | solution.py:525
  187.5 17.3 %all-to-all-start.4 = ((bf16[32,32,256]{2,1,0:T(8,128)(2,1)}), bf16[32,32,256]{2,1,0:T(8,128)(2,1)S(1)}, u32[]{:S(2)}, u32[]{:S(2)}) async-start(bf16[32,32,256]{2,1,0:T(8,128)(2,1)} %bitcast.17), calls=%async_computation.4 | async-start | bytes 1048576 | tf_op jit(solution)/shard_map/all_to_all | solution.py:556
  207.2 13.9 %all-to-all-done.4 = bf16[32,32,256]{2,1,0:T(8,128)(2,1)S(1)} async-done(((bf16[32,32,256]{2,1,0:T(8,128)(2,1)}), bf16[32,32,256]{2,1,0:T(8,128)(2,1)S(1)}, u32[]{:S(2)}, u32[]{:S(2)}) %all-to-all-start.4) | async-done | bytes 524320 | tf_op jit(solution)/shard_map/all_to_all | solution.py:556
  227.9 24.2 %all-to-all-done.7 = bf16[32,32,512]{2,1,0:T(8,128)(2,1)S(1)} async-done(((bf16[32,32,512]{2,1,0:T(8,128)(2,1)}), bf16[32,32,512]{2,1,0:T(8,128)(2,1)S(1)}, u32[]{:S(2)}, u32[]{:S(2)}) %all-to-all-start.7) | async-done | bytes 1048608 | tf_op jit(solution)/shard_map/all_to_all | solution.py:556
  255.7 4.4 %convolution_convert_fusion = bf16[1024,2048]{1,0:T(8,128)(2,1)} fusion(bf16[224,1024]{1,0:T(8,128)(2,1)S(1)} %copy-done.4, bf16[224,2048]{1,0:T(8,128)(2,1)} %bitcast.71), kind=kOutput, calls=%fused_computation.2 | convolution fusion | flops 941621248 | bytes 5570560 | tf_op jit(solution)/shard_map/dot_general | solution.py:60
  260.1 45.7 %all-to-all-done.9 = bf16[32,16,2048]{2,1,0:T(8,128)(2,1)} async-done(((bf16[32,16,2048]{2,1,0:T(8,128)(2,1)}), bf16[32,16,2048]{2,1,0:T(8,128)(2,1)}, u32[]{:S(2)}, u32[]{:S(2)}) %all-to-all-start.9) | async-done | bytes 2097184 | tf_op jit(solution)/shard_map/all_to_all | solution.py:556
  311.4 5.6 %clip_grad.1 = bf16[4,2,14,14,1024]{4,3,2,1,0:T(8,128)(2,1)} custom-call(s32[1]{0:T(128)} %bitcast.par_ref, bf16[4,448,256]{2,1,0:T(8,128)(2,1)} %get-tuple-element.75.grad_ref, bf16[1024,256]{1,0:T(8,128)(2,1)} %down_ref.5, f32[4,56,1024]{2,1,0:T(8,128)} %get-tuple-element.71.entry_grad_ref), custom_call_target="tpu_custom_call" | custom-call | bytes 5570564 | tf_op jit(solution)/shard_map/clip_grad/pallas_call | solution.py:525
  317.0 7.1 %copy.44 = bf16[4,2,14,14,1024]{4,1,3,2,0:T(2,128)(2,1)} copy(bf16[4,2,14,14,1024]{4,3,2,1,0:T(8,128)(2,1)} %clip_grad.1) | data formatting | bytes 6422528
  333.9 70.6 %all-to-all-done.8 = bf16[32,32,2048]{2,1,0:T(8,128)(2,1)} async-done(((bf16[32,32,2048]{2,1,0:T(8,128)(2,1)}), bf16[32,32,2048]{2,1,0:T(8,128)(2,1)}, u32[]{:S(2)}, u32[]{:S(2)}) %all-to-all-start.8) | async-done | bytes 4194336 | tf_op jit(solution)/shard_map/all_to_all | solution.py:556
  (142 shorter events, 109.9 us)
Async XLA Ops:
  0.6 56.7 %copy-start = (bf16[2048,400]{0,1:T(8,128)(2,1)S(1)}, bf16[2048,400]{0,1:T(8,128)(2,1)}, u32[]{:S(2)}) copy-start(bf16[2048,400]{0,1:T(8,128)(2,1)} %param.29) | copy-start | bytes 4915204
  17.0 40.3 %copy-start.19 = (f32[16,400]{1,0:T(8,128)S(1)}, f32[16,400]{1,0:T(8,128)}, u32[]{:S(2)}) copy-start(f32[16,400]{1,0:T(8,128)} %param.31) | copy-start | bytes 76804
  17.0 5.9 %collective-permute-start = (bf16[4,224,256]{2,1,0:T(8,128)(2,1)}, bf16[4,224,256]{2,1,0:T(8,128)(2,1)S(1)}, u32[]{:S(2)}, u32[]{:S(2)}) collective-permute-start(bf16[4,224,256]{2,1,0:T(8,128)(2,1)} %get-tuple-element.48.oz_ref), channel_id=1, source_target_pairs={{1,2},{2,1},{3,4},{4,3},{5,6},{6,5},{9,10},{10,9},{11,12},{12,11},... | collective-permute-start | bytes 1376264 | tf_op jit(solution)/shard_map/ppermute | solution.py:548
  17.9 6.1 %collective-permute-start.1 = (bf16[4,224,256]{2,1,0:T(8,128)(2,1)}, bf16[4,224,256]{2,1,0:T(8,128)(2,1)S(1)}, u32[]{:S(2)}, u32[]{:S(2)}) collective-permute-start(bf16[4,224,256]{2,1,0:T(8,128)(2,1)} %get-tuple-element.49.oc_ref), channel_id=1, source_target_pairs={{0,1},{1,0},{2,3},{3,2},{4,5},{5,4},{6,7},{7,6},{8,9},{9,8},{10,11... | collective-permute-start | bytes 1376264 | tf_op jit(solution)/shard_map/ppermute | solution.py:548
  36.2 16.2 %all-to-all-start = ((f32[8,2,1024]{2,1,0:T(2,128)}), f32[8,2,1024]{2,1,0:T(2,128)S(1)}, u32[]{:S(2)}, u32[]{:S(2)}) async-start(f32[8,2,1024]{2,1,0:T(2,128)} %broadcast_in_dim.25), calls=%async_computation | async-start | bytes 131072 | tf_op jit(solution)/shard_map/all_to_all | solution.py:541
  56.5 18.6 %copy-start.4 = (bf16[224,1024]{1,0:T(8,128)(2,1)S(1)}, bf16[224,1024]{1,0:T(8,128)(2,1)}, u32[]{:S(2)}) copy-start(bf16[224,1024]{1,0:T(8,128)(2,1)} %get-tuple-element.57) | copy-start | bytes 1376260
  56.5 2.2 collective-permute-start.3
  56.5 2.2 collective-permute-start.2
  68.2 13.7 %all-to-all-start.1 = ((f32[8,2,2048]{2,1,0:T(2,128)}), f32[8,2,2048]{2,1,0:T(2,128)S(1)}, u32[]{:S(2)}, u32[]{:S(2)}) async-start(f32[8,2,2048]{2,1,0:T(2,128)} %broadcast_in_dim.54), calls=%async_computation.1 | async-start | bytes 262144 | tf_op jit(solution)/shard_map/all_to_all | solution.py:541
  89.1 18.8 %all-to-all-start.2 = ((f32[8,6,2048]{2,1,0:T(8,128)}), f32[8,6,2048]{2,1,0:T(8,128)S(1)}, u32[]{:S(2)}, u32[]{:S(2)}) async-start(f32[8,6,2048]{2,1,0:T(8,128)} %broadcast_in_dim.57), calls=%async_computation.2 | async-start | bytes 1048576 | tf_op jit(solution)/shard_map/all_to_all | solution.py:541
  113.2 17.2 %copy-start.3 = (f32[8,6,2048]{2,1,0:T(8,128)S(1)}, f32[8,6,2048]{2,1,0:T(8,128)}, u32[]{:S(2)}) copy-start(f32[8,6,2048]{2,1,0:T(8,128)} %copy-done.2) | copy-start | bytes 1179652
  113.2 5.2 %collective-permute-start.5 = (bf16[4,56,512]{2,1,0:T(8,128)(2,1)}, bf16[4,56,512]{2,1,0:T(8,128)(2,1)S(1)}, u32[]{:S(2)}, u32[]{:S(2)}) collective-permute-start(bf16[4,56,512]{2,1,0:T(8,128)(2,1)} %get-tuple-element.63.own_ref.grad_ref), channel_id=1, source_target_pairs={{0,1},{1,0},{2,3},{3,2},{4,5},{5,4},{6,7},{7,6},{8,9},{9,8},{10,11... | collective-permute-start | bytes 688136 | tf_op jit(solution)/shard_map/ppermute | solution.py:548
  113.2 5.2 %collective-permute-start.4 = (bf16[4,56,512]{2,1,0:T(8,128)(2,1)}, bf16[4,56,512]{2,1,0:T(8,128)(2,1)S(1)}, u32[]{:S(2)}, u32[]{:S(2)}) collective-permute-start(bf16[4,56,512]{2,1,0:T(8,128)(2,1)} %get-tuple-element.63.own_ref.grad_ref), channel_id=1, source_target_pairs={{1,2},{2,1},{3,4},{4,3},{5,6},{6,5},{9,10},{10,9},{11,12},{12,11},... | collective-permute-start | bytes 688136 | tf_op jit(solution)/shard_map/ppermute | solution.py:548
  125.3 10.9 %all-to-all-start.3 = ((f32[8,2,1024]{2,1,0:T(2,128)}), f32[8,2,1024]{2,1,0:T(2,128)S(1)}, u32[]{:S(2)}, u32[]{:S(2)}) async-start(f32[8,2,1024]{2,1,0:T(2,128)} %broadcast_in_dim.58), calls=%async_computation.3 | async-start | bytes 131072 | tf_op jit(solution)/shard_map/all_to_all | solution.py:541
  136.9 18.8 %copy-start.1 = (bf16[4,2,224,256]{3,2,1,0:T(8,128)(2,1)S(1)}, bf16[4,2,224,256]{3,2,1,0:T(8,128)(2,1)}, u32[]{:S(2)}) copy-start(bf16[4,2,224,256]{3,2,1,0:T(8,128)(2,1)} %get-tuple-element.69.act_ref) | copy-start | bytes 2752516
  152.4 13.7 %all-to-all-start.5 = ((f32[32,16,128]{2,1,0:T(8,128)}), f32[32,16,128]{2,1,0:T(8,128)S(1)}, u32[]{:S(2)}, u32[]{:S(2)}) async-start(f32[32,16,128]{2,1,0:T(8,128)} %bitcast.68), calls=%async_computation.5 | async-start | bytes 524288 | tf_op jit(solution)/shard_map/all_to_all | solution.py:786
  166.1 21.4 %all-to-all-start.6 = ((bf16[32,8,1024]{2,1,0:T(8,128)(2,1)}), bf16[32,8,1024]{2,1,0:T(8,128)(2,1)S(1)}, u32[]{:S(2)}, u32[]{:S(2)}) async-start(bf16[32,8,1024]{2,1,0:T(8,128)(2,1)} %fusion.2), calls=%async_computation.6 | async-start | bytes 1048576 | tf_op jit(solution)/shard_map/all_to_all | solution.py:556
  168.7 3.8 collective-permute-start.6
  169.4 4.7 %collective-permute-start.7 = (bf16[4,224,256]{2,1,0:T(8,128)(2,1)}, bf16[4,224,256]{2,1,0:T(8,128)(2,1)S(1)}, u32[]{:S(2)}, u32[]{:S(2)}) collective-permute-start(bf16[4,224,256]{2,1,0:T(8,128)(2,1)} %get-tuple-element.73.gc_ref), channel_id=1, source_target_pairs={{0,1},{1,0},{2,3},{3,2},{4,5},{5,4},{6,7},{7,6},{8,9},{9,8},{10,11... | collective-permute-start | bytes 1376264 | tf_op jit(solution)/shard_map/ppermute | solution.py:548
  187.5 33.7 %copy-start.5 = (bf16[32,8,1024]{2,1,0:T(8,128)(2,1)}, bf16[32,8,1024]{2,1,0:T(8,128)(2,1)S(1)}, u32[]{:S(2)}) copy-start(bf16[32,8,1024]{2,1,0:T(8,128)(2,1)S(1)} %all-to-all-done.6) | copy-start | bytes 1572868
  187.5 33.7 %all-to-all-start.4 = ((bf16[32,32,256]{2,1,0:T(8,128)(2,1)}), bf16[32,32,256]{2,1,0:T(8,128)(2,1)S(1)}, u32[]{:S(2)}, u32[]{:S(2)}) async-start(bf16[32,32,256]{2,1,0:T(8,128)(2,1)} %bitcast.17), calls=%async_computation.4 | async-start | bytes 1048576 | tf_op jit(solution)/shard_map/all_to_all | solution.py:556
  221.9 30.2 %all-to-all-start.7 = ((bf16[32,32,512]{2,1,0:T(8,128)(2,1)}), bf16[32,32,512]{2,1,0:T(8,128)(2,1)S(1)}, u32[]{:S(2)}, u32[]{:S(2)}) async-start(bf16[32,32,512]{2,1,0:T(8,128)(2,1)} %bitcast.64), calls=%async_computation.7 | async-start | bytes 2097152 | tf_op jit(solution)/shard_map/all_to_all | solution.py:556
  252.2 53.6 %all-to-all-start.9 = ((bf16[32,16,2048]{2,1,0:T(8,128)(2,1)}), bf16[32,16,2048]{2,1,0:T(8,128)(2,1)}, u32[]{:S(2)}, u32[]{:S(2)}) async-start(bf16[32,16,2048]{2,1,0:T(8,128)(2,1)} %bitcast.63), calls=%async_computation.9 | async-start | bytes 4194304 | tf_op jit(solution)/shard_map/all_to_all | solution.py:556
  305.7 98.8 %all-to-all-start.8 = ((bf16[32,32,2048]{2,1,0:T(8,128)(2,1)}), bf16[32,32,2048]{2,1,0:T(8,128)(2,1)}, u32[]{:S(2)}, u32[]{:S(2)}) async-start(bf16[32,32,2048]{2,1,0:T(8,128)(2,1)} %bitcast.62), calls=%async_computation.8 | async-start | bytes 8388608 | tf_op jit(solution)/shard_map/all_to_all | solution.py:556
  (17 other events, 49.4 us)
where the time goes:
time: 411 us; the launch traced here: 408 us
  waiting for transfers between devices  185 us (45%)
  Pallas kernels  72.7 us (18%)
  starting transfers between devices  69.8 us (17%)
  local copies, waits for them, and re-layouts  33.4 us (8%)
  matrix products  26.8 us (7%)
  other arithmetic  17.9 us (4%)
    all_to_all x5, waiting for transfers between devices, reduce_rows(): lax.all_to_all(pieces, axes, split_axis=0, concat_axis=0, tiled=True)  154 us
    pallas_call x13, Pallas kernels, call(): pl.pallas_call(kernel, name=name, out_shape=[jax.ShapeDtypeStruct(s, d) f...  72.7 us
    all_to_all x5, starting transfers between devices, reduce_rows(): lax.all_to_all(pieces, axes, split_axis=0, concat_axis=0, tiled=True)  30 us
    all_to_all x4, starting transfers between devices, copies_exchange(): lax.all_to_all(copies, 'space', split_axis=0, concat_axis=0, tiled=True)  25.8 us
    all_to_all x4, waiting for transfers between devices, copies_exchange(): lax.all_to_all(copies, 'space', split_axis=0, concat_axis=0, tiled=True)  21.7 us
    unnamed x51, local copies, waits for them, and re-layouts  20 us
    dot_general x4, matrix products, t_dot(): lax.dot_general(left, right, (((0,), (0,)), ((), ())), preferred_element_...  14.2 us
    reduce_sum x5, other arithmetic, reduce_rows(): return jnp.sum(received.astype(f32), axis=0)  9.48 us
  transfers between devices with their start and end apart: 18, of which 11 were waited for; matrix products, arithmetic and copies ran while one was open for 12% of the time, Pallas kernels for 5%

commit v1 on v0

--- a/solution.py
+++ b/solution.py
@@ -94,7 +94,31 @@
     return pltpu.roll(sums[0], 1, 0) + sums[1] + pltpu.roll(sums[2], rows - 1, 0)
 
 
-def first_kernel(par_ref, scal_ref, x_ref, w_ref, first_ref, actz_ref, actc_ref, even_ref, xpad, xe):
+def frame_of(slot):
+    parity = lax.axis_index("space") & 1
+    return parity if slot == 0 else 1 - parity
+
+
+def frame_mask(counts_ref, k, frame):
+    return jnp.where(2 * lax.axis_index("space") + frame < counts_ref[k], 1.0, 0.0).astype(f32)
+
+
+def cell_total(counts_ref, late, cells):
+    total = 0
+    for k in range(counts_ref.shape[0]):
+        total += (counts_ref[k] + 1) // 2 if late else counts_ref[k]
+    return (total * cells).astype(f32)
+
+
+def received_sum(refs):
+    total = None
+    for ref in refs:
+        for i in range(ref.shape[0]):
+            total = ref[i] if total is None else total + ref[i]
+    return total
+
+
+def first_kernel(counts_ref, x_ref, w_ref, first_ref, actz_ref, actc_ref, even_ref, xpad, xe):
     k = pl.program_id(0)
     _, _, height, width, _ = x_ref.shape
     pitch = xe.shape[1]
@@ -105,12 +129,12 @@
         xe[...] = jnp.zeros_like(xe)
 
     for slot, act_ref in ((0, actz_ref), (1, actc_ref)):
-        frame = par_ref[0] if slot == 0 else 1 - par_ref[0]
+        frame = frame_of(slot)
         for h in range(height):
             xpad[pl.ds(h * pitch, width), :] = x_ref[0, frame, h]
         first = dot(xpad[...], w_ref[...])
         first_ref[0, slot] = first
-        act_ref[0] = (gelu(first) * scal_ref[slot, k]).astype(bf16)
+        act_ref[0] = (gelu(first) * frame_mask(counts_ref, k, frame)).astype(bf16)
     for h in range(0, height, 2):
         put_lanes(xe, 0, x_ref[0, 0, h].astype(f32))
         even_ref[0, pl.ds(h // 2 * (pitch // 2), pitch // 2), :] = get_even(xe, 0, pitch // 2)
@@ -129,7 +153,7 @@
 
 
 def mid_kernel(
-    width, par_ref, scal_ref, rz_ref, oz_ref, oc_ref, rc_ref, taps_ref, up_ref,
+    width, counts_ref, rz_ref, oz_ref, oc_ref, rc_ref, taps_ref, up_ref,
     mid_ref, act_ref, even_ref, moment_ref, frames, sums, total,
 ):
     k = pl.program_id(0)
@@ -160,13 +184,13 @@
         lax.fori_loop(0, rows // chunk, step, 0)
         third = dot(act_ref[0, slot], up_ref[...])
         put_lanes(sums, slot * rows, third)
-        scale = scal_ref[slot, k]
+        scale = frame_mask(counts_ref, k, frame_of(slot))
         total[0] += row_sums(third) * scale
         total[1] += row_sums(third * third) * scale
     half = pitch // 2
     for j in range(rows // chunk):
         even_ref[0, pl.ds(half * j, half), :] = get_even(
-            sums, par_ref[0] * rows + chunk * j, half
+            sums, frame_of(0) * rows + chunk * j, half
         )
 
     @pl.when(k == pl.num_programs(0) - 1)
@@ -174,19 +198,19 @@
         moment_ref[...] = jnp.sum(total[...], axis=1)
 
 
-def norm_stats(received_ref, inverse):
-    totals = received_ref[0]
-    for i in range(1, received_ref.shape[0]):
-        totals = totals + received_ref[i]
-    center = totals[0:1] * inverse
-    return center, lax.rsqrt(totals[1:2] * inverse - center * center + eps)
+def norm_stats(refs, cells):
+    totals = received_sum(refs)
+    center = totals[0:1] / cells
+    return center, lax.rsqrt(totals[1:2] / cells - center * center + eps)
 
 
 def entry_kernel(
-    width, scal_ref, moments_ref, even_x_ref, even_ref, gain_ref, shift_ref, down_ref,
-    stats_ref, hat_ref, entry_ref, first_ref, act_ref,
-):
-    center, scale = norm_stats(moments_ref, scal_ref[4, 0])
+    width, cells, parts, counts_ref, *refs
+):
+    moments, refs = refs[:parts], refs[parts:]
+    (even_x_ref, even_ref, gain_ref, shift_ref, down_ref,
+     stats_ref, hat_ref, entry_ref, first_ref, act_ref) = refs
+    center, scale = norm_stats(moments, cell_total(counts_ref, False, cells))
     stats_ref[0:1] = center
     stats_ref[1:2] = scale
     clips, rows, channels = even_ref.shape
@@ -199,12 +223,12 @@
     late = dot(entry_ref[...], down_ref[...])
     first_ref[...] = late
     for k in range(clips):
-        act_ref[k] = (gelu(late[k * rows : (k + 1) * rows]) * scal_ref[2, k]).astype(bf16)
+        act_ref[k] = (gelu(late[k * rows : (k + 1) * rows]) * frame_mask(counts_ref, k, 0)).astype(bf16)
 
 
 def late_kernel(
-    width, scal_ref, rz_ref, own_ref, rc_ref, taps_ref, up_ref,
-    mid_ref, act_ref, sum_ref, moment_ref, frames,
+    width, counts_ref, rz_ref, own_ref, rc_ref, taps_ref, up_ref,
+    mid_ref, act_ref, sum_ref, moment_ref, frames, wide,
 ):
     clips, rows, channels = own_ref.shape
     pitch = 8
@@ -224,35 +248,32 @@
                 rows,
             )
             mid_ref[k, :, cols] = mid
-            act = jnp.where(valid_rows(mid.shape, pitch, width), gelu(mid), 0.0)
-            act_ref[k, :, cols] = act
+            wide[k, :, cols] = jnp.where(valid_rows(mid.shape, pitch, width), gelu(mid), 0.0)
         return 0
 
     lax.fori_loop(0, clips, clip_step, 0)
-
-
-def late_sum_kernel(scal_ref, act_in_ref, up_ref, act_ref, sum_ref, moment_ref):
-    clips, rows, channels = act_in_ref.shape
     for k in range(clips):
-        act_ref[pl.ds(k * rows, rows), :] = act_in_ref[k].astype(bf16)
+        act_ref[pl.ds(k * rows, rows), :] = wide[k].astype(bf16)
     late = dot(act_ref[...], up_ref[...]).astype(bf16)
     sum_ref[...] = late
-    wide = late.astype(f32)
+    late = late.astype(f32)
     one = two = None
     for k in range(clips):
-        block = wide[k * rows : (k + 1) * rows]
-        a = row_sums(block) * scal_ref[2, k]
-        b = row_sums(block * block) * scal_ref[2, k]
+        block = late[k * rows : (k + 1) * rows]
+        mask = frame_mask(counts_ref, k, 0)
+        a, b = row_sums(block) * mask, row_sums(block * block) * mask
         one, two = (a, b) if one is None else (one + a, two + b)
     moment_ref[0:1] = jnp.sum(one, axis=0, keepdims=True)
     moment_ref[1:2] = jnp.sum(two, axis=0, keepdims=True)
 
 
 def post_kernel(
-    width, scal_ref, moments_ref, sum_ref, skip_ref, gain_ref, shift_ref, pooled_grad_ref,
-    stats_ref, back_ref, pooled_ref, pre_ref, skip_grad_ref,
-):
-    center, scale = norm_stats(moments_ref, scal_ref[4, 1])
+    width, cells, parts, counts_ref, *refs
+):
+    moments, refs = refs[:parts], refs[parts:]
+    (sum_ref, skip_ref, gain_ref, shift_ref, pooled_grad_ref,
+     stats_ref, back_ref, pooled_ref, pre_ref, skip_grad_ref) = refs
+    center, scale = norm_stats(moments, cell_total(counts_ref, True, cells))
     stats_ref[0:1] = center
     stats_ref[1:2] = scale
     clips, rows, channels = sum_ref.shape
@@ -261,9 +282,10 @@
         hat = (sum_ref[k].astype(f32) - center) * scale
         post, slope = gelu_both(hat * gain_ref[...] + shift_ref[...] + skip_ref[k].astype(f32))
         keep = valid_rows(post.shape, 8, width)
-        weight = scal_ref[3, k]
-        pooled_ref[pl.ds(k, 1)] = jnp.sum(jnp.where(keep, post, 0.0), axis=0, keepdims=True) * weight
-        pre = jnp.where(keep, pooled_grad_ref[pl.ds(k, 1)] * weight * slope, 0.0)
+        mask = frame_mask(counts_ref, k, 0)
+        pool = ((counts_ref[k] + 1) // 2 * cells).astype(f32)
+        pooled_ref[pl.ds(k, 1)] = jnp.sum(jnp.where(keep, post, 0.0), axis=0, keepdims=True) * mask / pool
+        pre = jnp.where(keep, pooled_grad_ref[pl.ds(k, 1)] * mask / pool * slope, 0.0)
         pre_ref[k] = pre
         skip_grad_ref[k] = pre.astype(bf16)
         a, b = row_sums(pre), row_sums(pre * hat)
@@ -273,19 +295,17 @@
 
 
 def sum_grad_kernel(
-    width, scal_ref, back_ref, stats_ref, sum_ref, pre_ref, gain_ref, up_ref, mid_ref,
-    sum_grad_ref, mid_grad_ref,
-):
-    totals = back_ref[0]
-    for i in range(1, back_ref.shape[0]):
-        totals = totals + back_ref[i]
-    inverse = scal_ref[4, 1]
+    width, cells, parts, counts_ref, *refs
+):
+    received, refs = refs[:parts], refs[parts:]
+    (stats_ref, sum_ref, pre_ref, gain_ref, up_ref, mid_ref, sum_grad_ref, mid_grad_ref) = refs
+    totals = received_sum(received)[0:2] / cell_total(counts_ref, True, cells)
     center, scale = stats_ref[0:1], stats_ref[1:2]
     lead = gain_ref[...] * scale
     clips, rows, channels = sum_ref.shape
     for k in range(clips):
         hat = (sum_ref[k].astype(f32) - center) * scale
-        weight = scal_ref[2, k] * inverse
+        weight = frame_mask(counts_ref, k, 0)
         grad = lead * (pre_ref[k] - weight * (totals[0:1] + hat * totals[1:2]))
         grad = jnp.where(valid_rows(grad.shape, 8, width), grad, 0.0)
         sum_grad_ref[pl.ds(k * rows, rows), :] = grad.astype(bf16)
@@ -295,7 +315,7 @@
 
 
 def late_back_kernel(
-    width, scal_ref, rz_ref, own_ref, rc_ref, taps_ref, first_ref, down_ref, skip_back_ref, hat_ref,
+    width, counts_ref, rz_ref, own_ref, rc_ref, taps_ref, first_ref, down_ref, skip_back_ref, hat_ref,
     first_grad_ref, entry_grad_ref, back_ref, frames, grads,
 ):
     clips, rows, channels = own_ref.shape
@@ -315,7 +335,7 @@
                 lambda a, b: frames[a, pl.ds(pitch * b, rows), cols],
                 rows,
             )
-            grad = grad * scal_ref[2, k] * gelu_slope(first_ref[k, :, cols])
+            grad = grad * frame_mask(counts_ref, k, 0) * gelu_slope(first_ref[k, :, cols])
             grads[k, :, cols] = jnp.where(valid_rows(grad.shape, pitch, width), grad, 0.0)
         return 0
 
@@ -327,7 +347,7 @@
     for k in range(clips):
         block = entry[k * rows : (k + 1) * rows]
         entry_grad_ref[k] = block
-        masked = block * scal_ref[2, k]
+        masked = block * frame_mask(counts_ref, k, 0)
         a, b = row_sums(masked), row_sums(masked * hat_ref[k])
         one, two = (a, b) if one is None else (one + a, two + b)
     back_ref[0:1] = jnp.sum(one, axis=0, keepdims=True)
@@ -347,6 +367,14 @@
         return tuple(new)
 
     return steps, step
+
+
+def tap_table(rows_of_tap):
+    swapped = (lax.axis_index("space") & 1) == 1
+    rows = [jnp.where(swapped, rows_of_tap[(2 - i // 9) * 9 + i % 9], rows_of_tap[i]) for i in range(27)]
+    table = jnp.concatenate(rows + [jnp.zeros_like(rows[0])] * 5, axis=0)
+    table = jnp.transpose(table)
+    return jnp.concatenate([table, jnp.zeros((table.shape[0], 96), f32)], axis=1)
 
 
 def late_taps_kernel(rz_ref, own_ref, rc_ref, grad_ref, out_ref, frames):
@@ -369,11 +397,13 @@
         )
         zero = jnp.zeros((8, lanes), f32)
         totals = lax.fori_loop(0, steps, step, (zero,) * 27)
-        for i in range(27):
-            out_ref[pl.ds(i, 1), cols] = jnp.sum(totals[i], axis=0, keepdims=True)
-
-
-def third_taps_kernel(rz_ref, oz_ref, oc_ref, rc_ref, gz_ref, gc_ref, out_ref, frames, grads, total):
+        rows_of_tap = [jnp.sum(total, axis=0, keepdims=True) for total in totals]
+        out_ref[cols, :] = tap_table(rows_of_tap)
+
+
+def third_sums_kernel(
+    rz_ref, oz_ref, oc_ref, rc_ref, gz_ref, gc_ref, act_ref, sum_grad_ref, out_ref, frames, grads, total, product
+):
     k = pl.program_id(0)
     rows, channels = oz_ref.shape[1], oz_ref.shape[2]
     pitch = 16
@@ -384,7 +414,10 @@
     def _():
         clear_edges(frames, pitch, rows)
         total[...] = jnp.zeros_like(total)
-
+        product[...] = jnp.zeros_like(product)
+
+    for slot in range(2):
+        product[...] += t_dot(act_ref[0, slot], sum_grad_ref[0, slot])
     fill_frames(frames, (rz_ref, oz_ref, oc_ref, rc_ref), pitch, rows)
     grads[0] = gz_ref[0].astype(f32)
     grads[1] = gc_ref[0].astype(f32)
@@ -407,24 +440,43 @@
 
     @pl.when(k == pl.num_programs(0) - 1)
     def _():
-        out_ref[...] = jnp.sum(total[...], axis=1)
+        wide = product.shape[1]
+        out_ref[:, pl.ds(0, wide)] = product[...].astype(bf16)
+        out_ref[:, pl.ds(wide, lanes)] = tap_table(
+            [jnp.sum(total[i], axis=0, keepdims=True) for i in range(27)]
+        ).astype(bf16)
+
+
+def pack_kernel(parts, count, back_ref, third_ref, taps_ref, *refs):
+    received, (pooled_ref, out_ref) = refs[:count], refs[count:]
+    clips, late_wide = pooled_ref.shape
+    pooled_ref[...] = received_sum(received)[2:].astype(bf16)
+    pooled = pooled_ref[...].astype(f32)
+    wide = third_ref.shape[1]
+    own, own_third, own_taps = late_wide // parts, wide // parts, taps_ref.shape[0] // parts
+    for d in range(parts):
+        at = pl.ds(d * own // 128 * 128, 128)
+        third_at = pl.ds(d * own_third // 128 * 128, 128)
+        out_ref[d, 0:2] = back_ref[:, at]
+        out_ref[d, 2:4] = third_ref[:, third_at]
+        out_ref[d, 4 : 4 + clips] = pooled[:, d * own // 128 * 128 : d * own // 128 * 128 + 128]
+        out_ref[d, pl.ds(4 + clips, own_taps)] = taps_ref[pl.ds(d * own_taps, own_taps), :]
 
 
 def third_grad_kernel(
-    width, par_ref, scal_ref, back_ref, stats_ref, act_ref, mid_ref, entry_grad_ref, gain_ref, up_ref,
-    sum_grad_ref, gz_ref, gc_ref, placed,
-):
+    width, cells, parts, counts_ref, *refs
+):
+    received, refs = refs[:parts], refs[parts:]
+    (stats_ref, act_ref, mid_ref, entry_grad_ref, gain_ref, up_ref,
+     sum_grad_ref, gz_ref, gc_ref, placed) = refs
     k = pl.program_id(0)
-    totals = back_ref[0]
-    for i in range(1, back_ref.shape[0]):
-        totals = totals + back_ref[i]
+    totals = received_sum(received) / cell_total(counts_ref, False, cells)
     rows = act_ref.shape[2]
     pitch = 16
     chunk = 2 * pitch
     half = pitch // 2
     center, scale = stats_ref[0:1], stats_ref[1:2]
     lead = gain_ref[...] * scale
-    inverse = scal_ref[4, 0]
 
     @pl.when(k == 0)
     def _():
@@ -432,10 +484,10 @@
 
     for j in range(rows // chunk):
         put_even(
-            placed, par_ref[0] * rows + chunk * j, lead * entry_grad_ref[0, pl.ds(half * j, half), :]
+            placed, frame_of(0) * rows + chunk * j, lead * entry_grad_ref[0, pl.ds(half * j, half), :]
         )
     for slot, out in ((0, gz_ref), (1, gc_ref)):
-        weight = scal_ref[slot, k] * inverse
+        weight = frame_mask(counts_ref, k, frame_of(slot))
         slope_hat = -(lead * scale * totals[1:2]) * weight
         offset = -(lead * (totals[0:1] - center * scale * totals[1:2])) * weight
         third = dot(act_ref[0, slot], up_ref[...])
@@ -446,8 +498,8 @@
 
 
 def first_grad_kernel(
-    width, par_ref, scal_ref, rz_ref, gz_ref, gc_ref, rc_ref, taps_ref, first_ref, x_ref,
-    grad_ref, down_grad_ref, frames, xpad,
+    width, counts_ref, rz_ref, gz_ref, gc_ref, rc_ref, taps_ref, first_ref, x_ref,
+    grad_ref, down_grad_ref, frames, xpad, product,
 ):
     k = pl.program_id(0)
     rows = gz_ref.shape[1]
@@ -459,14 +511,14 @@
     def _():
         clear_edges(frames, pitch, rows)
         xpad[...] = jnp.zeros_like(xpad)
-        down_grad_ref[...] = jnp.zeros_like(down_grad_ref)
+        product[...] = jnp.zeros_like(product)
 
     fill_frames(frames, (rz_ref, gz_ref, gc_ref, rc_ref), pitch, rows)
     for slot in range(2):
-        frame = par_ref[0] if slot == 0 else 1 - par_ref[0]
+        frame = frame_of(slot)
         for h in range(height):
             xpad[pl.ds(slot * rows + h * pitch, width), :] = x_ref[0, frame, h]
-        scale = scal_ref[slot, k]
+        scale = frame_mask(counts_ref, k, frame)
 
         def step(c, _):
             start = pl.multiple_of(c * chunk, chunk)
@@ -481,22 +533,25 @@
             return 0
 
         lax.fori_loop(0, rows // chunk, step, 0)
-    down_grad_ref[...] += t_dot(xpad[...], grad_ref[0])
-
-
-def clip_grad_kernel(par_ref, grad_ref, down_ref, entry_grad_ref, out_ref, wide):
+    product[...] += t_dot(xpad[...], grad_ref[0])
+
+    @pl.when(k == pl.num_programs(0) - 1)
+    def _():
+        down_grad_ref[...] = product[...].astype(bf16)
+
+
+def clip_grad_kernel(grad_ref, down_ref, entry_grad_ref, out_ref, wide):
     _, _, height, width, _ = out_ref.shape
     pitch = 16
     half = pitch // 2
     rows = height * pitch
     for slot in range(2):
-        frame = par_ref[0] if slot == 0 else 1 - par_ref[0]
         put_lanes(wide, slot * rows, dot_t(grad_ref[0, pl.ds(slot * rows, rows), :], down_ref[...]))
     for j in range(height // 2):
-        at = par_ref[0] * rows + 2 * pitch * j
+        at = frame_of(0) * rows + 2 * pitch * j
         put_even(wide, at, get_even(wide, at, half) + entry_grad_ref[0, pl.ds(half * j, half), :])
     for slot in range(2):
-        frame = par_ref[0] if slot == 0 else 1 - par_ref[0]
+        frame = frame_of(slot)
         for h in range(height):
             out_ref[0, frame, h] = get_lanes(wide, slot * rows + h * pitch, width).astype(bf16)
 
@@ -535,10 +590,14 @@
     )(*[a for a, _ in inputs])
 
 
-def copies_exchange(values):
+def group_parts(values):
     size = lax.axis_size("space")
-    copies = jnp.broadcast_to(values[None], (size,) + values.shape)
-    return lax.all_to_all(copies, "space", split_axis=0, concat_axis=0, tiled=True)
+    if size > 8:
+        copies = jnp.broadcast_to(values[None], (size,) + values.shape)
+        return [lax.all_to_all(copies, "space", split_axis=0, concat_axis=0, tiled=True)]
+    pair = values + lax.ppermute(values, "space", [(i, i ^ 1) for i in range(size)])
+    others = [lax.ppermute(pair, "space", [(i, i ^ b) for i in range(size)]) for b in range(2, size, 2)]
+    return [part[None] for part in [pair] + others]
 
 
 def swap_neighbours(to_z, to_core):
@@ -548,13 +607,98 @@
     return lax.ppermute(to_z, "space", z), lax.ppermute(to_core, "space", core)
 
 
-def reduce_rows(term, axes=("clip", "space")):
-    parts = 1
-    for axis in axes:
-        parts *= lax.axis_size(axis)
+def reduce_rows(term):
+    return add_rows(send_rows(term))
+
+
+def add_rows(received):
+    return jnp.sum(received.astype(f32), axis=0)
+
+
+def send_rows(term):
+    parts = lax.axis_size("clip") * lax.axis_size("space")
     pieces = term.astype(bf16).reshape((parts, term.shape[0] // parts) + term.shape[1:])
-    received = lax.all_to_all(pieces, axes, split_axis=0, concat_axis=0, tiled=True)
-    return jnp.sum(received.astype(f32), axis=0)
+    return lax.all_to_all(pieces, ("clip", "space"), split_axis=0, concat_axis=0, tiled=True)
+
+
+def core_swap(values):
+    return lax.ppermute(values, "space", [(i, i ^ 1) for i in range(lax.axis_size("space"))])
+
+
+def own_rows(left_ref, block, out):
+    core = lax.axis_index("space") & 1
+    out[0] = jnp.transpose(left_ref[...])
+    for j in range(out.shape[1] // block // 2):
+        start = pl.multiple_of((2 * j + core) * block, block)
+        out[1, pl.ds(j * block, block), :] = out[0, pl.ds(start, block), :]
+
+
+def skip_product_kernel(block, left_ref, left_other_ref, right_ref, right_other_ref, out_ref, left, left_other):
+    half = left.shape[1] // 2
+
+    @pl.when(pl.program_id(0) == 0)
+    def _():
+        own_rows(left_ref, block, left)
+        own_rows(left_other_ref, block, left_other)
+
+    total = dot(left[1, pl.ds(0, half)], right_ref[...]) + dot(left_other[1, pl.ds(0, half)], right_other_ref[...])
+    for j in range(out_ref.shape[0]):
+        out_ref[j] = total[j * block : (j + 1) * block].astype(bf16)
+
+
+def skip_product(left, left_other, right, right_other, parts):
+    block = left.shape[1] // parts
+    wide = right.shape[1]
+    lanes = min(wide, 512)
+    rows, deep = left.shape
+    return pl.pallas_call(
+        functools.partial(skip_product_kernel, block),
+        name="skip_product",
+        grid=(wide // lanes,),
+        out_shape=jax.ShapeDtypeStruct((parts // 2, block, wide), bf16),
+        in_specs=[pl.BlockSpec((rows, deep), lambda n: (0, 0))] * 2
+        + [pl.BlockSpec((rows, lanes), lambda n: (0, n))] * 2,
+        out_specs=pl.BlockSpec((parts // 2, block, lanes), lambda n: (0, 0, n)),
+        scratch_shapes=[pltpu.VMEM((2, deep, rows), bf16)] * 2,
+        compiler_params=pltpu.CompilerParams(vmem_limit_bytes=60 * mib),
+        cost_estimate=pl.CostEstimate(
+            flops=2 * rows * deep * wide, bytes_accessed=deep * wide + 4 * rows * (deep + wide), transcendentals=0
+        ),
+    )(left, left_other, right, right_other)
+
+
+def two_products_kernel(
+    up_block, down_block, act_ref, act_other_ref, sum_ref, sum_other_ref,
+    entry_ref, entry_other_ref, first_ref, first_other_ref, out_ref, act, act_other, entry, entry_other,
+):
+    own_rows(act_ref, up_block, act)
+    own_rows(act_other_ref, up_block, act_other)
+    own_rows(entry_ref, down_block, entry)
+    own_rows(entry_other_ref, down_block, entry_other)
+    half = act.shape[1] // 2
+    up = dot(act[1, pl.ds(0, half)], sum_ref[...]) + dot(act_other[1, pl.ds(0, half)], sum_other_ref[...])
+    half = entry.shape[1] // 2
+    down = dot(entry[1, pl.ds(0, half)], first_ref[...]) + dot(entry_other[1, pl.ds(0, half)], first_other_ref[...])
+    fold = up.shape[1] // down.shape[1]
+    part = down_block // fold
+    for j in range(out_ref.shape[0]):
+        block = down[j * down_block : (j + 1) * down_block]
+        block = jnp.concatenate([block[i * part : (i + 1) * part] for i in range(fold)], axis=1)
+        out_ref[j] = jnp.concatenate([up[j * up_block : (j + 1) * up_block], block], axis=0).astype(bf16)
+
+
+def after(values, token):
+    return lax.optimization_barrier((values, token))[0]
+
+
+def sum_over_clip(pieces):
+    return lax.psum_scatter(pieces, "clip", scatter_dimension=0, tiled=True)
+
+
+def sum_over_chips(pieces):
+    size = lax.axis_size("space")
+    groups = [[2 * z + c for z in range(size // 2)] for c in range(2)]
+    return lax.psum_scatter(pieces, "space", scatter_dimension=0, tiled=True, axis_index_groups=groups)
 
 
 def per_device(
@@ -570,35 +714,13 @@
     rows = height * 16
     late_rows = height // 2 * 8
     late_all = clips * late_rows
-    slab = lax.axis_index("space")
-    parity = slab & 1
-    par = parity.reshape(1)
-    flip = (parity == 1)
-
-    frame_ids = 2 * slab + jnp.stack((parity, 1 - parity))
-    masks = (frame_ids[:, None] < frame_counts[None, :]).astype(f32)
-    late_mask = (2 * slab < frame_counts).astype(f32)
-    late_counts = ((frame_counts + 1) // 2).astype(f32)
-    cells = (height // 2) * half_width
-    third_total = jnp.sum(frame_counts).astype(f32) * (height * width)
-    late_total = jnp.sum(late_counts) * cells
-    inverses = jnp.stack((1.0 / third_total, 1.0 / late_total))
-    scal = jnp.concatenate(
-        (
-            masks,
-            late_mask[None],
-            (late_mask / (late_counts * cells))[None],
-            jnp.pad(inverses, (0, clips - 2))[None],
-        )
-    )
+    flip = (lax.axis_index("space") & 1) == 1
+    cells = height * width
+    late_cells = (height // 2) * half_width
 
     def tap_rows(kernel):
         taps = jnp.transpose(kernel).reshape(3, 9, -1)
         return jnp.where(flip, taps[::-1], taps).reshape(27, -1)
-
-    def tap_columns(rows_out):
-        taps = rows_out.reshape(3, 9, -1)
-        return jnp.transpose(jnp.where(flip, taps[::-1], taps).reshape(27, -1))
 
     third_taps = tap_rows(third_depth)
     late_taps = tap_rows(fourth_depth)
@@ -613,7 +735,7 @@
 
     first, act_z, act_c, even_x = call(
         first_kernel, "first",
-        [(par, "s"), (scal, "s"), (clip_input, "c"), (third_down, "w")],
+        [(frame_counts, "s"), (clip_input, "c"), (third_down, "w")],
         [
             ((clips, 2, rows, inner), f32, "c"),
             ((clips, rows, inner), bf16, "c"),
@@ -626,7 +748,7 @@
     got_z, got_c = swap_neighbours(act_z, act_c)
     mid, mid_act, even_sum, moments = call(
         functools.partial(mid_kernel, width), "mid",
-        [(par, "s"), (scal, "s"), (got_z, "c"), (act_z, "c"), (act_c, "c"), (got_c, "c"),
+        [(frame_counts, "s"), (got_z, "c"), (act_z, "c"), (act_c, "c"), (got_c, "c"),
          (third_taps, "w"), (third_up, "w")],
         [
             ((clips, 2, rows, inner), f32, "c"),
@@ -641,9 +763,10 @@
         ],
         clips=clips,
     )
+    moments = [(part, "w") for part in group_parts(moments)]
     stats, even_hat, entry, late_first, late_act = call(
-        functools.partial(entry_kernel, half_width), "entry",
-        [(scal, "s"), (copies_exchange(moments), "w"), (even_x, "w"), (even_sum, "w"),
+        functools.partial(entry_kernel, half_width, cells, len(moments)), "entry",
+        [(frame_counts, "s"), *moments, (even_x, "w"), (even_sum, "w"),
          (third_gain, "w"), (third_shift, "w"), (fourth_down, "w")],
         [
             ((2, channels), f32, "w"),
@@ -657,29 +780,25 @@
     late_first = late_first.reshape(clips, late_rows, late_inner)
     late_z, late_c = swap_neighbours(late_act, late_act)
     skipped = dot(entry, fourth_skip).astype(bf16).reshape(clips, late_rows, late_wide)
-    late_mid, late_mid_wide = call(
-        lambda scal_ref, z, o, c, t, m, a, fr: late_kernel(
-            half_width, scal_ref, z, o, c, t, None, m, a, None, None, fr
-        ),
-        "late_mid",
-        [(scal, "s"), (late_z, "w"), (late_act, "w"), (late_c, "w"), (late_taps, "w")],
-        [((clips, late_rows, late_inner), f32, "w"), ((clips, late_rows, late_inner), f32, "w")],
-        [pltpu.VMEM((3, late_rows + 16, late_inner), f32)],
-    )
-    late_mid_act, late_sum, late_moments = call(
-        late_sum_kernel, "late_sum",
-        [(scal, "s"), (late_mid_wide, "w"), (fourth_up, "w")],
-        [
+    late_mid, late_mid_act, late_sum, late_moments = call(
+        functools.partial(late_kernel, half_width), "late_mid",
+        [(frame_counts, "s"), (late_z, "w"), (late_act, "w"), (late_c, "w"), (late_taps, "w"), (fourth_up, "w")],
+        [
+            ((clips, late_rows, late_inner), f32, "w"),
             ((late_all, late_inner), bf16, "w"),
             ((late_all, late_wide), bf16, "w"),
             ((2, late_wide), f32, "w"),
         ],
-        [],
+        [
+            pltpu.VMEM((3, late_rows + 16, late_inner), f32),
+            pltpu.VMEM((clips, late_rows, late_inner), f32),
+        ],
     )
     late_sum = late_sum.reshape(clips, late_rows, late_wide)
+    late_moments = [(part, "w") for part in group_parts(late_moments)]
     late_stats, late_back, pooled_term, pre_grad, skip_grad = call(
-        functools.partial(post_kernel, half_width), "post",
-        [(scal, "s"), (copies_exchange(late_moments), "w"), (late_sum, "w"), (skipped, "w"),
+        functools.partial(post_kernel, half_width, late_cells, len(late_moments)), "post",
+        [(frame_counts, "s"), *late_moments, (late_sum, "w"), (skipped, "w"),
          (fourth_gain, "w"), (fourth_shift, "w"), (pooled_grad, "w")],
         [
             ((2, late_wide), f32, "w"),
@@ -690,30 +809,29 @@
         ],
         [],
     )
-    received = copies_exchange(jnp.concatenate((late_back, pooled_term)))
-    pooled = jnp.sum(received[:, 2:], axis=0).astype(bf16)
-    logits = dot(pooled, classifier) + class_bias
+    received = group_parts(jnp.concatenate((late_back, pooled_term)))
     skip_rows = skip_grad.reshape(late_all, late_wide)
     skip_back = dot_t(skip_rows, fourth_skip)
-    fourth_skip_term = t_dot(entry, skip_rows)
+    parts = lax.axis_size("clip") * lax.axis_size("space")
+    by_pairs = channels // parts % 32 == 0 and late_inner // parts % 16 == 0
+    if by_pairs:
+        entry_other = core_swap(entry)
+        skip_pieces = skip_product(entry, entry_other, after(skip_rows, received[0]), core_swap(skip_rows), parts)
+        late_stats = after(late_stats, skip_pieces)
+        skip_pieces = sum_over_clip(skip_pieces)
+    else:
+        fourth_skip_grad = reduce_rows(t_dot(entry, skip_rows))
     late_sum_grad, late_mid_grad = call(
-        functools.partial(sum_grad_kernel, half_width), "sum_grad",
-        [(scal, "s"), (received, "w"), (late_stats, "w"), (late_sum, "w"), (pre_grad, "w"),
+        functools.partial(sum_grad_kernel, half_width, late_cells, len(received)), "sum_grad",
+        [(frame_counts, "s"), *[(part, "w") for part in received], (late_stats, "w"), (late_sum, "w"), (pre_grad, "w"),
          (fourth_gain, "w"), (fourth_up, "w"), (late_mid, "w")],
         [((late_all, late_wide), bf16, "w"), ((clips, late_rows, late_inner), bf16, "w")],
         [],
     )
     late_gz, late_gc = swap_neighbours(late_mid_grad, late_mid_grad)
-    fourth_up_term = t_dot(late_mid_act, late_sum_grad)
-    (fourth_depth_term,) = call(
-        late_taps_kernel, "late_taps",
-        [(late_z, "w"), (late_act, "w"), (late_c, "w"), (late_mid_grad, "w")],
-        [((27, late_inner), f32, "w")],
-        [pltpu.VMEM((3, clips, late_rows + 16, late_inner), f32)],
-    )
     late_first_grad, entry_grad, third_back = call(
         functools.partial(late_back_kernel, half_width), "late_back",
-        [(scal, "s"), (late_gz, "w"), (late_mid_grad, "w"), (late_gc, "w"), (late_taps, "w"),
+        [(frame_counts, "s"), (late_gz, "w"), (late_mid_grad, "w"), (late_gc, "w"), (late_taps, "w"),
          (late_first, "w"), (fourth_down, "w"), (skip_back, "w"), (even_hat, "w")],
         [
             ((late_all, late_inner), bf16, "w"),
@@ -725,10 +843,31 @@
             pltpu.VMEM((clips, late_rows, late_inner), f32),
         ],
     )
-    fourth_down_term = t_dot(entry, late_first_grad)
+    back_parts = group_parts(third_back)
+    (late_taps_table,) = call(
+        late_taps_kernel, "late_taps",
+        [(late_z, "w"), (late_act, "w"), (late_c, "w"), (after(late_mid_grad, back_parts[0]), "w")],
+        [((late_inner, 128), f32, "w")],
+        [pltpu.VMEM((3, clips, late_rows + 16, late_inner), f32)],
+    )
+    if by_pairs:
+        up_block, down_block = late_inner // parts, channels // parts
+        (pieces,) = call(
+            functools.partial(two_products_kernel, up_block, down_block), "two_products",
+            [(late_mid_act, "w"), (core_swap(late_mid_act), "w"), (after(late_sum_grad, back_parts[0]), "w"), (core_swap(late_sum_grad), "w"),
+             (entry, "w"), (entry_other, "w"), (late_first_grad, "w"), (core_swap(late_first_grad), "w")],
+            [((parts // 2, up_block + down_block * late_inner // late_wide, late_wide), bf16, "w")],
+            [pltpu.VMEM((2, late_inner, late_all), bf16)] * 2 + [pltpu.VMEM((2, channels, late_all), bf16)] * 2,
+        )
+        stats = after(stats, pieces)
+        pieces = sum_over_clip(pieces)
+    else:
+        fourth_up_grad = reduce_rows(t_dot(late_mid_act, late_sum_grad))
+        fourth_down_grad = reduce_rows(t_dot(entry, late_first_grad))
+    back_parts = [(part, "w") for part in back_parts]
     third_sum_grad, grad_z, grad_c = call(
-        functools.partial(third_grad_kernel, width), "third_grad",
-        [(par, "s"), (scal, "s"), (copies_exchange(third_back), "w"), (stats, "w"), (mid_act, "c"), (mid, "c"),
+        functools.partial(third_grad_kernel, width, cells, len(back_parts)), "third_grad",
+        [(frame_counts, "s"), *back_parts, (stats, "w"), (mid_act, "c"), (mid, "c"),
          (entry_grad, "c"), (third_gain, "w"), (third_up, "w")],
         [
             ((clips, 2, rows, channels), bf16, "c"),
@@ -739,76 +878,86 @@
         clips=clips,
     )
     third_gz, third_gc = swap_neighbours(grad_z, grad_c)
-    third_up_term = t_dot(
-        mid_act.reshape(clips * 2 * rows, inner), third_sum_grad.reshape(clips * 2 * rows, channels)
-    )
-    (third_depth_term,) = call(
-        third_taps_kernel, "third_taps",
-        [(got_z, "c"), (act_z, "c"), (act_c, "c"), (got_c, "c"), (grad_z, "c"), (grad_c, "c")],
-        [((27, inner), f32, "w")],
+    (third_terms,) = call(
+        third_sums_kernel, "third_sums",
+        [(got_z, "c"), (act_z, "c"), (act_c, "c"), (got_c, "c"), (grad_z, "c"), (grad_c, "c"),
+         (mid_act, "c"), (third_sum_grad, "c")],
+        [((inner, channels + 128), bf16, "w")],
         [
             pltpu.VMEM((4, rows + 32, inner), f32),
             pltpu.VMEM((2, rows, inner), f32),
             pltpu.VMEM((27, 8, inner), f32),
+            pltpu.VMEM((inner, channels), f32),
         ],
         clips=clips,
     )
+    first = after(first, third_terms)
+    third_terms = send_rows(third_terms)
     first_grad, third_down_term = call(
         functools.partial(first_grad_kernel, width), "first_grad",
-        [(par, "s"), (scal, "s"), (third_gz, "c"), (grad_z, "c"), (grad_c, "c"), (third_gc, "c"),
+        [(frame_counts, "s"), (third_gz, "c"), (grad_z, "c"), (grad_c, "c"), (third_gc, "c"),
          (third_taps, "w"), (first, "c"), (clip_input, "c")],
-        [((clips, 2 * rows, inner), bf16, "c"), ((channels, inner), f32, "w")],
-        [pltpu.VMEM((4, rows + 32, inner), f32), pltpu.VMEM((2 * rows, channels), bf16)],
+        [((clips, 2 * rows, inner), bf16, "c"), ((channels, inner), bf16, "w")],
+        [
+            pltpu.VMEM((4, rows + 32, inner), f32),
+            pltpu.VMEM((2 * rows, channels), bf16),
+            pltpu.VMEM((channels, inner), f32),
+        ],
         clips=clips,
     )
+    third_down_rows = send_rows(third_down_term)
+    if by_pairs:
+        pieces = jnp.concatenate((after(skip_pieces, first_grad), pieces), axis=1)
+        pieces = sum_over_chips(pieces)[0].astype(f32)
+        fourth_skip_grad = pieces[:down_block]
+        fourth_up_grad = pieces[down_block : down_block + up_block]
+        fold = late_wide // late_inner
+        fourth_down_grad = jnp.moveaxis(
+            pieces[down_block + up_block :].reshape(-1, fold, late_inner), 1, 0
+        ).reshape(down_block, late_inner)
+    third_terms = add_rows(after(third_terms, first_grad))
     (clip_grad,) = call(
         clip_grad_kernel, "clip_grad",
-        [(par, "s"), (first_grad, "c"), (third_down, "w"), (entry_grad, "c")],
+        [(first_grad, "c"), (third_down, "w"), (entry_grad, "c")],
         [(clip_input.shape, bf16, "c")],
         [pltpu.VMEM((channels // 128, 2 * rows, 128), f32)],
         clips=clips,
     )
 
-    parts = lax.axis_size("clip") * lax.axis_size("space")
-    small_terms = [
-        term.reshape(parts, -1)
-        for term in (
-            third_back[1], third_back[0], late_back[1], late_back[0],
-            tap_columns(third_depth_term), tap_columns(fourth_depth_term),
-        )
-    ]
-    widths = [term.shape[1] for term in small_terms]
-    pooled_pieces = jnp.moveaxis(pooled.astype(f32).reshape(clips, parts, -1), 1, 0)
-    own_width = pooled_pieces.shape[2]
-    packed = jnp.concatenate(small_terms + [pooled_pieces.reshape(parts, -1)], axis=1)
-    length = packed.shape[1]
-    packed = jnp.pad(packed, ((0, 0), (0, -length % 1024))).reshape(parts, -1, 128)
-    received = lax.all_to_all(packed, ("clip", "space"), split_axis=0, concat_axis=0, tiled=True)
-    received = received.reshape(parts, -1)
-    totals = jnp.sum(received[:, : sum(widths)], axis=0)
-    ends = [sum(widths[: i + 1]) for i in range(len(widths))]
-    pieces = [totals[end - size : end] for size, end in zip(widths, ends)]
-    gathered = received[:, sum(widths) : length].reshape(
-        lax.axis_size("clip"), lax.axis_size("space"), clips, own_width
-    )[:, 0]
+    own, own_third, own_taps = late_wide // parts, channels // parts, late_inner // parts
+    pooled, packed = call(
+        functools.partial(pack_kernel, parts, len(received)), "pack",
+        [(late_back, "w"), (third_back, "w"), (late_taps_table, "w"), *[(part, "w") for part in received]],
+        [((clips, late_wide), bf16, "w"), ((parts, 4 + clips + own_taps, 128), f32, "w")],
+        [],
+    )
+    logits = dot(pooled, classifier) + class_bias
+    packed = lax.all_to_all(packed, ("clip", "space"), split_axis=0, concat_axis=0, tiled=True)
+    packed = after(packed, first_grad)
+    device = lax.axis_index("clip") * lax.axis_size("space") + lax.axis_index("space")
+    totals = jnp.sum(packed, axis=0)
+    late_sums = lax.dynamic_slice_in_dim(totals[0:2], device * own % 128, own, 1)
+    third_sums = lax.dynamic_slice_in_dim(totals[2:4], device * own_third % 128, own_third, 1)
+    fourth_depth_grad = totals[4 + clips :, :27]
+    gathered = packed.reshape((lax.axis_size("clip"), lax.axis_size("space")) + packed.shape[1:])[:, 0, 4 : 4 + clips]
+    gathered = lax.dynamic_slice_in_dim(gathered.reshape(-1, 128), device * own % 128, own, 1)
     classifier_grad = lax.dot_general(
-        gathered.reshape(-1, own_width), logit_grad, (((0,), (0,)), ((), ())),
-        precision=lax.Precision.HIGHEST,
+        gathered, logit_grad, (((0,), (0,)), ((), ())), precision=lax.Precision.HIGHEST
     )
     return (
         logits,
         clip_grad,
-        reduce_rows(third_down_term),
-        pieces[4].reshape(-1, 27),
-        reduce_rows(third_up_term),
-        pieces[0],
-        pieces[1],
-        reduce_rows(fourth_down_term),
-        reduce_rows(fourth_skip_term),
-        pieces[5].reshape(-1, 27),
-        reduce_rows(fourth_up_term),
-        pieces[2],
-        pieces[3],
+        add_rows(third_down_rows),
+        third_terms[:, channels : channels + 27],
+        third_terms[:, :channels],
+        third_sums[1],
+        third_sums[0],
+        fourth_down_grad,
+        fourth_skip_grad,
+        fourth_depth_grad,
+        fourth_up_grad,
+        late_sums[1],
+        late_sums[0],
         classifier_grad,
         jnp.sum(logit_grad, axis=0),
     )

time: 411 us -> 243 us (0.59)
  waiting for transfers between devices: 185 us -> 37.9 us
  starting transfers between devices: 69.8 us -> 54.2 us
  matrix products: 26.8 us -> 13.1 us
  Pallas kernels: 72.7 us -> 86.2 us
  between operations: 2.39 us -> 14.2 us
  other arithmetic: 17.9 us -> 8.34 us
  local copies, waits for them, and re-layouts: 33.4 us -> 27.9 us
    all_to_all x9 -> x2, waiting for transfers between devices: 176 us -> 13.6 us  [send_rows(): lax.all_to_all(pieces, ('clip', 'space'), split_axis=0, concat_axis=0, ti...]
    all_to_all x9 -> x2, starting transfers between devices: 55.7 us -> 9.37 us  [send_rows(): lax.all_to_all(pieces, ('clip', 'space'), split_axis=0, concat_axis=0, ti...]
    ppermute x0 -> x21, starting transfers between devices: none -> 28.4 us  [the longest x12 16.9 us: group_parts(): lax.ppermute(pair, 'space', [(i, i ^ b) for i in range(size)])]
    ppermute x0 -> x21, waiting for transfers between devices: none -> 22.1 us  [the longest x12 18.8 us: group_parts(): lax.ppermute(pair, 'space', [(i, i ^ b) for i in range(size)])]
    dot_general x5 -> x1, matrix products: 15.2 us -> 1.04 us  [per_device(): lax.dot_general(gathered, logit_grad, (((0,), (0,)), ((), ())), precision...]
    reduce_sum x9 -> x3, other arithmetic: 11.5 us -> 0.83 us  [the longest x2 0.79 us: add_rows(): return jnp.sum(received.astype(f32), axis=0)]
    pallas_call x13 -> x14, Pallas kernels: 72.7 us -> 80.8 us  [call(): pl.pallas_call(kernel, name=name, out_shape=[jax.ShapeDtypeStruct(s, d) f...]
    all_to_all x1, waiting for transfers between devices: 6.36 us -> 0.01 us  [per_device(): lax.all_to_all(packed, ('clip', 'space'), split_axis=0, concat_axis=0, ti...]
  transfers between devices with their start and end apart: 18 -> 35, of which waited for: 11 -> 11; matrix products, arithmetic and copies ran while one was open for 12% -> 13% of each run, Pallas kernels for 5% -> 21%
where the time goes in v1:
time: 243 us; the launch traced here: 242 us
  Pallas kernels  86.2 us (35%)
  starting transfers between devices  54.2 us (22%)
  waiting for transfers between devices  37.9 us (16%)
  local copies, waits for them, and re-layouts  27.9 us (11%)
  between operations  14.2 us (6%)
  matrix products  13.1 us (5%)
  other arithmetic  8.34 us (3%)
    pallas_call x14, Pallas kernels, call(): pl.pallas_call(kernel, name=name, out_shape=[jax.ShapeDtypeStruct(s, d) f...  80.8 us
    unnamed x74, local copies, waits for them, and re-layouts  20.9 us
    ppermute x12, waiting for transfers between devices, group_parts(): lax.ppermute(pair, 'space', [(i, i ^ b) for i in range(size)])  18.8 us
    ppermute x12, starting transfers between devices, group_parts(): lax.ppermute(pair, 'space', [(i, i ^ b) for i in range(size)])  16.9 us
    all_to_all x2, waiting for transfers between devices, send_rows(): lax.all_to_all(pieces, ('clip', 'space'), split_axis=0, concat_axis=0, ti...  13.6 us
    ppermute x4, starting transfers between devices, group_parts(): lax.ppermute(values, 'space', [(i, i ^ 1) for i in range(size)])  10.9 us
    all_to_all x2, starting transfers between devices, send_rows(): lax.all_to_all(pieces, ('clip', 'space'), split_axis=0, concat_axis=0, ti...  9.37 us
    ppermute x4, starting transfers between devices, swap_neighbours(): lax.ppermute(to_core, 'space', core)  8.69 us
  transfers between devices with their start and end apart: 35, of which 11 were waited for; matrix products, arithmetic and copies ran while one was open for 13% of the time, Pallas kernels for 21%

profile of v1, /device:TPU:0, one launch (start us, length us, event | category | flops | bytes accessed | tf_op | source)
XLA Modules:
  0.0 241.9 jit_solution(13377131523693873123)
XLA Ops:
  7.2 4.9 %copy.34.x_ref = bf16[4,2,14,14,1024]{4,3,2,1,0:T(8,128)(2,1)} copy(bf16[4,2,14,14,1024]{4,1,3,2,0:T(2,128)(2,1)} %param.16) | data formatting | bytes 6422528 | tf_op args[0]
  12.2 5.4 %first.1 = (f32[4,2,224,256]{3,2,1,0:T(8,128)}, bf16[4,224,256]{2,1,0:T(8,128)(2,1)}, bf16[4,224,256]{2,1,0:T(8,128)(2,1)}, f32[4,56,1024]{2,1,0:T(8,128)}) custom-call(s32[4]{0:T(128)} %counts_ref.17, bf16[4,2,14,14,1024]{4,3,2,1,0:T(8,128)(2,1)} %copy.34.x_ref, bf16[1024,256]{1,0:T(8,128)(2,1)} %down_ref.3), custom_call_target="tpu_custom_call" | custom-call | bytes 7405584 | tf_op jit(solution)/shard_map/first/pallas_call | solution.py:580
  18.3 4.4 %collective-permute-start.1 = (bf16[4,224,256]{2,1,0:T(8,128)(2,1)}, bf16[4,224,256]{2,1,0:T(8,128)(2,1)S(1)}, u32[]{:S(2)}, u32[]{:S(2)}) collective-permute-start(bf16[4,224,256]{2,1,0:T(8,128)(2,1)} %get-tuple-element.59.oc_ref), channel_id=1, source_target_pairs={{0,1},{1,0},{2,3},{3,2},{4,5},{5,4},{6,7},{7,6},{8,9},{9,8},{10,11... | collective-permute-start | bytes 1376264 | tf_op jit(solution)/shard_map/ppermute | solution.py:607
  25.2 10.4 %mid.1 = (f32[4,2,224,256]{3,2,1,0:T(8,128)}, bf16[4,2,224,256]{3,2,1,0:T(8,128)(2,1)}, f32[4,56,1024]{2,1,0:T(8,128)}, f32[2,1024]{1,0:T(2,128)}) custom-call(s32[4]{0:T(128)} %counts_ref.17, bf16[4,224,256]{2,1,0:T(8,128)(2,1)} %copy-done.3, bf16[4,224,256]{2,1,0:T(8,128)(2,1)} %get-tuple-element.58.oz_ref, bf16[4,224,256]{2,1,0:T(8,128)(2,1)} %get-tuple-element.59.oc_ref, ...), custom_call_target="tpu_custom_call" | custom-call | bytes 6065168 | tf_op jit(solution)/shard_map/mid/pallas_call | solution.py:580
  35.5 5.5 %collective-permute-start.2 = (f32[2,1024]{1,0:T(2,128)}, f32[2,1024]{1,0:T(2,128)S(1)}, u32[]{:S(2)}, u32[]{:S(2)}) collective-permute-start(f32[2,1024]{1,0:T(2,128)} %get-tuple-element.60), channel_id=1, source_target_pairs={{0,1},{1,0},{2,3},{3,2},{4,5},{5,4},{6,7},{7,6},{8,9},{9,8},{10,11... | collective-permute-start | bytes 24584 | tf_op jit(solution)/shard_map/ppermute | solution.py:598
  60.1 4.8 %late_mid.1 = (f32[4,56,512]{2,1,0:T(8,128)}, bf16[224,512]{1,0:T(8,128)(2,1)}, bf16[224,2048]{1,0:T(8,128)(2,1)}, f32[2,2048]{1,0:T(2,128)}) custom-call(s32[4]{0:T(128)} %counts_ref.17, bf16[4,56,512]{2,1,0:T(8,128)(2,1)} %copy-done.5, bf16[4,56,512]{2,1,0:T(8,128)(2,1)} %get-tuple-element.63.own_ref, bf16[4,56,512]{2,1,0:T(8,128)(2,1)} %copy-done.6, ...), custom_call_target="tpu_custom_call" | custom-call | bytes 4462608 | tf_op jit(solution)/shard_map/late_mid/pallas_call | solution.py:580
  64.8 4.2 %collective-permute-start.8 = (f32[2,2048]{1,0:T(2,128)}, f32[2,2048]{1,0:T(2,128)S(1)}, u32[]{:S(2)}, u32[]{:S(2)}) collective-permute-start(f32[2,2048]{1,0:T(2,128)} %get-tuple-element.64), channel_id=1, source_target_pairs={{0,1},{1,0},{2,3},{3,2},{4,5},{5,4},{6,7},{7,6},{8,9},{9,8},{10,11... | collective-permute-start | bytes 49160 | tf_op jit(solution)/shard_map/ppermute | solution.py:598
  75.5 4.2 %convolution_convert_fusion = bf16[224,2048]{1,0:T(8,128)(2,1)} fusion(bf16[224,1024]{1,0:T(8,128)(2,1)S(1)} %copy-done.1, bf16[1024,2048]{1,0:T(8,128)(2,1)} %param.24), kind=kOutput, calls=%fused_computation | convolution fusion | flops 939982848 | bytes 5570560 | tf_op jit(solution)/shard_map/dot_general | solution.py:52
  80.3 5.0 %post.1 = (f32[2,2048]{1,0:T(2,128)}, f32[2,2048]{1,0:T(2,128)}, f32[4,2048]{1,0:T(4,128)}, f32[4,56,2048]{2,1,0:T(8,128)}, bf16[4,56,2048]{2,1,0:T(8,128)(2,1)}) custom-call(s32[4]{0:T(128)} %counts_ref.17, f32[1,2,2048]{2,1,0:T(2,128)} %bitcast.72, f32[1,2,2048]{2,1,0:T(2,128)} %bitcast.83, f32[1,2,2048]{2,1,0:T(2,128)} %bitcast.81, ...), custom_call_target="tpu_custom_call" | custom-call | bytes 4767760 | tf_op jit(solution)/shard_map/post/pallas_call | solution.py:580
  90.5 5.4 %skip_product.1 = bf16[16,32,2048]{2,1,0:T(8,128)(2,1)} custom-call(bf16[224,1024]{1,0:T(8,128)(2,1)} %get-tuple-element.66.left_ref.entry_ref, bf16[224,1024]{1,0:T(8,128)(2,1)} %copy-done.2, bf16[224,2048]{1,0:T(8,128)(2,1)} %bitcast.60, bf16[224,2048]{1,0:T(8,128)(2,1)} %copy-done.9), custom_call_target="tpu_custom_call" | custom-call | flops 939524096 | bytes 4849664 | tf_op jit(solution)/shard_map/skip_product/pallas_call | solution.py:654
  100.4 5.0 %collective-permute-done.14 = f32[6,2048]{1,0:T(8,128)S(1)} collective-permute-done((f32[6,2048]{1,0:T(8,128)S(1)}, f32[6,2048]{1,0:T(8,128)S(1)}, u32[]{:S(2)}, u32[]{:S(2)}) %collective-permute-start.14) | collective-permute-done | bytes 49184 | tf_op jit(solution)/shard_map/ppermute | solution.py:599
  106.0 4.7 %sum_grad.1 = (bf16[224,2048]{1,0:T(8,128)(2,1)}, bf16[4,56,512]{2,1,0:T(8,128)(2,1)}) custom-call(s32[4]{0:T(128)} %counts_ref.17, f32[1,6,2048]{2,1,0:T(8,128)} %bitcast.63, f32[1,6,2048]{2,1,0:T(8,128)} %bitcast.66, f32[1,6,2048]{2,1,0:T(8,128)} %bitcast.68, f32[1,6,2048]{2,1,0:T(8,128)} %bitcast.70, f32[2,2048]{1,0:T(2,128)} %get-tuple-element.72.refs_4_, ...), custom_call_target="tpu_custom_call" | custom-call | bytes 6676496 | tf_op jit(solution)/shard_map/sum_grad/pallas_call | solution.py:580
  114.8 4.6 %fusion.8.skip_back_ref = f32[224,1024]{1,0:T(8,128)} fusion(bf16[224,2048]{1,0:T(8,128)(2,1)S(1)} %bitcast.61, bf16[1024,2048]{1,0:T(8,128)(2,1)} %param.24), kind=kOutput, calls=%fused_computation.25 | convolution fusion | flops 939524096 | bytes 6029312 | tf_op jit(solution)/shard_map/dot_general | solution.py:56
  119.4 4.9 %late_back.1 = (bf16[224,512]{1,0:T(8,128)(2,1)}, f32[4,56,1024]{2,1,0:T(8,128)}, f32[2,1024]{1,0:T(2,128)}) custom-call(s32[4]{0:T(128)} %counts_ref.17, bf16[4,56,512]{2,1,0:T(8,128)(2,1)} %collective-permute-done.18.rz_ref, bf16[4,56,512]{2,1,0:T(8,128)(2,1)} %get-tuple-element.79.own_ref.grad_ref, bf16[4,56,512]{2,1,0:T(8,128)(2,1)} %collective-permute-done.19.rc_ref, ...), custom_call_target="tpu_custom_call" | custom-call | bytes 5240848 | tf_op jit(solution)/shard_map/late_back/pallas_call | solution.py:580
  128.5 4.5 %two_products.1 = bf16[16,24,2048]{2,1,0:T(8,128)(2,1)} custom-call(bf16[224,512]{1,0:T(8,128)(2,1)} %get-tuple-element.82.act_ref, bf16[224,512]{1,0:T(8,128)(2,1)} %copy-done.17, bf16[224,2048]{1,0:T(8,128)(2,1)} %get-tuple-element.84.sum_ref, bf16[224,2048]{1,0:T(8,128)(2,1)} %copy-done.8, bf16[224,1024]{1,0:T(8,128)(2,1)} %get-tuple-element.66.left_ref.entry_ref, ...), custom_call_target="tpu_custom_call" | custom-call | bytes 5242880 | tf_op jit(solution)/shard_map/two_products/pallas_call | solution.py:580
  138.5 3.9 %all-to-all-start.2 = ((f32[32,24,128]{2,1,0:T(8,128)}), f32[32,24,128]{2,1,0:T(8,128)S(1)}, u32[]{:S(2)}, u32[]{:S(2)}) async-start(f32[32,24,128]{2,1,0:T(8,128)} %get-tuple-element.98), calls=%async_computation.2 | async-start | bytes 786432 | tf_op jit(solution)/shard_map/all_to_all | solution.py:935
  149.8 5.4 %collective-permute-done.22 = f32[2,1024]{1,0:T(2,128)S(1)} collective-permute-done((f32[2,1024]{1,0:T(2,128)S(1)}, f32[2,1024]{1,0:T(2,128)S(1)}, u32[]{:S(2)}, u32[]{:S(2)}) %collective-permute-start.22) | collective-permute-done | bytes 8224 | tf_op jit(solution)/shard_map/ppermute | solution.py:599
  155.8 6.7 %third_grad.1 = (bf16[4,2,224,1024]{3,2,1,0:T(8,128)(2,1)}, bf16[4,224,256]{2,1,0:T(8,128)(2,1)}, bf16[4,224,256]{2,1,0:T(8,128)(2,1)}) custom-call(s32[4]{0:T(128)} %counts_ref.17, f32[1,2,1024]{2,1,0:T(2,128)} %bitcast.77, f32[1,2,1024]{2,1,0:T(2,128)} %bitcast.88, f32[1,2,1024]{2,1,0:T(2,128)} %bitcast.90, f32[1,2,1024]{2,1,0:T(2,128)} %bitcast.92, ...), custom_call_target="tpu_custom_call" | custom-call | bytes 8826896 | tf_op jit(solution)/shard_map/third_grad/pallas_call | solution.py:580
  165.2 9.4 %third_sums.1 = bf16[256,1152]{1,0:T(8,128)(2,1)} custom-call(bf16[4,224,256]{2,1,0:T(8,128)(2,1)} %copy-done.3, bf16[4,224,256]{2,1,0:T(8,128)(2,1)} %get-tuple-element.58.oz_ref, bf16[4,224,256]{2,1,0:T(8,128)(2,1)} %get-tuple-element.59.oc_ref, bf16[4,224,256]{2,1,0:T(8,128)(2,1)} %copy-done.4, bf16[4,224,256]{2,1,0:T(8,128)(2,1)} %get-tuple-element.90.gz_ref, ...), custom_call_target="tpu_custom_call" | custom-call | bytes 7929856 | tf_op jit(solution)/shard_map/third_sums/pallas_call | solution.py:580
  180.0 10.4 %first_grad.1 = (bf16[4,448,256]{2,1,0:T(8,128)(2,1)}, bf16[1024,256]{1,0:T(8,128)(2,1)}) custom-call(s32[4]{0:T(128)} %counts_ref.17, bf16[4,224,256]{2,1,0:T(8,128)(2,1)} %copy-done.11, bf16[4,224,256]{2,1,0:T(8,128)(2,1)} %get-tuple-element.90.gz_ref, bf16[4,224,256]{2,1,0:T(8,128)(2,1)} %get-tuple-element.91.gc_ref, bf16[4,224,256]{2,1,0:T(8,128)(2,1)} %copy-done.12, ...), custom_call_target="tpu_custom_call" | custom-call | bytes 8350736 | tf_op jit(solution)/shard_map/first_grad/pallas_call | solution.py:580
  194.6 5.6 %clip_grad.1 = bf16[4,2,14,14,1024]{4,3,2,1,0:T(8,128)(2,1)} custom-call(bf16[4,448,256]{2,1,0:T(8,128)(2,1)} %get-tuple-element.95.grad_ref, bf16[1024,256]{1,0:T(8,128)(2,1)} %down_ref.3, f32[4,56,1024]{2,1,0:T(8,128)} %get-tuple-element.89.refs_7_.entry_grad_ref), custom_call_target="tpu_custom_call" | custom-call | bytes 5570560 | tf_op jit(solution)/shard_map/clip_grad/pallas_call | solution.py:580
  200.8 7.1 %copy.36 = bf16[4,2,14,14,1024]{4,1,3,2,0:T(2,128)(2,1)} copy(bf16[4,2,14,14,1024]{4,3,2,1,0:T(8,128)(2,1)} %clip_grad.1) | data formatting | bytes 6422528
  207.9 5.8 %all-to-all-start = ((bf16[32,32,256]{2,1,0:T(8,128)(2,1)}), bf16[32,32,256]{2,1,0:T(8,128)(2,1)S(1)}, u32[]{:S(2)}, u32[]{:S(2)}) async-start(bf16[32,32,256]{2,1,0:T(8,128)(2,1)} %bitcast.26), calls=%async_computation | async-start | bytes 1048576 | tf_op jit(solution)/shard_map/all_to_all | solution.py:621
  217.2 13.6 %all-to-all-done = bf16[32,32,256]{2,1,0:T(8,128)(2,1)S(1)} async-done(((bf16[32,32,256]{2,1,0:T(8,128)(2,1)}), bf16[32,32,256]{2,1,0:T(8,128)(2,1)S(1)}, u32[]{:S(2)}, u32[]{:S(2)}) %all-to-all-start) | async-done | bytes 524320 | tf_op jit(solution)/shard_map/all_to_all | solution.py:621
  (172 shorter events, 81.8 us)
Async XLA Ops:
  7.2 183.3 %reduce-scatter.4.cloned.1.call-start = ((), (), s32[]{:S(2)}) async-start(), calls=%async_computation.6 | async-start | bytes 2621440 | tf_op jit(solution)/shard_map/reduce_scatter | solution.py:695
  17.5 5.9 %collective-permute-start = (bf16[4,224,256]{2,1,0:T(8,128)(2,1)}, bf16[4,224,256]{2,1,0:T(8,128)(2,1)S(1)}, u32[]{:S(2)}, u32[]{:S(2)}) collective-permute-start(bf16[4,224,256]{2,1,0:T(8,128)(2,1)} %get-tuple-element.58.oz_ref), channel_id=1, source_target_pairs={{1,2},{2,1},{3,4},{4,3},{5,6},{6,5},{9,10},{10,9},{11,12},{12,11},... | collective-permute-start | bytes 1376264 | tf_op jit(solution)/shard_map/ppermute | solution.py:607
  18.3 6.1 %collective-permute-start.1 = (bf16[4,224,256]{2,1,0:T(8,128)(2,1)}, bf16[4,224,256]{2,1,0:T(8,128)(2,1)S(1)}, u32[]{:S(2)}, u32[]{:S(2)}) collective-permute-start(bf16[4,224,256]{2,1,0:T(8,128)(2,1)} %get-tuple-element.59.oc_ref), channel_id=1, source_target_pairs={{0,1},{1,0},{2,3},{3,2},{4,5},{5,4},{6,7},{7,6},{8,9},{9,8},{10,11... | collective-permute-start | bytes 1376264 | tf_op jit(solution)/shard_map/ppermute | solution.py:607
  35.5 6.6 %collective-permute-start.2 = (f32[2,1024]{1,0:T(2,128)}, f32[2,1024]{1,0:T(2,128)S(1)}, u32[]{:S(2)}, u32[]{:S(2)}) collective-permute-start(f32[2,1024]{1,0:T(2,128)} %get-tuple-element.60), channel_id=1, source_target_pairs={{0,1},{1,0},{2,3},{3,2},{4,5},{5,4},{6,7},{7,6},{8,9},{9,8},{10,11... | collective-permute-start | bytes 24584 | tf_op jit(solution)/shard_map/ppermute | solution.py:598
  47.3 5.4 %collective-permute-start.5 = (f32[2,1024]{1,0:T(2,128)S(1)}, f32[2,1024]{1,0:T(2,128)S(1)}, u32[]{:S(2)}, u32[]{:S(2)}) collective-permute-start(f32[2,1024]{1,0:T(2,128)S(1)} %add.47), channel_id=1, source_target_pairs={{0,6},{1,7},{2,4},{3,5},{4,2},{5,3},{6,0},{7,1},{8,14},{9,15},{10,... | collective-permute-start | bytes 24584 | tf_op jit(solution)/shard_map/ppermute | solution.py:599
  64.8 6.3 %collective-permute-start.8 = (f32[2,2048]{1,0:T(2,128)}, f32[2,2048]{1,0:T(2,128)S(1)}, u32[]{:S(2)}, u32[]{:S(2)}) collective-permute-start(f32[2,2048]{1,0:T(2,128)} %get-tuple-element.64), channel_id=1, source_target_pairs={{0,1},{1,0},{2,3},{3,2},{4,5},{5,4},{6,7},{7,6},{8,9},{9,8},{10,11... | collective-permute-start | bytes 49160 | tf_op jit(solution)/shard_map/ppermute | solution.py:598
  71.9 7.8 %collective-permute-start.10 = (f32[2,2048]{1,0:T(2,128)S(1)}, f32[2,2048]{1,0:T(2,128)S(1)}, u32[]{:S(2)}, u32[]{:S(2)}) collective-permute-start(f32[2,2048]{1,0:T(2,128)S(1)} %add.48), channel_id=1, source_target_pairs={{0,4},{1,5},{2,6},{3,7},{4,0},{5,1},{6,2},{7,3},{8,12},{9,13},{10,... | collective-permute-start | bytes 49160 | tf_op jit(solution)/shard_map/ppermute | solution.py:599
  72.8 6.9 %collective-permute-start.11 = (f32[2,2048]{1,0:T(2,128)S(1)}, f32[2,2048]{1,0:T(2,128)S(1)}, u32[]{:S(2)}, u32[]{:S(2)}) collective-permute-start(f32[2,2048]{1,0:T(2,128)S(1)} %add.48), channel_id=1, source_target_pairs={{0,6},{1,7},{2,4},{3,5},{4,2},{5,3},{6,0},{7,1},{8,14},{9,15},{10,... | collective-permute-start | bytes 49160 | tf_op jit(solution)/shard_map/ppermute | solution.py:599
  95.9 94.7 %reduce-scatter.6.cloned.1.call-start = ((), (), s32[]{:S(2)}) async-start(), calls=%async_computation.7 | async-start | bytes 1966080 | tf_op jit(solution)/shard_map/reduce_scatter | solution.py:695
  97.1 8.3 %collective-permute-start.14 = (f32[6,2048]{1,0:T(8,128)S(1)}, f32[6,2048]{1,0:T(8,128)S(1)}, u32[]{:S(2)}, u32[]{:S(2)}) collective-permute-start(f32[6,2048]{1,0:T(8,128)S(1)} %fusion.6), channel_id=1, source_target_pairs={{0,4},{1,5},{2,6},{3,7},{4,0},{5,1},{6,2},{7,3},{8,12},{9,13},{10,... | collective-permute-start | bytes 147464 | tf_op jit(solution)/shard_map/ppermute | solution.py:599
  98.2 7.2 %collective-permute-start.15 = (f32[6,2048]{1,0:T(8,128)S(1)}, f32[6,2048]{1,0:T(8,128)S(1)}, u32[]{:S(2)}, u32[]{:S(2)}) collective-permute-start(f32[6,2048]{1,0:T(8,128)S(1)} %fusion.6), channel_id=1, source_target_pairs={{0,6},{1,7},{2,4},{3,5},{4,2},{5,3},{6,0},{7,1},{8,14},{9,15},{10,... | collective-permute-start | bytes 147464 | tf_op jit(solution)/shard_map/ppermute | solution.py:599
  110.8 16.0 %collective-permute-start.25 = (bf16[224,2048]{1,0:T(8,128)(2,1)}, bf16[224,2048]{1,0:T(8,128)(2,1)S(1)}, u32[]{:S(2)}, u32[]{:S(2)}) collective-permute-start(bf16[224,2048]{1,0:T(8,128)(2,1)} %get-tuple-element.84.sum_ref), channel_id=1, source_target_pairs={{0,1},{1,0},{2,3},{3,2},{4,5},{5,4},{6,7},{7,6},{8,9},{9,8},{10,11... | collective-permute-start | bytes 2752520 | tf_op jit(solution)/shard_map/ppermute | solution.py:625
  110.8 16.0 %collective-permute-start.24 = (bf16[224,512]{1,0:T(8,128)(2,1)S(1)}, bf16[224,512]{1,0:T(8,128)(2,1)S(1)}, u32[]{:S(2)}, u32[]{:S(2)}) collective-permute-start(bf16[224,512]{1,0:T(8,128)(2,1)S(1)} %copy-done.16), channel_id=1, source_target_pairs={{0,1},{1,0},{2,3},{3,2},{4,5},{5,4},{6,7},{7,6},{8,9},{9,8},{10,11... | collective-permute-start | bytes 688136 | tf_op jit(solution)/shard_map/ppermute | solution.py:625
  111.3 8.1 %collective-permute-start.18 = (bf16[4,56,512]{2,1,0:T(8,128)(2,1)}, bf16[4,56,512]{2,1,0:T(8,128)(2,1)}, u32[]{:S(2)}, u32[]{:S(2)}) collective-permute-start(bf16[4,56,512]{2,1,0:T(8,128)(2,1)} %get-tuple-element.79.own_ref.grad_ref), channel_id=1, source_target_pairs={{1,2},{2,1},{3,4},{4,3},{5,6},{6,5},{9,10},{10,9},{11,12},{12,11},... | collective-permute-start | bytes 688136 | tf_op jit(solution)/shard_map/ppermute | solution.py:607
  112.6 6.8 %collective-permute-start.19 = (bf16[4,56,512]{2,1,0:T(8,128)(2,1)}, bf16[4,56,512]{2,1,0:T(8,128)(2,1)}, u32[]{:S(2)}, u32[]{:S(2)}) collective-permute-start(bf16[4,56,512]{2,1,0:T(8,128)(2,1)} %get-tuple-element.79.own_ref.grad_ref), channel_id=1, source_target_pairs={{0,1},{1,0},{2,3},{3,2},{4,5},{5,4},{6,7},{7,6},{8,9},{9,8},{10,11... | collective-permute-start | bytes 688136 | tf_op jit(solution)/shard_map/ppermute | solution.py:607
  138.5 36.1 %all-to-all-start.2 = ((f32[32,24,128]{2,1,0:T(8,128)}), f32[32,24,128]{2,1,0:T(8,128)S(1)}, u32[]{:S(2)}, u32[]{:S(2)}) async-start(f32[32,24,128]{2,1,0:T(8,128)} %get-tuple-element.98), calls=%async_computation.2 | async-start | bytes 786432 | tf_op jit(solution)/shard_map/all_to_all | solution.py:935
  142.4 7.4 %collective-permute-start.21 = (f32[2,1024]{1,0:T(2,128)S(1)}, f32[2,1024]{1,0:T(2,128)S(1)}, u32[]{:S(2)}, u32[]{:S(2)}) collective-permute-start(f32[2,1024]{1,0:T(2,128)S(1)} %add.51), channel_id=1, source_target_pairs={{0,2},{1,3},{2,0},{3,1},{4,6},{5,7},{6,4},{7,5},{8,10},{9,11},{10,... | collective-permute-start | bytes 24584 | tf_op jit(solution)/shard_map/ppermute | solution.py:599
  144.2 11.0 %collective-permute-start.22 = (f32[2,1024]{1,0:T(2,128)S(1)}, f32[2,1024]{1,0:T(2,128)S(1)}, u32[]{:S(2)}, u32[]{:S(2)}) collective-permute-start(f32[2,1024]{1,0:T(2,128)S(1)} %add.51), channel_id=1, source_target_pairs={{0,4},{1,5},{2,6},{3,7},{4,0},{5,1},{6,2},{7,3},{8,12},{9,13},{10,... | collective-permute-start | bytes 24584 | tf_op jit(solution)/shard_map/ppermute | solution.py:599
  146.6 8.6 %collective-permute-start.23 = (f32[2,1024]{1,0:T(2,128)S(1)}, f32[2,1024]{1,0:T(2,128)S(1)}, u32[]{:S(2)}, u32[]{:S(2)}) collective-permute-start(f32[2,1024]{1,0:T(2,128)S(1)} %add.51), channel_id=1, source_target_pairs={{0,6},{1,7},{2,4},{3,5},{4,2},{5,3},{6,0},{7,1},{8,14},{9,15},{10,... | collective-permute-start | bytes 24584 | tf_op jit(solution)/shard_map/ppermute | solution.py:599
  162.5 15.9 %collective-permute-start.27 = (bf16[4,224,256]{2,1,0:T(8,128)(2,1)}, bf16[4,224,256]{2,1,0:T(8,128)(2,1)S(1)}, u32[]{:S(2)}, u32[]{:S(2)}) collective-permute-start(bf16[4,224,256]{2,1,0:T(8,128)(2,1)} %get-tuple-element.90.gz_ref), channel_id=1, source_target_pairs={{1,2},{2,1},{3,4},{4,3},{5,6},{6,5},{9,10},{10,9},{11,12},{12,11},... | collective-permute-start | bytes 1376264 | tf_op jit(solution)/shard_map/ppermute | solution.py:607
  163.2 15.3 %collective-permute-start.28 = (bf16[4,224,256]{2,1,0:T(8,128)(2,1)}, bf16[4,224,256]{2,1,0:T(8,128)(2,1)S(1)}, u32[]{:S(2)}, u32[]{:S(2)}) collective-permute-start(bf16[4,224,256]{2,1,0:T(8,128)(2,1)} %get-tuple-element.91.gc_ref), channel_id=1, source_target_pairs={{0,1},{1,0},{2,3},{3,2},{4,5},{5,4},{6,7},{7,6},{8,9},{9,8},{10,11... | collective-permute-start | bytes 1376264 | tf_op jit(solution)/shard_map/ppermute | solution.py:607
  174.6 33.2 %all-to-all-start.1 = ((bf16[32,8,1152]{2,1,0:T(8,128)(2,1)}), bf16[32,8,1152]{2,1,0:T(8,128)(2,1)S(1)}, u32[]{:S(2)}, u32[]{:S(2)}) async-start(bf16[32,8,1152]{2,1,0:T(8,128)(2,1)} %bitcast.57), calls=%async_computation.1 | async-start | bytes 1179648 | tf_op jit(solution)/shard_map/all_to_all | solution.py:621
  178.2 53.4 %reduce-scatter.8.cloned.1.call-start = ((), (), s32[]{:S(2)}) async-start(), calls=%async_computation.8 | async-start | bytes 1146880 | tf_op jit(solution)/shard_map/reduce_scatter | solution.py:701
  207.9 23.0 %all-to-all-start = ((bf16[32,32,256]{2,1,0:T(8,128)(2,1)}), bf16[32,32,256]{2,1,0:T(8,128)(2,1)S(1)}, u32[]{:S(2)}, u32[]{:S(2)}) async-start(bf16[32,32,256]{2,1,0:T(8,128)(2,1)} %bitcast.26), calls=%async_computation | async-start | bytes 1048576 | tf_op jit(solution)/shard_map/all_to_all | solution.py:621
  (47 other events, 270.7 us)
Sparse Core Ops, SparseCore 0:
  96.0 34.4 reduce-scatter.3
  133.8 34.9 reduce-scatter.5
  192.9 26.3 reduce-scatter.7

commit v2 on v1

--- a/solution.py
+++ b/solution.py
@@ -12,6 +12,7 @@
 f32 = jnp.float32
 bf16 = jnp.bfloat16
 mib = 1 << 20
+LIMIT = 16
 
 
 def gelu_terms(x):
@@ -82,16 +83,23 @@
         ref[j, pl.ds(start, rows, stride=2), :] = values[:, 128 * j : 128 * (j + 1)]
 
 
-def conv_rows(taps, load, rows):
+def conv_rows(taps, load, rows, times=(0, 1, 2)):
     sums = [None, None, None]
-    for a in range(3):
+    for a in times:
         for b in range(3):
             block = load(a, b)
             for e in range(3):
-                i = 9 * a + 3 * b + e
-                term = block * taps(i)
+                term = block * taps(9 * a + 3 * b + e)
                 sums[e] = term if sums[e] is None else sums[e] + term
     return pltpu.roll(sums[0], 1, 0) + sums[1] + pltpu.roll(sums[2], rows - 1, 0)
+
+
+def split(values, count):
+    parts = []
+    for _ in range(count):
+        parts.append(values.astype(bf16))
+        values = values - parts[-1].astype(f32)
+    return parts
 
 
 def frame_of(slot):
@@ -116,6 +124,37 @@
         for i in range(ref.shape[0]):
             total = ref[i] if total is None else total + ref[i]
     return total
+
+
+def taps_kernel(third_ref, fourth_ref, third_out, fourth_out):
+    swapped = (lax.axis_index("space") & 1) == 1
+    for source, out in ((third_ref, third_out), (fourth_ref, fourth_out)):
+        for a in range(3):
+            here, there = source[pl.ds(9 * a, 9), :], source[pl.ds(9 * (2 - a), 9), :]
+            out[pl.ds(9 * a, 9), :] = jnp.where(swapped, there, here)
+
+
+def pooled_grad_kernel(grad_ref, head_ref, out_ref):
+    full = sum(dot(part, head_ref[...]) for part in split(grad_ref[...], 3))
+    clips = out_ref.shape[0]
+    clip = lax.axis_index("clip")
+    own = full[:clips]
+    for g in range(1, full.shape[0] // clips):
+        own = jnp.where(clip == g, full[g * clips : (g + 1) * clips], own)
+    out_ref[...] = own.astype(bf16).astype(f32)
+
+
+def head_kernel(pooled_ref, head_ref, bias_ref, grad_ref, logits_ref, bias_grad_ref):
+    logits_ref[...] = dot_t(pooled_ref[...], head_ref[...]) + bias_ref[...]
+    bias_grad_ref[...] = jnp.sum(grad_ref[...], axis=0, keepdims=True)
+
+
+def add_kernel(one_ref, two_ref, out_ref):
+    out_ref[...] = one_ref[...] + two_ref[...]
+
+
+def skipped_kernel(entry_ref, weight_ref, out_ref):
+    out_ref[...] = dot(entry_ref[...], weight_ref[...]).astype(bf16)
 
 
 def first_kernel(counts_ref, x_ref, w_ref, first_ref, actz_ref, actc_ref, even_ref, xpad, xe):
@@ -152,50 +191,85 @@
         frames[s, pl.ds(pad + rows, pad), :] = edge
 
 
-def mid_kernel(
-    width, counts_ref, rz_ref, oz_ref, oc_ref, rc_ref, taps_ref, up_ref,
-    mid_ref, act_ref, even_ref, moment_ref, frames, sums, total,
-):
-    k = pl.program_id(0)
+def mid_own_kernel(oz_ref, oc_ref, taps_ref, part_ref, frames):
     rows = oz_ref.shape[1]
     pitch = 16
     chunk = 2 * pitch
 
+    @pl.when(pl.program_id(0) == 0)
+    def _():
+        clear_edges(frames, pitch, rows)
+
+    fill_frames(frames, (oz_ref, oc_ref), pitch, rows)
+    for slot in range(2):
+        def step(c, _):
+            start = pl.multiple_of(c * chunk, chunk)
+            part_ref[0, slot, pl.ds(start, chunk), :] = conv_rows(
+                lambda i: taps_ref[pl.ds(i, 1), :],
+                lambda a, b: frames[slot + a - 1, pl.ds(pl.multiple_of(start + pitch * b, pitch), chunk), :],
+                chunk,
+                (1, 2) if slot == 0 else (0, 1),
+            )
+            return 0
+
+        lax.fori_loop(0, rows // chunk, step, 0)
+
+
+def mid_kernel(
+    width, counts_ref, rz_ref, rc_ref, part_ref, taps_ref, up_ref,
+    mid_ref, act_ref, act_even_ref, even_ref, moment_ref, gram_up_ref, act_sum_ref,
+    frames, acts, evens, gram, total,
+):
+    k = pl.program_id(0)
+    rows = rz_ref.shape[1]
+    pitch = 16
+    chunk = 2 * pitch
+    half = pitch // 2
+
     @pl.when(k == 0)
     def _():
         clear_edges(frames, pitch, rows)
+        gram[...] = jnp.zeros_like(gram)
         total[...] = jnp.zeros_like(total)
 
-    fill_frames(frames, (rz_ref, oz_ref, oc_ref, rc_ref), pitch, rows)
-
+    fill_frames(frames, (rz_ref, rc_ref), pitch, rows)
     for slot in range(2):
         def step(c, _):
             start = pl.multiple_of(c * chunk, chunk)
-            mid = conv_rows(
+            mid = part_ref[0, slot, pl.ds(start, chunk), :] + conv_rows(
                 lambda i: taps_ref[pl.ds(i, 1), :],
-                lambda a, b: frames[slot + a, pl.ds(pl.multiple_of(start + pitch * b, pitch), chunk), :],
+                lambda a, b: frames[slot, pl.ds(pl.multiple_of(start + pitch * b, pitch), chunk), :],
                 chunk,
+                (0,) if slot == 0 else (2,),
             )
             mid_ref[0, slot, pl.ds(start, chunk), :] = mid
             act = jnp.where(valid_rows(mid.shape, pitch, width), gelu(mid), 0.0)
             act_ref[0, slot, pl.ds(start, chunk), :] = act.astype(bf16)
+            put_lanes(acts, slot * rows + start, act)
             return 0
 
         lax.fori_loop(0, rows // chunk, step, 0)
-        third = dot(act_ref[0, slot], up_ref[...])
-        put_lanes(sums, slot * rows, third)
-        scale = frame_mask(counts_ref, k, frame_of(slot))
-        total[0] += row_sums(third) * scale
-        total[1] += row_sums(third * third) * scale
-    half = pitch // 2
+        act = act_ref[0, slot]
+        mask = frame_mask(counts_ref, k, frame_of(slot))
+        gram[...] += t_dot(act, act) * mask
+        total[...] += row_sums(act.astype(f32)) * mask
     for j in range(rows // chunk):
-        even_ref[0, pl.ds(half * j, half), :] = get_even(
-            sums, frame_of(0) * rows + chunk * j, half
-        )
+        at = pl.multiple_of(k * (rows // 4) + half * j, half)
+        evens[pl.ds(at, half), :] = get_even(acts, frame_of(0) * rows + chunk * j, half)
 
     @pl.when(k == pl.num_programs(0) - 1)
     def _():
-        moment_ref[...] = jnp.sum(total[...], axis=1)
+        act_even_ref[...] = evens[...].astype(bf16)
+        even_ref[...] = dot(act_even_ref[...], up_ref[...])
+        gram_up = sum(dot(part, up_ref[...]) for part in split(gram[...], 3))
+        gram_up_ref[...] = gram_up
+        act_sum = jnp.sum(total[...], axis=0, keepdims=True)
+        act_sum_ref[...] = act_sum
+        rows_of_sum = jnp.concatenate(
+            [part.astype(f32) for part in split(act_sum, 3)] + [jnp.zeros((5,) + act_sum.shape[1:], f32)], axis=0
+        ).astype(bf16)
+        moment_ref[0:1] = jnp.sum(dot(rows_of_sum, up_ref[...]), axis=0, keepdims=True)
+        moment_ref[1:2] = jnp.sum(gram_up * up_ref[...].astype(f32), axis=0, keepdims=True)
 
 
 def norm_stats(refs, cells):
@@ -205,11 +279,10 @@
 
 
 def entry_kernel(
-    width, cells, parts, counts_ref, *refs
+    width, cells, count, counts_ref, *refs
 ):
-    moments, refs = refs[:parts], refs[parts:]
-    (even_x_ref, even_ref, gain_ref, shift_ref, down_ref,
-     stats_ref, hat_ref, entry_ref, first_ref, act_ref) = refs
+    moments, refs = refs[:count], refs[count:]
+    (even_x_ref, even_ref, gain_ref, shift_ref, down_ref, stats_ref, hat_ref, entry_ref, first_ref, act_ref) = refs
     center, scale = norm_stats(moments, cell_total(counts_ref, False, cells))
     stats_ref[0:1] = center
     stats_ref[1:2] = scale
@@ -268,11 +341,10 @@
 
 
 def post_kernel(
-    width, cells, parts, counts_ref, *refs
+    width, cells, count, counts_ref, *refs
 ):
-    moments, refs = refs[:parts], refs[parts:]
-    (sum_ref, skip_ref, gain_ref, shift_ref, pooled_grad_ref,
-     stats_ref, back_ref, pooled_ref, pre_ref, skip_grad_ref) = refs
+    moments, refs = refs[:count], refs[count:]
+    (sum_ref, skip_ref, gain_ref, shift_ref, pooled_grad_ref, stats_ref, back_ref, pre_ref, skip_grad_ref) = refs
     center, scale = norm_stats(moments, cell_total(counts_ref, True, cells))
     stats_ref[0:1] = center
     stats_ref[1:2] = scale
@@ -284,7 +356,8 @@
         keep = valid_rows(post.shape, 8, width)
         mask = frame_mask(counts_ref, k, 0)
         pool = ((counts_ref[k] + 1) // 2 * cells).astype(f32)
-        pooled_ref[pl.ds(k, 1)] = jnp.sum(jnp.where(keep, post, 0.0), axis=0, keepdims=True) * mask / pool
+        pooled = jnp.sum(jnp.where(keep, post, 0.0), axis=0, keepdims=True) * mask / pool
+        back_ref[pl.ds(2 + k, 1)] = pooled
         pre = jnp.where(keep, pooled_grad_ref[pl.ds(k, 1)] * mask / pool * slope, 0.0)
         pre_ref[k] = pre
         skip_grad_ref[k] = pre.astype(bf16)
@@ -295,11 +368,13 @@
 
 
 def sum_grad_kernel(
-    width, cells, parts, counts_ref, *refs
+    width, cells, count, counts_ref, *refs
 ):
-    received, refs = refs[:parts], refs[parts:]
-    (stats_ref, sum_ref, pre_ref, gain_ref, up_ref, mid_ref, sum_grad_ref, mid_grad_ref) = refs
-    totals = received_sum(received)[0:2] / cell_total(counts_ref, True, cells)
+    received, refs = refs[:count], refs[count:]
+    (stats_ref, sum_ref, pre_ref, gain_ref, up_ref, mid_ref, sum_grad_ref, mid_grad_ref, pooled_ref) = refs
+    totals = received_sum(received)
+    pooled_ref[...] = totals[2:].astype(bf16)
+    totals = totals[0:2] / cell_total(counts_ref, True, cells)
     center, scale = stats_ref[0:1], stats_ref[1:2]
     lead = gain_ref[...] * scale
     clips, rows, channels = sum_ref.shape
@@ -401,9 +476,11 @@
         out_ref[cols, :] = tap_table(rows_of_tap)
 
 
-def third_sums_kernel(
-    rz_ref, oz_ref, oc_ref, rc_ref, gz_ref, gc_ref, act_ref, sum_grad_ref, out_ref, frames, grads, total, product
+def third_taps_kernel(
+    orders, parts, rz_ref, oz_ref, oc_ref, rc_ref, gz_ref, gc_ref, up_terms_ref, back_ref, third_ref, pooled_ref,
+    taps_ref, *refs,
 ):
+    outs, (frames, grads, total, full) = refs[:-4], refs[-4:]
     k = pl.program_id(0)
     rows, channels = oz_ref.shape[1], oz_ref.shape[2]
     pitch = 16
@@ -414,10 +491,7 @@
     def _():
         clear_edges(frames, pitch, rows)
         total[...] = jnp.zeros_like(total)
-        product[...] = jnp.zeros_like(product)
-
-    for slot in range(2):
-        product[...] += t_dot(act_ref[0, slot], sum_grad_ref[0, slot])
+
     fill_frames(frames, (rz_ref, oz_ref, oc_ref, rc_ref), pitch, rows)
     grads[0] = gz_ref[0].astype(f32)
     grads[1] = gc_ref[0].astype(f32)
@@ -440,67 +514,96 @@
 
     @pl.when(k == pl.num_programs(0) - 1)
     def _():
-        wide = product.shape[1]
-        out_ref[:, pl.ds(0, wide)] = product[...].astype(bf16)
-        out_ref[:, pl.ds(wide, lanes)] = tap_table(
-            [jnp.sum(total[i], axis=0, keepdims=True) for i in range(27)]
-        ).astype(bf16)
-
-
-def pack_kernel(parts, count, back_ref, third_ref, taps_ref, *refs):
-    received, (pooled_ref, out_ref) = refs[:count], refs[count:]
-    clips, late_wide = pooled_ref.shape
-    pooled_ref[...] = received_sum(received)[2:].astype(bf16)
-    pooled = pooled_ref[...].astype(f32)
-    wide = third_ref.shape[1]
-    own, own_third, own_taps = late_wide // parts, wide // parts, taps_ref.shape[0] // parts
-    for d in range(parts):
-        at = pl.ds(d * own // 128 * 128, 128)
-        third_at = pl.ds(d * own_third // 128 * 128, 128)
-        out_ref[d, 0:2] = back_ref[:, at]
-        out_ref[d, 2:4] = third_ref[:, third_at]
-        out_ref[d, 4 : 4 + clips] = pooled[:, d * own // 128 * 128 : d * own // 128 * 128 + 128]
-        out_ref[d, pl.ds(4 + clips, own_taps)] = taps_ref[pl.ds(d * own_taps, own_taps), :]
+        wide = up_terms_ref.shape[1]
+        late_wide = back_ref.shape[1]
+        full[:, pl.ds(0, wide)] = up_terms_ref[...].astype(f32)
+        full[:, pl.ds(wide, lanes)] = tap_table([jnp.sum(total[i], axis=0, keepdims=True) for i in range(27)])
+        own, own_third, own_taps = late_wide // parts, wide // parts, taps_ref.shape[0] // parts
+        deep = channels // parts
+        clip, space = lax.axis_index("clip"), lax.axis_index("space")
+        clips = pooled_ref.shape[0]
+        pooled = pooled_ref[...].astype(f32)
+        pooled = jnp.concatenate(
+            [jnp.where((clip == g) & (space == 0), pooled, 0.0) for g in range(lax.axis_size("clip"))], axis=0
+        )
+        for d in range(parts):
+            at, third_at = d * own // lanes * lanes, d * own_third // lanes * lanes
+            block = jnp.concatenate(
+                [
+                    back_ref[0:2, pl.ds(at, lanes)],
+                    third_ref[:, pl.ds(third_at, lanes)],
+                    jnp.zeros((4, lanes), f32),
+                    pooled[:, at : at + lanes],
+                    taps_ref[pl.ds(d * own_taps, own_taps), :],
+                ],
+                axis=0,
+            )
+            for i in range(block.shape[0] // deep):
+                full[pl.ds(d * deep, deep), pl.ds(wide + (1 + i) * lanes, lanes)] = block[i * deep : (i + 1) * deep]
+        if orders is None:
+            outs[0][...] = full[...].astype(bf16)
+        else:
+            clip_count, chips = orders
+            keep_ref, send_ref = outs
+            for b in range(clip_count):
+                for z in range(chips):
+                    at = ((clip ^ b) * chips + z) * 2
+                    mine = pl.multiple_of((at + (space & 1)) * deep, deep)
+                    other = pl.multiple_of((at + 1 - (space & 1)) * deep, deep)
+                    keep_ref[b, z] = full[pl.ds(mine, deep), :]
+                    send_ref[b, z] = full[pl.ds(other, deep), :].astype(bf16)
 
 
 def third_grad_kernel(
-    width, cells, parts, counts_ref, *refs
+    width, cells, count, counts_ref, *refs
 ):
-    received, refs = refs[:parts], refs[parts:]
-    (stats_ref, act_ref, mid_ref, entry_grad_ref, gain_ref, up_ref,
-     sum_grad_ref, gz_ref, gc_ref, placed) = refs
+    received, refs = refs[:count], refs[count:]
+    (stats_ref, gain_ref, entry_grad_ref, up_ref, act_even_ref, act_sum_ref, gram_up_ref, act_ref, mid_ref,
+     gz_ref, gc_ref, terms_ref, back_even, mix, shift, placed) = refs
     k = pl.program_id(0)
-    totals = received_sum(received) / cell_total(counts_ref, False, cells)
     rows = act_ref.shape[2]
     pitch = 16
     chunk = 2 * pitch
     half = pitch // 2
-    center, scale = stats_ref[0:1], stats_ref[1:2]
-    lead = gain_ref[...] * scale
 
     @pl.when(k == 0)
     def _():
         placed[...] = jnp.zeros_like(placed)
+        totals = received_sum(received) / cell_total(counts_ref, False, cells)
+        center, scale = stats_ref[0:1], stats_ref[1:2]
+        lead = gain_ref[...] * scale
+        slope = -(lead * scale * totals[1:2])
+        offset = -(lead * (totals[0:1] - center * scale * totals[1:2]))
+        grad = (entry_grad_ref[...] * lead).astype(bf16)
+        back_even[...] = dot_t(grad, up_ref[...])
+        product = sum(dot_t(part, up_ref[...]) for part in split(up_ref[...].astype(f32) * slope, 2))
+        mix[0], mix[1] = split(product, 2)
+        offsets = [part.astype(f32) for part in split(offset, 2)]
+        sums = [part.astype(f32) for part in split(act_sum_ref[...], 2)]
+        none = jnp.zeros((4, offset.shape[1]), f32)
+        offset_rows = jnp.concatenate(offsets + offsets + [none], axis=0).astype(bf16)
+        none = jnp.zeros((4, act_sum_ref.shape[1]), f32)
+        sum_rows = jnp.concatenate([sums[0], sums[0], sums[1], sums[1], none], axis=0).astype(bf16)
+        shift[...] = jnp.sum(dot_t(offset_rows, up_ref[...])[0:2], axis=0, keepdims=True)
+        terms = t_dot(act_even_ref[...], grad) + t_dot(sum_rows, offset_rows) + gram_up_ref[...] * slope
+        terms_ref[...] = terms.astype(bf16)
 
     for j in range(rows // chunk):
-        put_even(
-            placed, frame_of(0) * rows + chunk * j, lead * entry_grad_ref[0, pl.ds(half * j, half), :]
-        )
+        at = pl.multiple_of(k * (rows // 4) + half * j, half)
+        put_even(placed, frame_of(0) * rows + chunk * j, back_even[pl.ds(at, half), :])
     for slot, out in ((0, gz_ref), (1, gc_ref)):
-        weight = frame_mask(counts_ref, k, frame_of(slot))
-        slope_hat = -(lead * scale * totals[1:2]) * weight
-        offset = -(lead * (totals[0:1] - center * scale * totals[1:2])) * weight
-        third = dot(act_ref[0, slot], up_ref[...])
-        grad = get_lanes(placed, slot * rows, rows) + (offset + third * slope_hat)
-        sum_grad_ref[0, slot] = grad.astype(bf16)
-        back = dot_t(sum_grad_ref[0, slot], up_ref[...]) * gelu_slope(mid_ref[0, slot])
+        mask = frame_mask(counts_ref, k, frame_of(slot))
+        act = act_ref[0, slot]
+        back = (dot(act, mix[0]) + dot(act, mix[1]) + shift[...]) * mask + get_lanes(placed, slot * rows, rows)
+        back = back * gelu_slope(mid_ref[0, slot])
         out[0] = jnp.where(valid_rows(back.shape, pitch, width), back, 0.0).astype(bf16)
 
 
 def first_grad_kernel(
-    width, counts_ref, rz_ref, gz_ref, gc_ref, rc_ref, taps_ref, first_ref, x_ref,
-    grad_ref, down_grad_ref, frames, xpad, product,
+    width, orders, counts_ref, rz_ref, gz_ref, gc_ref, rc_ref, taps_ref, first_ref, x_ref,
+    grad_ref, *refs
 ):
+    outs, (frames, xpad, product) = refs[:-3], refs[-3:]
     k = pl.program_id(0)
     rows = gz_ref.shape[1]
     height, width = x_ref.shape[2], x_ref.shape[3]
@@ -533,11 +636,98 @@
             return 0
 
         lax.fori_loop(0, rows // chunk, step, 0)
-    product[...] += t_dot(xpad[...], grad_ref[0])
+    product[...] += t_dot(grad_ref[0], xpad[...])
 
     @pl.when(k == pl.num_programs(0) - 1)
     def _():
-        down_grad_ref[...] = product[...].astype(bf16)
+        terms = jnp.transpose(product[...])
+        if orders is None:
+            outs[0][...] = terms.astype(bf16)
+        else:
+            clips, chips, block = orders
+            xpad_rows = terms.reshape(clips * chips * 2, block, terms.shape[1])
+            space, clip = lax.axis_index("space"), lax.axis_index("clip")
+            keep_ref, send_ref, full = outs[0], outs[1], outs[2]
+            full[...] = xpad_rows
+            for b in range(clips):
+                for z in range(chips):
+                    at = ((clip ^ b) * chips + z) * 2
+                    keep_ref[b, z] = full[at + (space & 1)]
+                    send_ref[b, z] = full[at + 1 - (space & 1)].astype(bf16)
+
+
+def pair_sum_kernel(keep_ref, got_ref, keep_terms_ref, got_terms_ref, *out_refs):
+    wide, inner = keep_terms_ref.shape[-1], keep_ref.shape[-1]
+    deep = keep_terms_ref.shape[-2]
+    for b, out_ref in enumerate(out_refs):
+        out_ref[:, :, pl.ds(0, wide)] = (keep_terms_ref[b] + got_terms_ref[b].astype(f32)).astype(bf16)
+        total = keep_ref[b] + got_ref[b].astype(f32)
+        for i in range(keep_ref.shape[-2] // deep):
+            out_ref[:, :, pl.ds(wide + i * inner, inner)] = total[:, i * deep : (i + 1) * deep].astype(bf16)
+
+
+def chip_totals_kernel(count, *refs):
+    terms, outs = refs[:count], refs[count:]
+    for z, out_ref in enumerate(outs):
+        at = (lax.axis_index("space") // 2) ^ z
+        total = terms[0][at].astype(f32)
+        for term in terms[1:]:
+            total = total + term[at].astype(f32)
+        out_ref[...] = total.astype(bf16)
+
+
+def finish_kernel(count, *refs):
+    skip, up = refs[:count], refs[count : 2 * count]
+    skip_ref, up_ref, fourth_down_ref = refs[2 * count :]
+
+    def total(terms):
+        return sum(term[...].astype(f32) for term in terms)
+
+    skip_ref[...] = total(skip)
+    both = total(up)
+    block, lanes = up_ref.shape[0], fourth_down_ref.shape[1]
+    up_ref[...] = both[:block]
+    part = both.shape[0] - block
+    for i in range(both.shape[1] // lanes):
+        fourth_down_ref[pl.ds(i * part, part), :] = both[block:, i * lanes : (i + 1) * lanes]
+
+
+def terms_kernel(
+    count, clips, wide, small_rows, *refs
+):
+    received, refs = refs[:count], refs[count:]
+    (grad_ref, up_ref, depth_ref, gain_ref, shift_ref, late_gain_ref, late_shift_ref, late_depth_ref, head_ref,
+     *down_refs) = refs
+    lanes = 128
+    total = None
+    for ref in received:
+        for i in range(ref.shape[0]):
+            total = ref[i].astype(f32) if total is None else total + ref[i].astype(f32)
+    deep = total.shape[0]
+    up_ref[...] = total[:, :wide]
+    depth_ref[...] = total[:, wide : wide + 27]
+    device = lax.axis_index("clip") * lax.axis_size("space") + lax.axis_index("space")
+    end = wide + lanes * (1 + small_rows // deep)
+    small = jnp.concatenate([total[:, i : i + lanes] for i in range(wide + lanes, end, lanes)], axis=0)
+
+    def own_lanes(values, width):
+        moved = pltpu.roll(values, (lanes - device * width % lanes) % lanes, 1)
+        return moved[:, :width]
+
+    late = own_lanes(small, late_gain_ref.shape[1])
+    third = own_lanes(small, gain_ref.shape[1])
+    late_gain_ref[...] = late[1:2]
+    late_shift_ref[...] = late[0:1]
+    gain_ref[...] = third[3:4]
+    shift_ref[...] = third[2:3]
+    everyone = clips * lax.axis_size("clip")
+    late_depth_ref[...] = small[8 + everyone :, :27]
+    pooled = late[8 : 8 + everyone].astype(bf16)
+    head_ref[...] = sum(t_dot(pooled, part) for part in split(grad_ref[...], 3))
+    for down_ref in down_refs:
+        inner = down_ref.shape[1]
+        for i in range(down_ref.shape[0] // deep):
+            down_ref[pl.ds(i * deep, deep), :] = total[:, end + i * inner : end + (i + 1) * inner]
 
 
 def clip_grad_kernel(grad_ref, down_ref, entry_grad_ref, out_ref, wide):
@@ -556,6 +746,11 @@
             out_ref[0, frame, h] = get_lanes(wide, slot * rows + h * pitch, width).astype(bf16)
 
 
+kernel_micros = {
+    "first": 5.3, "mid_own": 5.0, "mid": 8.6, "entry": 3.4, "late_mid": 4.7, "post": 6.0, "skip_sums": 7.0,
+    "sum_grad": 4.6, "late_taps": 3.6, "late_back": 5.0, "up_down_sums": 5.5, "third_grad": 6.7, "third_taps": 7.7,
+    "up_down_total": 2.3, "skip_total": 3.0, "finish": 2.0, "terms": 1.5, "taps": 0.6, "pooled_grad": 1.5, "head": 1.0, "add": 0.6, "skipped": 2.5, "first_grad": 10.7, "pair_sum": 1.9, "clip_sum": 1.6, "clip_grad": 5.5,
+}
 smem = pl.BlockSpec(memory_space=pltpu.SMEM)
 
 
@@ -567,15 +762,17 @@
     return pl.BlockSpec((1,) + shape[1:], lambda k: (k,) + (0,) * (len(shape) - 1))
 
 
-def call(kernel, name, inputs, outputs, scratch, clips=None, limit=60, flops=0):
+def cost(micros):
+    return pl.CostEstimate(flops=0, bytes_accessed=int(micros * 3.4e6), transcendentals=0)
+
+
+def call(kernel, name, inputs, outputs, scratch, clips=None, limit=LIMIT):
     if clips is None:
         def spec(kind, shape):
             return smem if kind == "s" else pl.BlockSpec(memory_space=pltpu.VMEM)
     else:
         def spec(kind, shape):
             return smem if kind == "s" else whole(shape) if kind == "w" else by_clip(shape)
-    size = sum(math.prod(a.shape) * a.dtype.itemsize for a, _ in inputs)
-    size += sum(math.prod(s) * jnp.dtype(d).itemsize for s, d, _ in outputs)
     options = {} if clips is None else {"grid": (clips,)}
     return pl.pallas_call(
         kernel,
@@ -585,19 +782,22 @@
         out_specs=[spec(kind, s) for s, _, kind in outputs],
         scratch_shapes=scratch,
         compiler_params=pltpu.CompilerParams(vmem_limit_bytes=limit * mib),
-        cost_estimate=pl.CostEstimate(flops=flops, bytes_accessed=size, transcendentals=0),
+        cost_estimate=cost(kernel_micros[name]),
         **options,
     )(*[a for a, _ in inputs])
 
 
 def group_parts(values):
     size = lax.axis_size("space")
-    if size > 8:
+    if size != 8:
         copies = jnp.broadcast_to(values[None], (size,) + values.shape)
         return [lax.all_to_all(copies, "space", split_axis=0, concat_axis=0, tiled=True)]
-    pair = values + lax.ppermute(values, "space", [(i, i ^ 1) for i in range(size)])
-    others = [lax.ppermute(pair, "space", [(i, i ^ b) for i in range(size)]) for b in range(2, size, 2)]
-    return [part[None] for part in [pair] + others]
+    (pair,) = call(add_kernel, "add", [(values, "w"), (core_swap(values), "w")], [(values.shape, f32, "w")], [])
+    return [part[None] for part in over_chips([pair] * 4)]
+
+
+def w(arrays):
+    return [(array, "w") for array in arrays]
 
 
 def swap_neighbours(to_z, to_core):
@@ -625,80 +825,152 @@
     return lax.ppermute(values, "space", [(i, i ^ 1) for i in range(lax.axis_size("space"))])
 
 
-def own_rows(left_ref, block, out):
-    core = lax.axis_index("space") & 1
+def own_rows(left_ref, out, starts):
     out[0] = jnp.transpose(left_ref[...])
-    for j in range(out.shape[1] // block // 2):
-        start = pl.multiple_of((2 * j + core) * block, block)
-        out[1, pl.ds(j * block, block), :] = out[0, pl.ds(start, block), :]
-
-
-def skip_product_kernel(block, left_ref, left_other_ref, right_ref, right_other_ref, out_ref, left, left_other):
-    half = left.shape[1] // 2
+    block = out.shape[1] // 2 // len(starts)
+    for j, start in enumerate(starts):
+        out[1, pl.ds(j * block, block), :] = out[0, pl.ds(pl.multiple_of(start * block, block), block), :]
+
+
+def own_blocks(orders):
+    space, clip = lax.axis_index("space"), lax.axis_index("clip")
+    clips, chips = orders
+    return [((clip ^ b) * chips + z) * 2 + (space & 1) for b in range(clips) for z in range(chips)]
+
+
+def skip_kernel(
+    orders, left_ref, left_other_ref, right_ref, right_other_ref, weight_ref, back_ref, *refs
+):
+    clips, chips = orders
+    outs, (left, left_other) = refs[:clips], refs[clips:]
 
     @pl.when(pl.program_id(0) == 0)
     def _():
-        own_rows(left_ref, block, left)
-        own_rows(left_other_ref, block, left_other)
-
+        own_rows(left_ref, left, own_blocks(orders))
+        own_rows(left_other_ref, left_other, own_blocks(orders))
+        back_ref[...] = jnp.zeros_like(back_ref)
+
+    half = left.shape[1] // 2
     total = dot(left[1, pl.ds(0, half)], right_ref[...]) + dot(left_other[1, pl.ds(0, half)], right_other_ref[...])
-    for j in range(out_ref.shape[0]):
-        out_ref[j] = total[j * block : (j + 1) * block].astype(bf16)
-
-
-def skip_product(left, left_other, right, right_other, parts):
+    block = half // (clips * chips)
+    for j in range(clips * chips):
+        outs[j // chips][j % chips] = total[j * block : (j + 1) * block].astype(bf16)
+    back_ref[...] += dot_t(right_ref[...], weight_ref[...])
+
+
+def skip_sums(left, left_other, right, right_other, weight, parts, orders):
     block = left.shape[1] // parts
     wide = right.shape[1]
-    lanes = min(wide, 512)
+    lanes = 512
     rows, deep = left.shape
     return pl.pallas_call(
-        functools.partial(skip_product_kernel, block),
-        name="skip_product",
+        functools.partial(skip_kernel, orders),
+        name="skip_sums",
         grid=(wide // lanes,),
-        out_shape=jax.ShapeDtypeStruct((parts // 2, block, wide), bf16),
+        out_shape=[
+            jax.ShapeDtypeStruct((rows, deep), f32),
+            *[jax.ShapeDtypeStruct((orders[1], block, wide), bf16)] * orders[0],
+        ],
         in_specs=[pl.BlockSpec((rows, deep), lambda n: (0, 0))] * 2
-        + [pl.BlockSpec((rows, lanes), lambda n: (0, n))] * 2,
-        out_specs=pl.BlockSpec((parts // 2, block, lanes), lambda n: (0, 0, n)),
+        + [pl.BlockSpec((rows, lanes), lambda n: (0, n))] * 2
+        + [pl.BlockSpec((deep, lanes), lambda n: (0, n))],
+        out_specs=[
+            pl.BlockSpec((rows, deep), lambda n: (0, 0)),
+            *[pl.BlockSpec((orders[1], block, lanes), lambda n: (0, 0, n))] * orders[0],
+        ],
         scratch_shapes=[pltpu.VMEM((2, deep, rows), bf16)] * 2,
-        compiler_params=pltpu.CompilerParams(vmem_limit_bytes=60 * mib),
-        cost_estimate=pl.CostEstimate(
-            flops=2 * rows * deep * wide, bytes_accessed=deep * wide + 4 * rows * (deep + wide), transcendentals=0
-        ),
-    )(left, left_other, right, right_other)
-
-
-def two_products_kernel(
-    up_block, down_block, act_ref, act_other_ref, sum_ref, sum_other_ref,
-    entry_ref, entry_other_ref, first_ref, first_other_ref, out_ref, act, act_other, entry, entry_other,
+        compiler_params=pltpu.CompilerParams(vmem_limit_bytes=LIMIT * mib),
+        cost_estimate=cost(kernel_micros["skip_sums"]),
+    )(left, left_other, right, right_other, weight)
+
+
+def products_kernel(
+    orders, act_ref, act_other_ref, entry_ref, entry_other_ref, first_ref, first_other_ref, sum_ref, sum_other_ref,
+    *refs
 ):
-    own_rows(act_ref, up_block, act)
-    own_rows(act_other_ref, up_block, act_other)
-    own_rows(entry_ref, down_block, entry)
-    own_rows(entry_other_ref, down_block, entry_other)
+    clips, chips = orders
+    outs, (act, act_other, entry, entry_other, down) = refs[:clips], refs[clips:]
+    n = pl.program_id(0)
+
+    @pl.when(n == 0)
+    def _():
+        blocks = own_blocks(orders)
+        own_rows(act_ref, act, blocks)
+        own_rows(act_other_ref, act_other, blocks)
+        own_rows(entry_ref, entry, blocks)
+        own_rows(entry_other_ref, entry_other, blocks)
+        half = entry.shape[1] // 2
+        down[...] = (
+            dot(entry[1, pl.ds(0, half)], first_ref[...]) + dot(entry_other[1, pl.ds(0, half)], first_other_ref[...])
+        ).reshape(down.shape)
+
     half = act.shape[1] // 2
     up = dot(act[1, pl.ds(0, half)], sum_ref[...]) + dot(act_other[1, pl.ds(0, half)], sum_other_ref[...])
-    half = entry.shape[1] // 2
-    down = dot(entry[1, pl.ds(0, half)], first_ref[...]) + dot(entry_other[1, pl.ds(0, half)], first_other_ref[...])
-    fold = up.shape[1] // down.shape[1]
-    part = down_block // fold
-    for j in range(out_ref.shape[0]):
-        block = down[j * down_block : (j + 1) * down_block]
-        block = jnp.concatenate([block[i * part : (i + 1) * part] for i in range(fold)], axis=1)
-        out_ref[j] = jnp.concatenate([up[j * up_block : (j + 1) * up_block], block], axis=0).astype(bf16)
+    block = half // (clips * chips)
+    part = outs[0].shape[1] - block
+    for b in range(clips):
+        for z in range(chips):
+            j = b * chips + z
+            under = down[j, pl.ds(pl.multiple_of(n * part, part), part), :]
+            outs[b][z] = jnp.concatenate([up[j * block : (j + 1) * block], under], axis=0).astype(bf16)
+
+
+def up_down_sums(act, act_other, entry, entry_other, first, first_other, sums, sums_other, parts, orders):
+    rows, deep = entry.shape
+    inner, wide = act.shape[1], sums.shape[1]
+    lanes = inner
+    clips, chips = orders
+    up_block, down_block = inner // parts, deep // parts
+    block = up_block + down_block * inner // wide
+    same = lambda n: (0, 0)
+    return pl.pallas_call(
+        functools.partial(products_kernel, orders),
+        name="up_down_sums",
+        grid=(wide // lanes,),
+        out_shape=[jax.ShapeDtypeStruct((chips, block, wide), bf16)] * clips,
+        in_specs=[pl.BlockSpec((rows, inner), same)] * 2
+        + [pl.BlockSpec((rows, deep), same)] * 2
+        + [pl.BlockSpec((rows, inner), same)] * 2
+        + [pl.BlockSpec((rows, lanes), lambda n: (0, n))] * 2,
+        out_specs=[pl.BlockSpec((chips, block, lanes), lambda n: (0, 0, n))] * clips,
+        scratch_shapes=[pltpu.VMEM((2, inner, rows), bf16)] * 2
+        + [pltpu.VMEM((2, deep, rows), bf16)] * 2
+        + [pltpu.VMEM((clips * chips, down_block, inner), f32)],
+        compiler_params=pltpu.CompilerParams(vmem_limit_bytes=LIMIT * mib),
+        cost_estimate=cost(kernel_micros["up_down_sums"]),
+    )(act, act_other, entry, entry_other, first, first_other, sums, sums_other)
+
+
+def over_clip(pieces):
+    size = len(pieces)
+    return [pieces[0]] + [lax.ppermute(pieces[b], "clip", [(i, i ^ b) for i in range(size)]) for b in range(1, size)]
+
+
+def over_chips(pieces):
+    size = len(pieces)
+    return [pieces[0]] + [
+        lax.ppermute(pieces[z], "space", [(i, i ^ (2 * z)) for i in range(2 * size)]) for z in range(1, size)
+    ]
+
+
+def skipped_sums(entry, weight):
+    rows, deep = entry.shape
+    wide = weight.shape[1]
+    lanes = 512
+    return pl.pallas_call(
+        skipped_kernel,
+        name="skipped",
+        grid=(wide // lanes,),
+        out_shape=jax.ShapeDtypeStruct((rows, wide), bf16),
+        in_specs=[pl.BlockSpec((rows, deep), lambda n: (0, 0)), pl.BlockSpec((deep, lanes), lambda n: (0, n))],
+        out_specs=pl.BlockSpec((rows, lanes), lambda n: (0, n)),
+        compiler_params=pltpu.CompilerParams(vmem_limit_bytes=LIMIT * mib),
+        cost_estimate=cost(kernel_micros["skipped"]),
+    )(entry, weight)
 
 
 def after(values, token):
     return lax.optimization_barrier((values, token))[0]
-
-
-def sum_over_clip(pieces):
-    return lax.psum_scatter(pieces, "clip", scatter_dimension=0, tiled=True)
-
-
-def sum_over_chips(pieces):
-    size = lax.axis_size("space")
-    groups = [[2 * z + c for z in range(size // 2)] for c in range(2)]
-    return lax.psum_scatter(pieces, "space", scatter_dimension=0, tiled=True, axis_index_groups=groups)
 
 
 def per_device(
@@ -714,24 +986,15 @@
     rows = height * 16
     late_rows = height // 2 * 8
     late_all = clips * late_rows
-    flip = (lax.axis_index("space") & 1) == 1
     cells = height * width
     late_cells = (height // 2) * half_width
-
-    def tap_rows(kernel):
-        taps = jnp.transpose(kernel).reshape(3, 9, -1)
-        return jnp.where(flip, taps[::-1], taps).reshape(27, -1)
-
-    third_taps = tap_rows(third_depth)
-    late_taps = tap_rows(fourth_depth)
+    parts = lax.axis_size("clip") * lax.axis_size("space")
+    clip_axis, chips = lax.axis_size("clip"), lax.axis_size("space") // 2
+    by_pairs = clip_axis == 4 and chips == 4 and channels // parts % 32 == 0 and late_inner // parts % 16 == 0
+    orders = (clip_axis, chips) if by_pairs else None
     third_gain, third_shift = third_gain[None], third_shift[None]
     fourth_gain, fourth_shift = fourth_gain[None], fourth_shift[None]
-
-    own_start = lax.axis_index("clip") * clips
-    grad_rows = lax.dynamic_slice_in_dim(logit_grad, own_start, clips, 0)
-    pooled_grad = lax.dot_general(
-        grad_rows, classifier.astype(f32), (((1,), (1,)), ((), ())), precision=lax.Precision.HIGHEST
-    ).astype(bf16).astype(f32)
+    head = jnp.transpose(classifier)
 
     first, act_z, act_c, even_x = call(
         first_kernel, "first",
@@ -746,27 +1009,43 @@
         clips=clips,
     )
     got_z, got_c = swap_neighbours(act_z, act_c)
-    mid, mid_act, even_sum, moments = call(
+    third_taps, late_taps = call(
+        taps_kernel, "taps", w([jnp.transpose(third_depth), jnp.transpose(fourth_depth)]),
+        [((27, inner), f32, "w"), ((27, late_inner), f32, "w")], [],
+    )
+    (mid_part,) = call(
+        mid_own_kernel, "mid_own",
+        [(act_z, "c"), (act_c, "c"), (third_taps, "w")],
+        [((clips, 2, rows, inner), f32, "c")],
+        [pltpu.VMEM((2, rows + 32, inner), f32)],
+        clips=clips,
+    )
+    mid, mid_act, act_even, even_sum, moments, gram_up, act_sum = call(
         functools.partial(mid_kernel, width), "mid",
-        [(frame_counts, "s"), (got_z, "c"), (act_z, "c"), (act_c, "c"), (got_c, "c"),
-         (third_taps, "w"), (third_up, "w")],
+        [(frame_counts, "s"), (got_z, "c"), (got_c, "c"), (mid_part, "c"), (third_taps, "w"), (third_up, "w")],
         [
             ((clips, 2, rows, inner), f32, "c"),
             ((clips, 2, rows, inner), bf16, "c"),
-            ((clips, late_rows, channels), f32, "c"),
+            ((late_all, inner), bf16, "w"),
+            ((late_all, channels), f32, "w"),
             ((2, channels), f32, "w"),
-        ],
-        [
-            pltpu.VMEM((4, rows + 32, inner), f32),
-            pltpu.VMEM((channels // 128, 2 * rows, 128), f32),
-            pltpu.VMEM((2, 8, channels), f32),
+            ((inner, channels), f32, "w"),
+            ((1, inner), f32, "w"),
+        ],
+        [
+            pltpu.VMEM((2, rows + 32, inner), f32),
+            pltpu.VMEM((inner // 128, 2 * rows, 128), f32),
+            pltpu.VMEM((late_all, inner), f32),
+            pltpu.VMEM((inner, inner), f32),
+            pltpu.VMEM((8, inner), f32),
         ],
         clips=clips,
     )
-    moments = [(part, "w") for part in group_parts(moments)]
+    even_sum = even_sum.reshape(clips, late_rows, channels)
+    moments = group_parts(moments)
     stats, even_hat, entry, late_first, late_act = call(
         functools.partial(entry_kernel, half_width, cells, len(moments)), "entry",
-        [(frame_counts, "s"), *moments, (even_x, "w"), (even_sum, "w"),
+        [(frame_counts, "s"), *w(moments), (even_x, "w"), (even_sum, "w"),
          (third_gain, "w"), (third_shift, "w"), (fourth_down, "w")],
         [
             ((2, channels), f32, "w"),
@@ -779,7 +1058,8 @@
     )
     late_first = late_first.reshape(clips, late_rows, late_inner)
     late_z, late_c = swap_neighbours(late_act, late_act)
-    skipped = dot(entry, fourth_skip).astype(bf16).reshape(clips, late_rows, late_wide)
+    (pooled_grad,) = call(pooled_grad_kernel, "pooled_grad", w([logit_grad, head]), [((clips, late_wide), f32, "w")], [])
+    skipped = skipped_sums(entry, fourth_skip).reshape(clips, late_rows, late_wide)
     late_mid, late_mid_act, late_sum, late_moments = call(
         functools.partial(late_kernel, half_width), "late_mid",
         [(frame_counts, "s"), (late_z, "w"), (late_act, "w"), (late_c, "w"), (late_taps, "w"), (fourth_up, "w")],
@@ -795,40 +1075,51 @@
         ],
     )
     late_sum = late_sum.reshape(clips, late_rows, late_wide)
-    late_moments = [(part, "w") for part in group_parts(late_moments)]
-    late_stats, late_back, pooled_term, pre_grad, skip_grad = call(
+    late_moments = group_parts(late_moments)
+    late_stats, late_back, pre_grad, skip_grad = call(
         functools.partial(post_kernel, half_width, late_cells, len(late_moments)), "post",
-        [(frame_counts, "s"), *late_moments, (late_sum, "w"), (skipped, "w"),
+        [(frame_counts, "s"), *w(late_moments), (late_sum, "w"), (skipped, "w"),
          (fourth_gain, "w"), (fourth_shift, "w"), (pooled_grad, "w")],
         [
             ((2, late_wide), f32, "w"),
-            ((2, late_wide), f32, "w"),
-            ((clips, late_wide), f32, "w"),
+            ((2 + clips, late_wide), f32, "w"),
             ((clips, late_rows, late_wide), f32, "w"),
             ((clips, late_rows, late_wide), bf16, "w"),
         ],
         [],
     )
-    received = group_parts(jnp.concatenate((late_back, pooled_term)))
+    received = group_parts(late_back)
     skip_rows = skip_grad.reshape(late_all, late_wide)
-    skip_back = dot_t(skip_rows, fourth_skip)
-    parts = lax.axis_size("clip") * lax.axis_size("space")
-    by_pairs = channels // parts % 32 == 0 and late_inner // parts % 16 == 0
     if by_pairs:
         entry_other = core_swap(entry)
-        skip_pieces = skip_product(entry, entry_other, after(skip_rows, received[0]), core_swap(skip_rows), parts)
-        late_stats = after(late_stats, skip_pieces)
-        skip_pieces = sum_over_clip(skip_pieces)
+        skip_back, *skip_pieces = skip_sums(
+            entry, entry_other, skip_rows, core_swap(skip_rows), fourth_skip, parts, (clip_axis, chips)
+        )
     else:
+        skip_back = dot_t(skip_rows, fourth_skip)
         fourth_skip_grad = reduce_rows(t_dot(entry, skip_rows))
-    late_sum_grad, late_mid_grad = call(
+    late_stats = after(late_stats, skip_back)
+    late_sum_grad, late_mid_grad, pooled = call(
         functools.partial(sum_grad_kernel, half_width, late_cells, len(received)), "sum_grad",
-        [(frame_counts, "s"), *[(part, "w") for part in received], (late_stats, "w"), (late_sum, "w"), (pre_grad, "w"),
+        [(frame_counts, "s"), *w(received), (late_stats, "w"), (late_sum, "w"), (pre_grad, "w"),
          (fourth_gain, "w"), (fourth_up, "w"), (late_mid, "w")],
-        [((late_all, late_wide), bf16, "w"), ((clips, late_rows, late_inner), bf16, "w")],
+        [
+            ((late_all, late_wide), bf16, "w"),
+            ((clips, late_rows, late_inner), bf16, "w"),
+            ((clips, late_wide), bf16, "w"),
+        ],
         [],
     )
     late_gz, late_gc = swap_neighbours(late_mid_grad, late_mid_grad)
+    if by_pairs:
+        skip_pieces = over_clip(after(skip_pieces, late_mid_grad))
+    (late_taps_table,) = call(
+        late_taps_kernel, "late_taps",
+        [(late_z, "w"), (late_act, "w"), (late_c, "w"), (late_mid_grad, "w")],
+        [((late_inner, 128), f32, "w")],
+        [pltpu.VMEM((3, clips, late_rows + 16, late_inner), f32)],
+    )
+    late_first = after(late_first, late_taps_table)
     late_first_grad, entry_grad, third_back = call(
         functools.partial(late_back_kernel, half_width), "late_back",
         [(frame_counts, "s"), (late_gz, "w"), (late_mid_grad, "w"), (late_gc, "w"), (late_taps, "w"),
@@ -843,79 +1134,122 @@
             pltpu.VMEM((clips, late_rows, late_inner), f32),
         ],
     )
-    back_parts = group_parts(third_back)
-    (late_taps_table,) = call(
-        late_taps_kernel, "late_taps",
-        [(late_z, "w"), (late_act, "w"), (late_c, "w"), (after(late_mid_grad, back_parts[0]), "w")],
-        [((late_inner, 128), f32, "w")],
-        [pltpu.VMEM((3, clips, late_rows + 16, late_inner), f32)],
-    )
+    received = group_parts(third_back)
     if by_pairs:
-        up_block, down_block = late_inner // parts, channels // parts
-        (pieces,) = call(
-            functools.partial(two_products_kernel, up_block, down_block), "two_products",
-            [(late_mid_act, "w"), (core_swap(late_mid_act), "w"), (after(late_sum_grad, back_parts[0]), "w"), (core_swap(late_sum_grad), "w"),
-             (entry, "w"), (entry_other, "w"), (late_first_grad, "w"), (core_swap(late_first_grad), "w")],
-            [((parts // 2, up_block + down_block * late_inner // late_wide, late_wide), bf16, "w")],
-            [pltpu.VMEM((2, late_inner, late_all), bf16)] * 2 + [pltpu.VMEM((2, channels, late_all), bf16)] * 2,
+        up_pieces = up_down_sums(
+            late_mid_act, core_swap(late_mid_act), entry, entry_other, late_first_grad, core_swap(late_first_grad),
+            late_sum_grad, core_swap(late_sum_grad), parts, (clip_axis, chips),
         )
-        stats = after(stats, pieces)
-        pieces = sum_over_clip(pieces)
+        skip_pieces = call(
+            functools.partial(chip_totals_kernel, clip_axis), "skip_total",
+            [(part, "w") for part in after(skip_pieces, up_pieces[0])],
+            [(skip_pieces[0].shape[1:], bf16, "w")] * chips, [],
+        )
+        stats = after(stats, skip_pieces[0])
     else:
         fourth_up_grad = reduce_rows(t_dot(late_mid_act, late_sum_grad))
         fourth_down_grad = reduce_rows(t_dot(entry, late_first_grad))
-    back_parts = [(part, "w") for part in back_parts]
-    third_sum_grad, grad_z, grad_c = call(
-        functools.partial(third_grad_kernel, width, cells, len(back_parts)), "third_grad",
-        [(frame_counts, "s"), *back_parts, (stats, "w"), (mid_act, "c"), (mid, "c"),
-         (entry_grad, "c"), (third_gain, "w"), (third_up, "w")],
-        [
-            ((clips, 2, rows, channels), bf16, "c"),
+    grad_z, grad_c, up_terms = call(
+        functools.partial(third_grad_kernel, width, cells, len(received)), "third_grad",
+        [(frame_counts, "s"), *w(received), (stats, "w"), (third_gain, "w"),
+         (entry_grad.reshape(late_all, channels), "w"), (third_up, "w"), (act_even, "w"), (act_sum, "w"),
+         (gram_up, "w"), (mid_act, "c"), (mid, "c")],
+        [
             ((clips, rows, inner), bf16, "c"),
             ((clips, rows, inner), bf16, "c"),
-        ],
-        [pltpu.VMEM((channels // 128, 2 * rows, 128), f32)],
+            ((inner, channels), bf16, "w"),
+        ],
+        [
+            pltpu.VMEM((late_all, inner), f32),
+            pltpu.VMEM((2, inner, inner), bf16),
+            pltpu.VMEM((1, inner), f32),
+            pltpu.VMEM((inner // 128, 2 * rows, 128), f32),
+        ],
         clips=clips,
     )
     third_gz, third_gc = swap_neighbours(grad_z, grad_c)
-    (third_terms,) = call(
-        third_sums_kernel, "third_sums",
+    small_rows = 8 + clips * clip_axis + late_inner // parts
+    deep = inner // parts
+    extra = 128 * (1 + small_rows // deep)
+    if by_pairs:
+        term_outputs = [
+            ((clip_axis, chips, deep, channels + extra), f32, "w"),
+            ((clip_axis, chips, deep, channels + extra), bf16, "w"),
+        ]
+    else:
+        term_outputs = [((inner, channels + extra), bf16, "w")]
+    third_terms = call(
+        functools.partial(third_taps_kernel, orders, parts), "third_taps",
         [(got_z, "c"), (act_z, "c"), (act_c, "c"), (got_c, "c"), (grad_z, "c"), (grad_c, "c"),
-         (mid_act, "c"), (third_sum_grad, "c")],
-        [((inner, channels + 128), bf16, "w")],
+         (up_terms, "w"), (late_back, "w"), (third_back, "w"), (pooled, "w"), (late_taps_table, "w")],
+        term_outputs,
         [
             pltpu.VMEM((4, rows + 32, inner), f32),
             pltpu.VMEM((2, rows, inner), f32),
             pltpu.VMEM((27, 8, inner), f32),
-            pltpu.VMEM((inner, channels), f32),
+            pltpu.VMEM((inner, channels + extra), f32),
         ],
         clips=clips,
     )
-    first = after(first, third_terms)
-    third_terms = send_rows(third_terms)
-    first_grad, third_down_term = call(
-        functools.partial(first_grad_kernel, width), "first_grad",
+    first = after(first, third_terms[0])
+    if by_pairs:
+        up_pieces = over_clip(after(up_pieces, skip_pieces[0]))
+        skip_pieces = over_chips(after(skip_pieces, third_terms[0]))
+    block = channels // parts
+    if by_pairs:
+        down_outputs = [
+            ((clip_axis, chips, block, inner), f32, "w"),
+            ((clip_axis, chips, block, inner), bf16, "w"),
+        ]
+        down_scratch = [pltpu.VMEM((parts, block, inner), f32)]
+    else:
+        down_outputs, down_scratch = [((channels, inner), bf16, "w")], []
+    first_grad, *down_terms = call(
+        functools.partial(first_grad_kernel, width, (clip_axis, chips, block) if by_pairs else None), "first_grad",
         [(frame_counts, "s"), (third_gz, "c"), (grad_z, "c"), (grad_c, "c"), (third_gc, "c"),
          (third_taps, "w"), (first, "c"), (clip_input, "c")],
-        [((clips, 2 * rows, inner), bf16, "c"), ((channels, inner), bf16, "w")],
-        [
+        [((clips, 2 * rows, inner), bf16, "c"), *down_outputs],
+        [
+            *down_scratch,
             pltpu.VMEM((4, rows + 32, inner), f32),
             pltpu.VMEM((2 * rows, channels), bf16),
-            pltpu.VMEM((channels, inner), f32),
+            pltpu.VMEM((inner, channels), f32),
         ],
         clips=clips,
     )
-    third_down_rows = send_rows(third_down_term)
     if by_pairs:
-        pieces = jnp.concatenate((after(skip_pieces, first_grad), pieces), axis=1)
-        pieces = sum_over_chips(pieces)[0].astype(f32)
-        fourth_skip_grad = pieces[:down_block]
-        fourth_up_grad = pieces[down_block : down_block + up_block]
-        fold = late_wide // late_inner
-        fourth_down_grad = jnp.moveaxis(
-            pieces[down_block + up_block :].reshape(-1, fold, late_inner), 1, 0
-        ).reshape(down_block, late_inner)
-    third_terms = add_rows(after(third_terms, first_grad))
+        keep, send = down_terms
+        keep_terms, send_terms = third_terms
+        clip_parts = call(
+            pair_sum_kernel, "pair_sum",
+            w([keep, core_swap(send), keep_terms, core_swap(after(send_terms, third_gz))]),
+            [((chips, deep, channels + extra + block // deep * inner), bf16, "w")] * clip_axis,
+            [],
+        )
+        up_pieces = call(
+            functools.partial(chip_totals_kernel, clip_axis), "up_down_total", w(after(up_pieces, clip_parts[0])),
+            [(up_pieces[0].shape[1:], bf16, "w")] * chips, [],
+        )
+        clip_parts = over_clip(clip_parts)
+        up_pieces = over_chips(up_pieces)
+        chip_parts = call(
+            functools.partial(chip_totals_kernel, clip_axis), "clip_sum", w(after(clip_parts, up_pieces[0])),
+            [(clip_parts[0].shape[1:], bf16, "w")] * chips, [],
+        )
+        third_terms = [part[None] for part in over_chips(chip_parts)]
+        up_block = late_inner // parts
+        fourth_skip_grad, fourth_up_grad, fourth_down_grad = call(
+            functools.partial(finish_kernel, chips), "finish", w(skip_pieces + up_pieces),
+            [
+                ((block, late_wide), f32, "w"),
+                ((up_block, late_wide), f32, "w"),
+                ((block, late_inner), f32, "w"),
+            ],
+            [],
+        )
+    else:
+        third_down_grad = add_rows(send_rows(down_terms[0]))
+        third_terms = [send_rows(third_terms[0])]
     (clip_grad,) = call(
         clip_grad_kernel, "clip_grad",
         [(first_grad, "c"), (third_down, "w"), (entry_grad, "c")],
@@ -924,42 +1258,45 @@
         clips=clips,
     )
 
+    logits, bias_grad = call(
+        head_kernel, "head", w([after(pooled, first_grad), head, class_bias[None], logit_grad]),
+        [((clips, logit_grad.shape[1]), f32, "w"), ((1, logit_grad.shape[1]), f32, "w")], [],
+    )
     own, own_third, own_taps = late_wide // parts, channels // parts, late_inner // parts
-    pooled, packed = call(
-        functools.partial(pack_kernel, parts, len(received)), "pack",
-        [(late_back, "w"), (third_back, "w"), (late_taps_table, "w"), *[(part, "w") for part in received]],
-        [((clips, late_wide), bf16, "w"), ((parts, 4 + clips + own_taps, 128), f32, "w")],
+    third_up_grad, third_depth_grad, gain, shift, late_gain, late_shift, fourth_depth_grad, classifier_grad, *down = call(
+        functools.partial(terms_kernel, len(third_terms), clips, channels, small_rows), "terms",
+        w(third_terms + [logit_grad]),
+        [
+            ((deep, channels), f32, "w"),
+            ((deep, 27), f32, "w"),
+            ((1, own_third), f32, "w"),
+            ((1, own_third), f32, "w"),
+            ((1, own), f32, "w"),
+            ((1, own), f32, "w"),
+            ((own_taps, 27), f32, "w"),
+            ((own, logit_grad.shape[1]), f32, "w"),
+            *([((block, inner), f32, "w")] if by_pairs else []),
+        ],
         [],
     )
-    logits = dot(pooled, classifier) + class_bias
-    packed = lax.all_to_all(packed, ("clip", "space"), split_axis=0, concat_axis=0, tiled=True)
-    packed = after(packed, first_grad)
-    device = lax.axis_index("clip") * lax.axis_size("space") + lax.axis_index("space")
-    totals = jnp.sum(packed, axis=0)
-    late_sums = lax.dynamic_slice_in_dim(totals[0:2], device * own % 128, own, 1)
-    third_sums = lax.dynamic_slice_in_dim(totals[2:4], device * own_third % 128, own_third, 1)
-    fourth_depth_grad = totals[4 + clips :, :27]
-    gathered = packed.reshape((lax.axis_size("clip"), lax.axis_size("space")) + packed.shape[1:])[:, 0, 4 : 4 + clips]
-    gathered = lax.dynamic_slice_in_dim(gathered.reshape(-1, 128), device * own % 128, own, 1)
-    classifier_grad = lax.dot_general(
-        gathered, logit_grad, (((0,), (0,)), ((), ())), precision=lax.Precision.HIGHEST
-    )
+    if by_pairs:
+        (third_down_grad,) = down
     return (
         logits,
         clip_grad,
-        add_rows(third_down_rows),
-        third_terms[:, channels : channels + 27],
-        third_terms[:, :channels],
-        third_sums[1],
-        third_sums[0],
+        third_down_grad,
+        third_depth_grad,
+        third_up_grad,
+        gain.reshape(-1),
+        shift.reshape(-1),
         fourth_down_grad,
         fourth_skip_grad,
         fourth_depth_grad,
         fourth_up_grad,
-        late_sums[1],
-        late_sums[0],
+        late_gain.reshape(-1),
+        late_shift.reshape(-1),
         classifier_grad,
-        jnp.sum(logit_grad, axis=0),
+        bias_grad.reshape(-1),
     )
 
 

time: 243 us -> 175 us (0.72)
  Pallas kernels: 86.2 us -> 57.6 us
  starting transfers between devices: 54.2 us -> 76 us
  local copies, waits for them, and re-layouts: 27.9 us -> 8.16 us
  matrix products: 13.1 us -> 0 us
  between operations: 14.2 us -> 1.19 us
  other arithmetic: 8.34 us -> 0 us
  waiting for transfers between devices: 37.9 us -> 32.3 us
    pallas_call x14 -> x26, Pallas kernels: 80.8 us -> 49.2 us  [call(): pl.pallas_call(kernel, name=name, out_shape=[jax.ShapeDtypeStruct(s, d) f...]
    ppermute x16 -> x30, starting transfers between devices: 27.8 us -> 51.5 us  [the longest x21 40.2 us: over_chips(): lax.ppermute(pieces[z], 'space', [(i, i ^ 2 * z) for i in range(2 * size)])]
    all_to_all x3 -> x0, waiting for transfers between devices: 13.6 us -> none  [the longest x2 13.6 us: send_rows(): lax.all_to_all(pieces, ('clip', 'space'), split_axis=0, concat_axis=0, ti...]
    all_to_all x3 -> x0, starting transfers between devices: 13.2 us -> none  [the longest x2 9.37 us: send_rows(): lax.all_to_all(pieces, ('clip', 'space'), split_axis=0, concat_axis=0, ti...]
    dot_general x5 -> x0, matrix products: 13.1 us -> none  [the longest x2 5.38 us: dot(): return jnp.dot(left, right, preferred_element_type=f32)]
    unnamed x74 -> x32, local copies, waits for them, and re-layouts: 20.9 us -> 8.16 us
    ppermute x5 -> x11, starting transfers between devices: 0.59 us -> 11.7 us  [core_swap(): lax.ppermute(values, 'space', [(i, i ^ 1) for i in range(lax.axis_size('s...]
    ppermute x5 -> x11, waiting for transfers between devices: 0.01 us -> 6.79 us  [core_swap(): lax.ppermute(values, 'space', [(i, i ^ 1) for i in range(lax.axis_size('s...]
  transfers between devices with their start and end apart: 35 -> 49, of which waited for: 11 -> 15; matrix products, arithmetic and copies ran while one was open for 13% -> 3% of each run, Pallas kernels for 21% -> 21%
where the time goes in v2:
time: 175 us
  starting transfers between devices  76 us (43%)
  Pallas kernels  57.6 us (33%)
  waiting for transfers between devices  32.3 us (18%)
  local copies, waits for them, and re-layouts  8.16 us (5%)
    pallas_call x26, Pallas kernels, call(): pl.pallas_call(kernel, name=name, out_shape=[jax.ShapeDtypeStruct(s, d) f...  49.2 us
    ppermute x21, starting transfers between devices, over_chips(): lax.ppermute(pieces[z], 'space', [(i, i ^ 2 * z) for i in range(2 * size)])  40.2 us
    ppermute x9, waiting for transfers between devices, over_clip(): lax.ppermute(pieces[b], 'clip', [(i, i ^ b) for i in range(size)])  16.1 us
    ppermute x11, starting transfers between devices, core_swap(): lax.ppermute(values, 'space', [(i, i ^ 1) for i in range(lax.axis_size('s...  11.7 us
    ppermute x9, starting transfers between devices, over_clip(): lax.ppermute(pieces[b], 'clip', [(i, i ^ b) for i in range(size)])  11.4 us
    ppermute x4, starting transfers between devices, swap_neighbours(): lax.ppermute(to_core, 'space', core)  9.75 us
    unnamed x32, local copies, waits for them, and re-layouts  8.16 us
    ppermute x21, waiting for transfers between devices, over_chips(): lax.ppermute(pieces[z], 'space', [(i, i ^ 2 * z) for i in range(2 * size)])  7.88 us
  transfers between devices with their start and end apart: 49, of which 15 were waited for; matrix products, arithmetic and copies ran while one was open for 3% of the time, Pallas kernels for 21%

profile of v2, /device:TPU:0, one launch (start us, length us, event | category | flops | bytes accessed | tf_op | source)
XLA Modules:
  0.0 175.2 jit_solution(104941227005749511)
XLA Ops:
  0.7 3.0 %copy.31.x_ref = bf16[4,2,14,14,1024]{4,3,2,1,0:T(8,128)(2,1)S(1)} copy(bf16[4,2,14,14,1024]{4,1,3,2,0:T(2,128)(2,1)} %param.16) | data formatting | bytes 6422528 | tf_op args[0]
  3.8 3.0 %first.1 = (f32[4,2,224,256]{3,2,1,0:T(8,128)S(1)}, bf16[4,224,256]{2,1,0:T(8,128)(2,1)S(1)}, bf16[4,224,256]{2,1,0:T(8,128)(2,1)S(1)}, f32[4,56,1024]{2,1,0:T(8,128)S(1)}) custom-call(s32[4]{0:T(128)S(1)} %copy-done.8, bf16[4,2,14,14,1024]{4,3,2,1,0:T(8,128)(2,1)S(1)} %copy.31.x_ref, bf16[1024,256]{1,0:T(8,128)(2,1)S(1)} %copy-done.4), custom_call_target="tpu_custom_call" | custom-call | bytes 18020000 | tf_op jit(solution)/shard_map/first/pallas_call | solution.py:777
  7.6 4.4 %collective-permute-start.1 = (bf16[4,224,256]{2,1,0:T(8,128)(2,1)S(1)}, bf16[4,224,256]{2,1,0:T(8,128)(2,1)S(1)}, u32[]{:S(2)}, u32[]{:S(2)}) collective-permute-start(bf16[4,224,256]{2,1,0:T(8,128)(2,1)S(1)} %get-tuple-element.125.oc_ref), channel_id=1, source_target_pairs={{0,1},{1,0},{2,3},{3,2},{4,5},{5,4},{6,7},{7,6},{8,9},{9,8},{10,11... | collective-permute-start | bytes 1376264 | tf_op jit(solution)/shard_map/ppermute | solution.py:807
  12.0 3.0 %mid_own.1.part_ref = f32[4,2,224,256]{3,2,1,0:T(8,128)S(1)} custom-call(bf16[4,224,256]{2,1,0:T(8,128)(2,1)S(1)} %get-tuple-element.124.oz_ref, bf16[4,224,256]{2,1,0:T(8,128)(2,1)S(1)} %get-tuple-element.125.oc_ref, f32[27,256]{1,0:T(8,128)S(1)} %get-tuple-element.126.taps_ref), custom_call_target="tpu_custom_call" | custom-call | bytes 17000000 | tf_op jit(solution)/shard_map/mid_own/pallas_call | solution.py:777
  15.1 6.1 %mid.1 = (f32[4,2,224,256]{3,2,1,0:T(8,128)S(1)}, bf16[4,2,224,256]{3,2,1,0:T(8,128)(2,1)S(1)}, bf16[224,256]{1,0:T(8,128)(2,1)S(1)}, f32[224,1024]{1,0:T(8,128)...) custom-call(s32[4]{0:T(128)S(1)} %copy-done.8, ...), custom_call_target="tpu_custom_call" | custom-call | bytes 29240000 | tf_op jit(solution)/shard_map/mid/pallas_call | solution.py:777
  21.2 3.0 %collective-permute-start.2 = (f32[2,1024]{1,0:T(2,128)S(1)}, f32[2,1024]{1,0:T(2,128)S(1)}, u32[]{:S(2)}, u32[]{:S(2)}) collective-permute-start(f32[2,1024]{1,0:T(2,128)S(1)} %get-tuple-element.127.one_ref), channel_id=1, source_target_pairs={{0,1},{1,0},{2,3},{3,2},{4,5},{5,4},{6,7},{7,6},{8,9},{9,8},{10,11... | collective-permute-start | bytes 24584 | tf_op jit(solution)/shard_map/ppermute | solution.py:825
  31.6 3.5 %collective-permute-done.5 = f32[2,1024]{1,0:T(2,128)S(1)} collective-permute-done((f32[2,1024]{1,0:T(2,128)S(1)}, f32[2,1024]{1,0:T(2,128)S(1)}, u32[]{:S(2)}, u32[]{:S(2)}) %collective-permute-start.5) | collective-permute-done | bytes 8224 | tf_op jit(solution)/shard_map/ppermute | solution.py:952
  40.9 3.6 %collective-permute-start.8 = (f32[2,2048]{1,0:T(2,128)S(1)}, f32[2,2048]{1,0:T(2,128)S(1)}, u32[]{:S(2)}, u32[]{:S(2)}) collective-permute-start(f32[2,2048]{1,0:T(2,128)S(1)} %get-tuple-element.132.one_ref), channel_id=1, source_target_pairs={{0,1},{1,0},{2,3},{3,2},{4,5},{5,4},{6,7},{7,6},{8,9},{9,8},{10,11... | collective-permute-start | bytes 49160 | tf_op jit(solution)/shard_map/ppermute | solution.py:825
  53.4 2.9 %post.1 = (f32[2,2048]{1,0:T(2,128)S(1)}, f32[6,2048]{1,0:T(8,128)S(1)}, f32[4,56,2048]{2,1,0:T(8,128)S(1)}, bf16[4,56,2048]{2,1,0:T(8,128)(2,1)S(1)}) custom-call(s32[4]{0:T(128)S(1)} %copy-done.8, f32[1,2,2048]{2,1,0:T(2,128)S(1)} %bitcast.53, f32[1,2,2048]{2,1,0:T(2,128)S(1)} %bitcast.64, f32[1,2,2048]{2,1,0:T(2,128)S(1)} %bitcast.65, ...), custom_call_target="tpu_custom_call" | custom-call | bytes 20400000 | tf_op jit(solution)/shard_map/post/pallas_call | solution.py:777
  57.0 2.6 %collective-permute-done.12.two_ref = f32[6,2048]{1,0:T(8,128)S(1)} collective-permute-done((f32[6,2048]{1,0:T(8,128)S(1)}, f32[6,2048]{1,0:T(8,128)S(1)}, u32[]{:S(2)}, u32[]{:S(2)}) %collective-permute-start.12) | collective-permute-done | bytes 49184 | tf_op jit(solution)/shard_map/ppermute | solution.py:825
  64.1 4.1 %skip_sums.1 = (f32[224,1024]{1,0:T(8,128)S(1)}, bf16[4,32,2048]{2,1,0:T(8,128)(2,1)S(1)}, bf16[4,32,2048]{2,1,0:T(8,128)(2,1)S(1)}, bf16[4,32,2048]{2,1,0:T(8,128)(2,1)S(1)}, bf16[4,32,2048]{2,1,0:T(8,128)(2,1)S(1)}) custom-call(bf16[224,1024]{1,0:T(8,128)(2,1)S(1)} %get-tuple-element.134.entry_ref.left_ref, ...), custom_call_target="tpu_custom_call" | custom-call | bytes 23800000 | tf_op jit(solution)/shard_map/skip_sums/pallas_call | solution.py:866
  70.9 2.7 %collective-permute-start.19 = (bf16[4,56,512]{2,1,0:T(8,128)(2,1)S(1)}, bf16[4,56,512]{2,1,0:T(8,128)(2,1)S(1)}, u32[]{:S(2)}, u32[]{:S(2)}) collective-permute-start(bf16[4,56,512]{2,1,0:T(8,128)(2,1)S(1)} %get-tuple-element.143.grad_ref.own_ref), channel_id=1, source_target_pairs={{0,1},{1,0},{2,3},{3,2},{4,5},{5,4},{6,7},{7,6},{8,9},{9,8},{10,11... | collective-permute-start | bytes 688136 | tf_op jit(solution)/shard_map/ppermute | solution.py:807
  77.1 3.3 %collective-permute-start.27 = (bf16[224,512]{1,0:T(8,128)(2,1)S(1)}, bf16[224,512]{1,0:T(8,128)(2,1)S(1)}, u32[]{:S(2)}, u32[]{:S(2)}) collective-permute-start(bf16[224,512]{1,0:T(8,128)(2,1)S(1)} %get-tuple-element.157.act_ref), channel_id=1, source_target_pairs={{0,1},{1,0},{2,3},{3,2},{4,5},{5,4},{6,7},{7,6},{8,9},{9,8},{10,11... | collective-permute-start | bytes 688136 | tf_op jit(solution)/shard_map/ppermute | solution.py:825
  94.0 5.9 %collective-permute-done.25.refs_2_ = bf16[4,32,2048]{2,1,0:T(8,128)(2,1)S(1)} collective-permute-done((bf16[4,32,2048]{2,1,0:T(8,128)(2,1)S(1)}, bf16[4,32,2048]{2,1,0:T(8,128)(2,1)S(1)}, u32[]{:S(2)}, u32[]{:S(2)}) %collective-permute-start.25) | collective-permute-done | bytes 524320 | tf_op jit(solution)/shard_map/ppermute | solution.py:946
  100.2 3.6 %third_grad.1 = (bf16[4,224,256]{2,1,0:T(8,128)(2,1)S(1)}, bf16[4,224,256]{2,1,0:T(8,128)(2,1)S(1)}, bf16[256,1024]{1,0:T(8,128)(2,1)S(1)}) custom-call(s32[4]{0:T(128)S(1)} %copy-done.8, f32[1,2,1024]{2,1,0:T(2,128)S(1)} %bitcast.61, f32[1,2,1024]{2,1,0:T(2,128)S(1)} %bitcast.70, f32[1,2,1024]{2,1,0:T(2,128)S(1)} %bitcast.71, f32[1,2,1024]{2,1,0:T(2,128)S(1)} %bitcast.72, ...), custom_call_target="tpu_custom_call" | custom-call | bytes 22780000 | tf_op jit(solution)/shard_map/third_grad/pallas_call | solution.py:777
  107.1 5.3 %third_taps.1 = (f32[4,4,8,1792]{3,2,1,0:T(8,128)S(1)}, bf16[4,4,8,1792]{3,2,1,0:T(8,128)(2,1)S(1)}) custom-call(bf16[4,224,256]{2,1,0:T(8,128)(2,1)S(1)} %collective-permute-done.rz_ref, bf16[4,224,256]{2,1,0:T(8,128)(2,1)S(1)} %get-tuple-element.124.oz_ref, bf16[4,224,256]{2,1,0:T(8,128)(2,1)S(1)} %get-tuple-element.125.oc_ref, ...), custom_call_target="tpu_custom_call" | custom-call | bytes 26180000 | tf_op jit(solution)/shard_map/third_taps/pallas_call | solution.py:777
  113.2 9.1 %first_grad.1 = (bf16[4,448,256]{2,1,0:T(8,128)(2,1)S(1)}, f32[4,4,32,256]{3,2,1,0:T(8,128)S(1)}, bf16[4,4,32,256]{3,2,1,0:T(8,128)(2,1)S(1)}) custom-call(s32[4]{0:T(128)S(1)} %copy-done.8, bf16[4,224,256]{2,1,0:T(8,128)(2,1)S(1)} %collective-permute-done.30.rz_ref, bf16[4,224,256]{2,1,0:T(8,128)(2,1)S(1)} %get-tuple-element.173.gz_ref, ...), custom_call_target="tpu_custom_call" | custom-call | bytes 36380000 | tf_op jit(solution)/shard_map/first_grad/pallas_call | solution.py:777
  135.8 8.2 %collective-permute-done.38.refs_2_ = bf16[4,24,2048]{2,1,0:T(8,128)(2,1)S(1)} collective-permute-done((bf16[4,24,2048]{2,1,0:T(8,128)(2,1)S(1)}, bf16[4,24,2048]{2,1,0:T(8,128)(2,1)S(1)}, u32[]{:S(2)}, u32[]{:S(2)}) %collective-permute-start.38) | collective-permute-done | bytes 393248 | tf_op jit(solution)/shard_map/ppermute | solution.py:946
  144.0 2.8 %collective-permute-start.44 = (bf16[32,2048]{1,0:T(8,128)(2,1)S(1)}, bf16[32,2048]{1,0:T(8,128)(2,1)S(1)}, u32[]{:S(2)}, u32[]{:S(2)}) collective-permute-start(bf16[32,2048]{1,0:T(8,128)(2,1)S(1)} %get-tuple-element.220), channel_id=1, source_target_pairs={{0,4},{1,5},{2,6},{3,7},{4,0},{5,1},{6,2},{7,3},{8,12},{9,13},{10,... | collective-permute-start | bytes 393224 | tf_op jit(solution)/shard_map/ppermute | solution.py:952
  148.8 2.7 %collective-permute-start.47 = (bf16[24,2048]{1,0:T(8,128)(2,1)S(1)}, bf16[24,2048]{1,0:T(8,128)(2,1)S(1)}, u32[]{:S(2)}, u32[]{:S(2)}) collective-permute-start(bf16[24,2048]{1,0:T(8,128)(2,1)S(1)} %get-tuple-element.223), channel_id=1, source_target_pairs={{0,4},{1,5},{2,6},{3,7},{4,0},{5,1},{6,2},{7,3},{8,12},{9,13},{10,... | collective-permute-start | bytes 294920 | tf_op jit(solution)/shard_map/ppermute | solution.py:952
  154.0 3.4 %collective-permute-start.40 = (bf16[8,2816]{1,0:T(8,128)(2,1)S(1)}, bf16[8,2816]{1,0:T(8,128)(2,1)S(1)}, u32[]{:S(2)}, u32[]{:S(2)}) collective-permute-start(bf16[8,2816]{1,0:T(8,128)(2,1)S(1)} %get-tuple-element.207), channel_id=1, source_target_pairs={{0,2},{1,3},{2,0},{3,1},{4,6},{5,7},{6,4},{7,5},{8,10},{9,11},{10,... | collective-permute-start | bytes 135176 | tf_op jit(solution)/shard_map/ppermute | solution.py:952
  157.3 6.7 %collective-permute-start.41 = (bf16[8,2816]{1,0:T(8,128)(2,1)S(1)}, bf16[8,2816]{1,0:T(8,128)(2,1)S(1)}, u32[]{:S(2)}, u32[]{:S(2)}) collective-permute-start(bf16[8,2816]{1,0:T(8,128)(2,1)S(1)} %get-tuple-element.208), channel_id=1, source_target_pairs={{0,4},{1,5},{2,6},{3,7},{4,0},{5,1},{6,2},{7,3},{8,12},{9,13},{10,... | collective-permute-start | bytes 135176 | tf_op jit(solution)/shard_map/ppermute | solution.py:952
  164.5 2.7 %clip_grad.1 = bf16[4,2,14,14,1024]{4,3,2,1,0:T(8,128)(2,1)S(1)} custom-call(bf16[4,448,256]{2,1,0:T(8,128)(2,1)S(1)} %get-tuple-element.179.grad_ref, bf16[1024,256]{1,0:T(8,128)(2,1)S(1)} %copy-done.4, f32[4,56,1024]{2,1,0:T(8,128)S(1)} %get-tuple-element.167.entry_grad_ref), custom_call_target="tpu_custom_call" | custom-call | bytes 18700000 | tf_op jit(solution)/shard_map/clip_grad/pallas_call | solution.py:777
  167.2 5.0 %copy.33 = bf16[4,2,14,14,1024]{4,1,3,2,0:T(2,128)(2,1)} copy(bf16[4,2,14,14,1024]{4,3,2,1,0:T(8,128)(2,1)S(1)} %clip_grad.1) | data formatting | bytes 6422528
  (135 shorter events, 73.5 us)
Async XLA Ops:
  59.7 8.6 %collective-permute-start.14 = (f32[6,2048]{1,0:T(8,128)S(1)}, f32[6,2048]{1,0:T(8,128)S(1)}, u32[]{:S(2)}, u32[]{:S(2)}) collective-permute-start(f32[6,2048]{1,0:T(8,128)S(1)} %add.6), channel_id=1, source_target_pairs={{0,4},{1,5},{2,6},{3,7},{4,0},{5,1},{6,2},{7,3},{8,12},{9,13},{10,... | collective-permute-start | bytes 147464 | tf_op jit(solution)/shard_map/ppermute | solution.py:952
  70.0 19.9 %collective-permute-start.29 = (bf16[224,2048]{1,0:T(8,128)(2,1)S(1)}, bf16[224,2048]{1,0:T(8,128)(2,1)S(1)}, u32[]{:S(2)}, u32[]{:S(2)}) collective-permute-start(bf16[224,2048]{1,0:T(8,128)(2,1)S(1)} %get-tuple-element.159.sum_ref), channel_id=1, source_target_pairs={{0,1},{1,0},{2,3},{3,2},{4,5},{5,4},{6,7},{7,6},{8,9},{9,8},{10,11... | collective-permute-start | bytes 2752520 | tf_op jit(solution)/shard_map/ppermute | solution.py:825
  73.6 14.8 %collective-permute-start.24 = (bf16[4,32,2048]{2,1,0:T(8,128)(2,1)S(1)}, bf16[4,32,2048]{2,1,0:T(8,128)(2,1)S(1)}, u32[]{:S(2)}, u32[]{:S(2)}) collective-permute-start(bf16[4,32,2048]{2,1,0:T(8,128)(2,1)S(1)} %get-tuple-element.154), channel_id=1, source_target_pairs={{0,8},{8,0},{16,24},{24,16},{1,9},{9,1},{17,25},{25,17},{2,10},{10... | collective-permute-start | bytes 1572872 | tf_op jit(solution)/shard_map/ppermute | solution.py:946
  75.1 24.9 %collective-permute-start.25 = (bf16[4,32,2048]{2,1,0:T(8,128)(2,1)S(1)}, bf16[4,32,2048]{2,1,0:T(8,128)(2,1)S(1)}, u32[]{:S(2)}, u32[]{:S(2)}) collective-permute-start(bf16[4,32,2048]{2,1,0:T(8,128)(2,1)S(1)} %get-tuple-element.155), channel_id=1, source_target_pairs={{0,16},{8,24},{16,0},{24,8},{1,17},{9,25},{17,1},{25,9},{2,18},{10... | collective-permute-start | bytes 1572872 | tf_op jit(solution)/shard_map/ppermute | solution.py:946
  76.6 23.3 %collective-permute-start.26 = (bf16[4,32,2048]{2,1,0:T(8,128)(2,1)S(1)}, bf16[4,32,2048]{2,1,0:T(8,128)(2,1)S(1)}, u32[]{:S(2)}, u32[]{:S(2)}) collective-permute-start(bf16[4,32,2048]{2,1,0:T(8,128)(2,1)S(1)} %get-tuple-element.156), channel_id=1, source_target_pairs={{0,24},{8,16},{16,8},{24,0},{1,25},{9,17},{17,9},{25,1},{2,26},{10... | collective-permute-start | bytes 1572872 | tf_op jit(solution)/shard_map/ppermute | solution.py:946
  87.1 13.1 %collective-permute-start.21 = (f32[2,1024]{1,0:T(2,128)S(1)}, f32[2,1024]{1,0:T(2,128)S(1)}, u32[]{:S(2)}, u32[]{:S(2)}) collective-permute-start(f32[2,1024]{1,0:T(2,128)S(1)} %add.7), channel_id=1, source_target_pairs={{0,2},{1,3},{2,0},{3,1},{4,6},{5,7},{6,4},{7,5},{8,10},{9,11},{10,... | collective-permute-start | bytes 24584 | tf_op jit(solution)/shard_map/ppermute | solution.py:952
  88.4 11.8 %collective-permute-start.22 = (f32[2,1024]{1,0:T(2,128)S(1)}, f32[2,1024]{1,0:T(2,128)S(1)}, u32[]{:S(2)}, u32[]{:S(2)}) collective-permute-start(f32[2,1024]{1,0:T(2,128)S(1)} %add.7), channel_id=1, source_target_pairs={{0,4},{1,5},{2,6},{3,7},{4,0},{5,1},{6,2},{7,3},{8,12},{9,13},{10,... | collective-permute-start | bytes 24584 | tf_op jit(solution)/shard_map/ppermute | solution.py:952
  89.8 10.4 %collective-permute-start.23 = (f32[2,1024]{1,0:T(2,128)S(1)}, f32[2,1024]{1,0:T(2,128)S(1)}, u32[]{:S(2)}, u32[]{:S(2)}) collective-permute-start(f32[2,1024]{1,0:T(2,128)S(1)} %add.7), channel_id=1, source_target_pairs={{0,6},{1,7},{2,4},{3,5},{4,2},{5,3},{6,0},{7,1},{8,14},{9,15},{10,... | collective-permute-start | bytes 24584 | tf_op jit(solution)/shard_map/ppermute | solution.py:952
  104.5 8.7 %collective-permute-start.31 = (bf16[4,224,256]{2,1,0:T(8,128)(2,1)S(1)}, bf16[4,224,256]{2,1,0:T(8,128)(2,1)S(1)}, u32[]{:S(2)}, u32[]{:S(2)}) collective-permute-start(bf16[4,224,256]{2,1,0:T(8,128)(2,1)S(1)} %get-tuple-element.174.gc_ref), channel_id=1, source_target_pairs={{0,1},{1,0},{2,3},{3,2},{4,5},{5,4},{6,7},{7,6},{8,9},{9,8},{10,11... | collective-permute-start | bytes 1376264 | tf_op jit(solution)/shard_map/ppermute | solution.py:807
  112.3 15.6 %collective-permute-start.33 = (bf16[4,4,8,1792]{3,2,1,0:T(8,128)(2,1)S(1)}, bf16[4,4,8,1792]{3,2,1,0:T(8,128)(2,1)S(1)}, u32[]{:S(2)}, u32[]{:S(2)}) collective-permute-start(bf16[4,4,8,1792]{3,2,1,0:T(8,128)(2,1)S(1)} %get-tuple-element.185), channel_id=1, source_target_pairs={{0,1},{1,0},{2,3},{3,2},{4,5},{5,4},{6,7},{7,6},{8,9},{9,8},{10,11... | collective-permute-start | bytes 1376264 | tf_op jit(solution)/shard_map/ppermute | solution.py:825
  122.3 12.0 %collective-permute-start.37 = (bf16[4,24,2048]{2,1,0:T(8,128)(2,1)S(1)}, bf16[4,24,2048]{2,1,0:T(8,128)(2,1)S(1)}, u32[]{:S(2)}, u32[]{:S(2)}) collective-permute-start(bf16[4,24,2048]{2,1,0:T(8,128)(2,1)S(1)} %get-tuple-element.194), channel_id=1, source_target_pairs={{0,8},{8,0},{16,24},{24,16},{1,9},{9,1},{17,25},{25,17},{2,10},{10... | collective-permute-start | bytes 1179656 | tf_op jit(solution)/shard_map/ppermute | solution.py:946
  123.6 20.4 %collective-permute-start.38 = (bf16[4,24,2048]{2,1,0:T(8,128)(2,1)S(1)}, bf16[4,24,2048]{2,1,0:T(8,128)(2,1)S(1)}, u32[]{:S(2)}, u32[]{:S(2)}) collective-permute-start(bf16[4,24,2048]{2,1,0:T(8,128)(2,1)S(1)} %get-tuple-element.195), channel_id=1, source_target_pairs={{0,16},{8,24},{16,0},{24,8},{1,17},{9,25},{17,1},{25,9},{2,18},{10... | collective-permute-start | bytes 1179656 | tf_op jit(solution)/shard_map/ppermute | solution.py:946
  124.4 22.4 %collective-permute-start.39 = (bf16[4,24,2048]{2,1,0:T(8,128)(2,1)S(1)}, bf16[4,24,2048]{2,1,0:T(8,128)(2,1)S(1)}, u32[]{:S(2)}, u32[]{:S(2)}) collective-permute-start(bf16[4,24,2048]{2,1,0:T(8,128)(2,1)S(1)} %get-tuple-element.196), channel_id=1, source_target_pairs={{0,24},{8,16},{16,8},{24,0},{1,25},{9,17},{17,9},{25,1},{2,26},{10... | collective-permute-start | bytes 1179656 | tf_op jit(solution)/shard_map/ppermute | solution.py:946
  128.1 20.6 %collective-permute-start.34 = (bf16[4,8,2816]{2,1,0:T(8,128)(2,1)S(1)}, bf16[4,8,2816]{2,1,0:T(8,128)(2,1)S(1)}, u32[]{:S(2)}, u32[]{:S(2)}) collective-permute-start(bf16[4,8,2816]{2,1,0:T(8,128)(2,1)S(1)} %get-tuple-element.187), channel_id=1, source_target_pairs={{0,8},{8,0},{16,24},{24,16},{1,9},{9,1},{17,25},{25,17},{2,10},{10... | collective-permute-start | bytes 540680 | tf_op jit(solution)/shard_map/ppermute | solution.py:946
  130.9 17.9 %collective-permute-start.35 = (bf16[4,8,2816]{2,1,0:T(8,128)(2,1)S(1)}, bf16[4,8,2816]{2,1,0:T(8,128)(2,1)S(1)}, u32[]{:S(2)}, u32[]{:S(2)}) collective-permute-start(bf16[4,8,2816]{2,1,0:T(8,128)(2,1)S(1)} %get-tuple-element.188), channel_id=1, source_target_pairs={{0,16},{8,24},{16,0},{24,8},{1,17},{9,25},{17,1},{25,9},{2,18},{10... | collective-permute-start | bytes 540680 | tf_op jit(solution)/shard_map/ppermute | solution.py:946
  134.3 17.2 %collective-permute-start.36 = (bf16[4,8,2816]{2,1,0:T(8,128)(2,1)S(1)}, bf16[4,8,2816]{2,1,0:T(8,128)(2,1)S(1)}, u32[]{:S(2)}, u32[]{:S(2)}) collective-permute-start(bf16[4,8,2816]{2,1,0:T(8,128)(2,1)S(1)} %get-tuple-element.189), channel_id=1, source_target_pairs={{0,24},{8,16},{16,8},{24,0},{1,25},{9,17},{17,9},{25,1},{2,26},{10... | collective-permute-start | bytes 540680 | tf_op jit(solution)/shard_map/ppermute | solution.py:946
  144.0 10.0 %collective-permute-start.44 = (bf16[32,2048]{1,0:T(8,128)(2,1)S(1)}, bf16[32,2048]{1,0:T(8,128)(2,1)S(1)}, u32[]{:S(2)}, u32[]{:S(2)}) collective-permute-start(bf16[32,2048]{1,0:T(8,128)(2,1)S(1)} %get-tuple-element.220), channel_id=1, source_target_pairs={{0,4},{1,5},{2,6},{3,7},{4,0},{5,1},{6,2},{7,3},{8,12},{9,13},{10,... | collective-permute-start | bytes 393224 | tf_op jit(solution)/shard_map/ppermute | solution.py:952
  146.8 10.5 %collective-permute-start.45 = (bf16[32,2048]{1,0:T(8,128)(2,1)S(1)}, bf16[32,2048]{1,0:T(8,128)(2,1)S(1)}, u32[]{:S(2)}, u32[]{:S(2)}) collective-permute-start(bf16[32,2048]{1,0:T(8,128)(2,1)S(1)} %get-tuple-element.221), channel_id=1, source_target_pairs={{0,6},{1,7},{2,4},{3,5},{4,2},{5,3},{6,0},{7,1},{8,14},{9,15},{10,... | collective-permute-start | bytes 393224 | tf_op jit(solution)/shard_map/ppermute | solution.py:952
  148.7 15.3 %collective-permute-start.46 = (bf16[24,2048]{1,0:T(8,128)(2,1)S(1)}, bf16[24,2048]{1,0:T(8,128)(2,1)S(1)}, u32[]{:S(2)}, u32[]{:S(2)}) collective-permute-start(bf16[24,2048]{1,0:T(8,128)(2,1)S(1)} %get-tuple-element.222), channel_id=1, source_target_pairs={{0,2},{1,3},{2,0},{3,1},{4,6},{5,7},{6,4},{7,5},{8,10},{9,11},{10,... | collective-permute-start | bytes 294920 | tf_op jit(solution)/shard_map/ppermute | solution.py:952
  148.8 24.6 %collective-permute-start.47 = (bf16[24,2048]{1,0:T(8,128)(2,1)S(1)}, bf16[24,2048]{1,0:T(8,128)(2,1)S(1)}, u32[]{:S(2)}, u32[]{:S(2)}) collective-permute-start(bf16[24,2048]{1,0:T(8,128)(2,1)S(1)} %get-tuple-element.223), channel_id=1, source_target_pairs={{0,4},{1,5},{2,6},{3,7},{4,0},{5,1},{6,2},{7,3},{8,12},{9,13},{10,... | collective-permute-start | bytes 294920 | tf_op jit(solution)/shard_map/ppermute | solution.py:952
  151.5 21.9 %collective-permute-start.48 = (bf16[24,2048]{1,0:T(8,128)(2,1)S(1)}, bf16[24,2048]{1,0:T(8,128)(2,1)S(1)}, u32[]{:S(2)}, u32[]{:S(2)}) collective-permute-start(bf16[24,2048]{1,0:T(8,128)(2,1)S(1)} %get-tuple-element.224), channel_id=1, source_target_pairs={{0,6},{1,7},{2,4},{3,5},{4,2},{5,3},{6,0},{7,1},{8,14},{9,15},{10,... | collective-permute-start | bytes 294920 | tf_op jit(solution)/shard_map/ppermute | solution.py:952
  154.0 20.2 %collective-permute-start.40 = (bf16[8,2816]{1,0:T(8,128)(2,1)S(1)}, bf16[8,2816]{1,0:T(8,128)(2,1)S(1)}, u32[]{:S(2)}, u32[]{:S(2)}) collective-permute-start(bf16[8,2816]{1,0:T(8,128)(2,1)S(1)} %get-tuple-element.207), channel_id=1, source_target_pairs={{0,2},{1,3},{2,0},{3,1},{4,6},{5,7},{6,4},{7,5},{8,10},{9,11},{10,... | collective-permute-start | bytes 135176 | tf_op jit(solution)/shard_map/ppermute | solution.py:952
  157.3 16.9 %collective-permute-start.41 = (bf16[8,2816]{1,0:T(8,128)(2,1)S(1)}, bf16[8,2816]{1,0:T(8,128)(2,1)S(1)}, u32[]{:S(2)}, u32[]{:S(2)}) collective-permute-start(bf16[8,2816]{1,0:T(8,128)(2,1)S(1)} %get-tuple-element.208), channel_id=1, source_target_pairs={{0,4},{1,5},{2,6},{3,7},{4,0},{5,1},{6,2},{7,3},{8,12},{9,13},{10,... | collective-permute-start | bytes 135176 | tf_op jit(solution)/shard_map/ppermute | solution.py:952
  164.0 10.2 %collective-permute-start.42 = (bf16[8,2816]{1,0:T(8,128)(2,1)S(1)}, bf16[8,2816]{1,0:T(8,128)(2,1)S(1)}, u32[]{:S(2)}, u32[]{:S(2)}) collective-permute-start(bf16[8,2816]{1,0:T(8,128)(2,1)S(1)} %get-tuple-element.209), channel_id=1, source_target_pairs={{0,6},{1,7},{2,4},{3,5},{4,2},{5,3},{6,0},{7,1},{8,14},{9,15},{10,... | collective-permute-start | bytes 135176 | tf_op jit(solution)/shard_map/ppermute | solution.py:952
  (40 other events, 312.8 us)

commit v3 on v2

--- a/solution.py
+++ b/solution.py
@@ -144,8 +144,13 @@
     out_ref[...] = own.astype(bf16).astype(f32)
 
 
-def head_kernel(pooled_ref, head_ref, bias_ref, grad_ref, logits_ref, bias_grad_ref):
-    logits_ref[...] = dot_t(pooled_ref[...], head_ref[...]) + bias_ref[...]
+def head_kernel(pooled_ref, head_ref, grad_ref, logits_ref, bias_grad_ref):
+    terms = sum(dot_t(part, head_ref[...]) for part in split(pooled_ref[...], 3))
+    clips, classes = terms.shape
+    wide = logits_ref.shape[1] // 2
+    logits_ref[...] = jnp.zeros_like(logits_ref)
+    for k in range(clips):
+        logits_ref[pl.ds(k // 2, 1), pl.ds(k % 2 * wide, classes)] = terms[k : k + 1]
     bias_grad_ref[...] = jnp.sum(grad_ref[...], axis=0, keepdims=True)
 
 
@@ -344,7 +349,8 @@
     width, cells, count, counts_ref, *refs
 ):
     moments, refs = refs[:count], refs[count:]
-    (sum_ref, skip_ref, gain_ref, shift_ref, pooled_grad_ref, stats_ref, back_ref, pre_ref, skip_grad_ref) = refs
+    (sum_ref, skip_ref, gain_ref, shift_ref, pooled_grad_ref, stats_ref, back_ref, pooled_ref, pre_ref,
+     skip_grad_ref) = refs
     center, scale = norm_stats(moments, cell_total(counts_ref, True, cells))
     stats_ref[0:1] = center
     stats_ref[1:2] = scale
@@ -357,7 +363,7 @@
         mask = frame_mask(counts_ref, k, 0)
         pool = ((counts_ref[k] + 1) // 2 * cells).astype(f32)
         pooled = jnp.sum(jnp.where(keep, post, 0.0), axis=0, keepdims=True) * mask / pool
-        back_ref[pl.ds(2 + k, 1)] = pooled
+        pooled_ref[pl.ds(k, 1)] = pooled
         pre = jnp.where(keep, pooled_grad_ref[pl.ds(k, 1)] * mask / pool * slope, 0.0)
         pre_ref[k] = pre
         skip_grad_ref[k] = pre.astype(bf16)
@@ -371,10 +377,8 @@
     width, cells, count, counts_ref, *refs
 ):
     received, refs = refs[:count], refs[count:]
-    (stats_ref, sum_ref, pre_ref, gain_ref, up_ref, mid_ref, sum_grad_ref, mid_grad_ref, pooled_ref) = refs
-    totals = received_sum(received)
-    pooled_ref[...] = totals[2:].astype(bf16)
-    totals = totals[0:2] / cell_total(counts_ref, True, cells)
+    (stats_ref, sum_ref, pre_ref, gain_ref, up_ref, mid_ref, sum_grad_ref, mid_grad_ref) = refs
+    totals = received_sum(received) / cell_total(counts_ref, True, cells)
     center, scale = stats_ref[0:1], stats_ref[1:2]
     lead = gain_ref[...] * scale
     clips, rows, channels = sum_ref.shape
@@ -390,7 +394,7 @@
 
 
 def late_back_kernel(
-    width, counts_ref, rz_ref, own_ref, rc_ref, taps_ref, first_ref, down_ref, skip_back_ref, hat_ref,
+    width, counts_ref, rz_ref, own_ref, rc_ref, taps_ref, first_ref, down_ref, skip_back_ref, hat_ref, logits_ref,
     first_grad_ref, entry_grad_ref, back_ref, frames, grads,
 ):
     clips, rows, channels = own_ref.shape
@@ -427,6 +431,7 @@
         one, two = (a, b) if one is None else (one + a, two + b)
     back_ref[0:1] = jnp.sum(one, axis=0, keepdims=True)
     back_ref[1:2] = jnp.sum(two, axis=0, keepdims=True)
+    back_ref[2:] = logits_ref[...]
 
 
 def tap_grads(load, grad_of, steps, rows):
@@ -521,17 +526,16 @@
         own, own_third, own_taps = late_wide // parts, wide // parts, taps_ref.shape[0] // parts
         deep = channels // parts
         clip, space = lax.axis_index("clip"), lax.axis_index("space")
-        clips = pooled_ref.shape[0]
-        pooled = pooled_ref[...].astype(f32)
+        pooled = pooled_ref[...]
         pooled = jnp.concatenate(
-            [jnp.where((clip == g) & (space == 0), pooled, 0.0) for g in range(lax.axis_size("clip"))], axis=0
+            [jnp.where(clip == g, pooled, 0.0) for g in range(lax.axis_size("clip"))], axis=0
         )
         for d in range(parts):
             at, third_at = d * own // lanes * lanes, d * own_third // lanes * lanes
             block = jnp.concatenate(
                 [
                     back_ref[0:2, pl.ds(at, lanes)],
-                    third_ref[:, pl.ds(third_at, lanes)],
+                    third_ref[0:2, pl.ds(third_at, lanes)],
                     jnp.zeros((4, lanes), f32),
                     pooled[:, at : at + lanes],
                     taps_ref[pl.ds(d * own_taps, own_taps), :],
@@ -558,8 +562,8 @@
     width, cells, count, counts_ref, *refs
 ):
     received, refs = refs[:count], refs[count:]
-    (stats_ref, gain_ref, entry_grad_ref, up_ref, act_even_ref, act_sum_ref, gram_up_ref, act_ref, mid_ref,
-     gz_ref, gc_ref, terms_ref, back_even, mix, shift, placed) = refs
+    (stats_ref, gain_ref, entry_grad_ref, up_ref, act_even_ref, act_sum_ref, gram_up_ref, bias_ref, act_ref, mid_ref,
+     gz_ref, gc_ref, terms_ref, logits_ref, back_even, mix, shift, placed) = refs
     k = pl.program_id(0)
     rows = act_ref.shape[2]
     pitch = 16
@@ -569,7 +573,13 @@
     @pl.when(k == 0)
     def _():
         placed[...] = jnp.zeros_like(placed)
-        totals = received_sum(received) / cell_total(counts_ref, False, cells)
+        totals = received_sum(received)
+        clips, classes = logits_ref.shape
+        wide = totals.shape[1] // 2
+        for i in range(clips):
+            row = totals[2 + i // 2 : 3 + i // 2, i % 2 * wide : i % 2 * wide + classes]
+            logits_ref[pl.ds(i, 1)] = row + bias_ref[...]
+        totals = totals[0:2] / cell_total(counts_ref, False, cells)
         center, scale = stats_ref[0:1], stats_ref[1:2]
         lead = gain_ref[...] * scale
         slope = -(lead * scale * totals[1:2])
@@ -749,7 +759,7 @@
 kernel_micros = {
     "first": 5.3, "mid_own": 5.0, "mid": 8.6, "entry": 3.4, "late_mid": 4.7, "post": 6.0, "skip_sums": 7.0,
     "sum_grad": 4.6, "late_taps": 3.6, "late_back": 5.0, "up_down_sums": 5.5, "third_grad": 6.7, "third_taps": 7.7,
-    "up_down_total": 2.3, "skip_total": 3.0, "finish": 2.0, "terms": 1.5, "taps": 0.6, "pooled_grad": 1.5, "head": 1.0, "add": 0.6, "skipped": 2.5, "first_grad": 10.7, "pair_sum": 1.9, "clip_sum": 1.6, "clip_grad": 5.5,
+    "up_down_total": 2.3, "skip_total": 3.0, "skip_phase": 1.0, "up_down_phase": 1.0, "finish": 2.0, "terms": 1.5, "taps": 0.6, "pooled_grad": 1.5, "head": 1.0, "add": 0.6, "skipped": 2.5, "first_grad": 10.7, "pair_sum": 1.9, "clip_sum": 1.6, "clip_grad": 5.5,
 }
 smem = pl.BlockSpec(memory_space=pltpu.SMEM)
 
@@ -838,11 +848,51 @@
     return [((clip ^ b) * chips + z) * 2 + (space & 1) for b in range(clips) for z in range(chips)]
 
 
+def place(outs, chips, j, values):
+    b, z = j // chips, j % chips
+    if z < chips // 2:
+        outs[b % 2][b // 2, z] = values.astype(bf16)
+    else:
+        outs[2 + b // 2][b % 2, z - chips // 2] = values.astype(bf16)
+
+
+def first_phase(pieces):
+    keep_low, send_low, keep_high, send_high = pieces
+    return [keep_low, clip_swap(send_low, 1), keep_high, clip_swap(send_high, 2)]
+
+
+def clip_swap(values, bit):
+    return lax.ppermute(values, "clip", [(i, i ^ bit) for i in range(lax.axis_size("clip"))])
+
+
+def phase_kernel(keep_low_ref, got_low_ref, keep_high_ref, got_high_ref, low_ref, low_send_ref, high_ref, high_send_ref):
+    for keep, got, out, send in (
+        (keep_low_ref, got_low_ref, low_ref, low_send_ref), (keep_high_ref, got_high_ref, high_ref, high_send_ref)
+    ):
+        out[...] = (keep[0].astype(f32) + got[0].astype(f32)).astype(bf16)
+        send[...] = (keep[1].astype(f32) + got[1].astype(f32)).astype(bf16)
+
+
+def second_phase(name, pieces):
+    shape = pieces[0].shape[1:]
+    low, low_send, high, high_send = call(phase_kernel, name, w(pieces), [(shape, bf16, "w")] * 4, [])
+    return [low, clip_swap(low_send, 2), high, clip_swap(high_send, 1)]
+
+
+def halves_total_kernel(low_ref, got_low_ref, high_ref, got_high_ref, *outs):
+    half = low_ref.shape[0]
+    for z, out_ref in enumerate(outs):
+        at = (lax.axis_index("space") // 2) ^ z
+        low = low_ref[at % half].astype(f32) + got_low_ref[at % half].astype(f32)
+        high = high_ref[at % half].astype(f32) + got_high_ref[at % half].astype(f32)
+        out_ref[...] = jnp.where(at < half, low, high).astype(bf16)
+
+
 def skip_kernel(
     orders, left_ref, left_other_ref, right_ref, right_other_ref, weight_ref, back_ref, *refs
 ):
     clips, chips = orders
-    outs, (left, left_other) = refs[:clips], refs[clips:]
+    outs, (left, left_other) = refs[:4], refs[4:]
 
     @pl.when(pl.program_id(0) == 0)
     def _():
@@ -854,7 +904,7 @@
     total = dot(left[1, pl.ds(0, half)], right_ref[...]) + dot(left_other[1, pl.ds(0, half)], right_other_ref[...])
     block = half // (clips * chips)
     for j in range(clips * chips):
-        outs[j // chips][j % chips] = total[j * block : (j + 1) * block].astype(bf16)
+        place(outs, chips, j, total[j * block : (j + 1) * block])
     back_ref[...] += dot_t(right_ref[...], weight_ref[...])
 
 
@@ -869,14 +919,14 @@
         grid=(wide // lanes,),
         out_shape=[
             jax.ShapeDtypeStruct((rows, deep), f32),
-            *[jax.ShapeDtypeStruct((orders[1], block, wide), bf16)] * orders[0],
+            *[jax.ShapeDtypeStruct((2, orders[1] // 2, block, wide), bf16)] * 4,
         ],
         in_specs=[pl.BlockSpec((rows, deep), lambda n: (0, 0))] * 2
         + [pl.BlockSpec((rows, lanes), lambda n: (0, n))] * 2
         + [pl.BlockSpec((deep, lanes), lambda n: (0, n))],
         out_specs=[
             pl.BlockSpec((rows, deep), lambda n: (0, 0)),
-            *[pl.BlockSpec((orders[1], block, lanes), lambda n: (0, 0, n))] * orders[0],
+            *[pl.BlockSpec((2, orders[1] // 2, block, lanes), lambda n: (0, 0, 0, n))] * 4,
         ],
         scratch_shapes=[pltpu.VMEM((2, deep, rows), bf16)] * 2,
         compiler_params=pltpu.CompilerParams(vmem_limit_bytes=LIMIT * mib),
@@ -889,7 +939,7 @@
     *refs
 ):
     clips, chips = orders
-    outs, (act, act_other, entry, entry_other, down) = refs[:clips], refs[clips:]
+    outs, (act, act_other, entry, entry_other, down) = refs[:4], refs[4:]
     n = pl.program_id(0)
 
     @pl.when(n == 0)
@@ -907,12 +957,10 @@
     half = act.shape[1] // 2
     up = dot(act[1, pl.ds(0, half)], sum_ref[...]) + dot(act_other[1, pl.ds(0, half)], sum_other_ref[...])
     block = half // (clips * chips)
-    part = outs[0].shape[1] - block
-    for b in range(clips):
-        for z in range(chips):
-            j = b * chips + z
-            under = down[j, pl.ds(pl.multiple_of(n * part, part), part), :]
-            outs[b][z] = jnp.concatenate([up[j * block : (j + 1) * block], under], axis=0).astype(bf16)
+    part = outs[0].shape[2] - block
+    for j in range(clips * chips):
+        under = down[j, pl.ds(pl.multiple_of(n * part, part), part), :]
+        place(outs, chips, j, jnp.concatenate([up[j * block : (j + 1) * block], under], axis=0))
 
 
 def up_down_sums(act, act_other, entry, entry_other, first, first_other, sums, sums_other, parts, orders):
@@ -927,12 +975,12 @@
         functools.partial(products_kernel, orders),
         name="up_down_sums",
         grid=(wide // lanes,),
-        out_shape=[jax.ShapeDtypeStruct((chips, block, wide), bf16)] * clips,
+        out_shape=[jax.ShapeDtypeStruct((2, chips // 2, block, wide), bf16)] * 4,
         in_specs=[pl.BlockSpec((rows, inner), same)] * 2
         + [pl.BlockSpec((rows, deep), same)] * 2
         + [pl.BlockSpec((rows, inner), same)] * 2
         + [pl.BlockSpec((rows, lanes), lambda n: (0, n))] * 2,
-        out_specs=[pl.BlockSpec((chips, block, lanes), lambda n: (0, 0, n))] * clips,
+        out_specs=[pl.BlockSpec((2, chips // 2, block, lanes), lambda n: (0, 0, 0, n))] * 4,
         scratch_shapes=[pltpu.VMEM((2, inner, rows), bf16)] * 2
         + [pltpu.VMEM((2, deep, rows), bf16)] * 2
         + [pltpu.VMEM((clips * chips, down_block, inner), f32)],
@@ -1076,43 +1124,48 @@
     )
     late_sum = late_sum.reshape(clips, late_rows, late_wide)
     late_moments = group_parts(late_moments)
-    late_stats, late_back, pre_grad, skip_grad = call(
+    late_stats, late_back, pooled, pre_grad, skip_grad = call(
         functools.partial(post_kernel, half_width, late_cells, len(late_moments)), "post",
         [(frame_counts, "s"), *w(late_moments), (late_sum, "w"), (skipped, "w"),
          (fourth_gain, "w"), (fourth_shift, "w"), (pooled_grad, "w")],
         [
             ((2, late_wide), f32, "w"),
-            ((2 + clips, late_wide), f32, "w"),
+            ((2, late_wide), f32, "w"),
+            ((clips, late_wide), f32, "w"),
             ((clips, late_rows, late_wide), f32, "w"),
             ((clips, late_rows, late_wide), bf16, "w"),
         ],
         [],
     )
     received = group_parts(late_back)
+    logit_terms, bias_grad = call(
+        head_kernel, "head", w([after(pooled, received[0]), head, logit_grad]),
+        [((clips // 2, channels), f32, "w"), ((1, logit_grad.shape[1]), f32, "w")], [],
+    )
+    late_stats = after(late_stats, logit_terms)
     skip_rows = skip_grad.reshape(late_all, late_wide)
     if by_pairs:
         entry_other = core_swap(entry)
         skip_back, *skip_pieces = skip_sums(
-            entry, entry_other, skip_rows, core_swap(skip_rows), fourth_skip, parts, (clip_axis, chips)
+            entry, entry_other, skip_rows, core_swap(after(skip_rows, received[0])), fourth_skip, parts, (clip_axis, chips)
         )
     else:
         skip_back = dot_t(skip_rows, fourth_skip)
         fourth_skip_grad = reduce_rows(t_dot(entry, skip_rows))
     late_stats = after(late_stats, skip_back)
-    late_sum_grad, late_mid_grad, pooled = call(
+    late_sum_grad, late_mid_grad = call(
         functools.partial(sum_grad_kernel, half_width, late_cells, len(received)), "sum_grad",
         [(frame_counts, "s"), *w(received), (late_stats, "w"), (late_sum, "w"), (pre_grad, "w"),
          (fourth_gain, "w"), (fourth_up, "w"), (late_mid, "w")],
         [
             ((late_all, late_wide), bf16, "w"),
             ((clips, late_rows, late_inner), bf16, "w"),
-            ((clips, late_wide), bf16, "w"),
         ],
         [],
     )
     late_gz, late_gc = swap_neighbours(late_mid_grad, late_mid_grad)
     if by_pairs:
-        skip_pieces = over_clip(after(skip_pieces, late_mid_grad))
+        skip_pieces = first_phase(after(skip_pieces, late_mid_grad))
     (late_taps_table,) = call(
         late_taps_kernel, "late_taps",
         [(late_z, "w"), (late_act, "w"), (late_c, "w"), (late_mid_grad, "w")],
@@ -1123,11 +1176,11 @@
     late_first_grad, entry_grad, third_back = call(
         functools.partial(late_back_kernel, half_width), "late_back",
         [(frame_counts, "s"), (late_gz, "w"), (late_mid_grad, "w"), (late_gc, "w"), (late_taps, "w"),
-         (late_first, "w"), (fourth_down, "w"), (skip_back, "w"), (even_hat, "w")],
+         (late_first, "w"), (fourth_down, "w"), (skip_back, "w"), (even_hat, "w"), (logit_terms, "w")],
         [
             ((late_all, late_inner), bf16, "w"),
             ((clips, late_rows, channels), f32, "w"),
-            ((2, channels), f32, "w"),
+            ((2 + clips // 2, channels), f32, "w"),
         ],
         [
             pltpu.VMEM((3, late_rows + 16, late_inner), f32),
@@ -1140,24 +1193,21 @@
             late_mid_act, core_swap(late_mid_act), entry, entry_other, late_first_grad, core_swap(late_first_grad),
             late_sum_grad, core_swap(late_sum_grad), parts, (clip_axis, chips),
         )
-        skip_pieces = call(
-            functools.partial(chip_totals_kernel, clip_axis), "skip_total",
-            [(part, "w") for part in after(skip_pieces, up_pieces[0])],
-            [(skip_pieces[0].shape[1:], bf16, "w")] * chips, [],
-        )
+        skip_pieces = second_phase("skip_phase", after(skip_pieces, up_pieces[0]))
         stats = after(stats, skip_pieces[0])
     else:
         fourth_up_grad = reduce_rows(t_dot(late_mid_act, late_sum_grad))
         fourth_down_grad = reduce_rows(t_dot(entry, late_first_grad))
-    grad_z, grad_c, up_terms = call(
+    grad_z, grad_c, up_terms, logits = call(
         functools.partial(third_grad_kernel, width, cells, len(received)), "third_grad",
         [(frame_counts, "s"), *w(received), (stats, "w"), (third_gain, "w"),
          (entry_grad.reshape(late_all, channels), "w"), (third_up, "w"), (act_even, "w"), (act_sum, "w"),
-         (gram_up, "w"), (mid_act, "c"), (mid, "c")],
+         (gram_up, "w"), (class_bias[None], "w"), (mid_act, "c"), (mid, "c")],
         [
             ((clips, rows, inner), bf16, "c"),
             ((clips, rows, inner), bf16, "c"),
             ((inner, channels), bf16, "w"),
+            ((clips, logit_grad.shape[1]), f32, "w"),
         ],
         [
             pltpu.VMEM((late_all, inner), f32),
@@ -1193,7 +1243,12 @@
     )
     first = after(first, third_terms[0])
     if by_pairs:
-        up_pieces = over_clip(after(up_pieces, skip_pieces[0]))
+        skip_pieces = call(
+            halves_total_kernel, "skip_total", w(after(skip_pieces, third_terms[0])),
+            [(skip_pieces[0].shape[1:], bf16, "w")] * chips, [],
+        )
+        first = after(first, skip_pieces[0])
+        up_pieces = first_phase(after(up_pieces, third_terms[0]))
         skip_pieces = over_chips(after(skip_pieces, third_terms[0]))
     block = channels // parts
     if by_pairs:
@@ -1217,9 +1272,17 @@
         ],
         clips=clips,
     )
+    (clip_grad,) = call(
+        clip_grad_kernel, "clip_grad",
+        [(first_grad, "c"), (third_down, "w"), (entry_grad, "c")],
+        [(clip_input.shape, bf16, "c")],
+        [pltpu.VMEM((channels // 128, 2 * rows, 128), f32)],
+        clips=clips,
+    )
     if by_pairs:
         keep, send = down_terms
         keep_terms, send_terms = third_terms
+        up_pieces = second_phase("up_down_phase", after(up_pieces, first_grad))
         clip_parts = call(
             pair_sum_kernel, "pair_sum",
             w([keep, core_swap(send), keep_terms, core_swap(after(send_terms, third_gz))]),
@@ -1227,13 +1290,13 @@
             [],
         )
         up_pieces = call(
-            functools.partial(chip_totals_kernel, clip_axis), "up_down_total", w(after(up_pieces, clip_parts[0])),
+            halves_total_kernel, "up_down_total", w(after(up_pieces, (clip_parts[0], skip_pieces))),
             [(up_pieces[0].shape[1:], bf16, "w")] * chips, [],
         )
         clip_parts = over_clip(clip_parts)
         up_pieces = over_chips(up_pieces)
         chip_parts = call(
-            functools.partial(chip_totals_kernel, clip_axis), "clip_sum", w(after(clip_parts, up_pieces[0])),
+            functools.partial(chip_totals_kernel, clip_axis), "clip_sum", w(after(clip_parts, (up_pieces[0], clip_grad))),
             [(clip_parts[0].shape[1:], bf16, "w")] * chips, [],
         )
         third_terms = [part[None] for part in over_chips(chip_parts)]
@@ -1250,18 +1313,6 @@
     else:
         third_down_grad = add_rows(send_rows(down_terms[0]))
         third_terms = [send_rows(third_terms[0])]
-    (clip_grad,) = call(
-        clip_grad_kernel, "clip_grad",
-        [(first_grad, "c"), (third_down, "w"), (entry_grad, "c")],
-        [(clip_input.shape, bf16, "c")],
-        [pltpu.VMEM((channels // 128, 2 * rows, 128), f32)],
-        clips=clips,
-    )
-
-    logits, bias_grad = call(
-        head_kernel, "head", w([after(pooled, first_grad), head, class_bias[None], logit_grad]),
-        [((clips, logit_grad.shape[1]), f32, "w"), ((1, logit_grad.shape[1]), f32, "w")], [],
-    )
     own, own_third, own_taps = late_wide // parts, channels // parts, late_inner // parts
     third_up_grad, third_depth_grad, gain, shift, late_gain, late_shift, fourth_depth_grad, classifier_grad, *down = call(
         functools.partial(terms_kernel, len(third_terms), clips, channels, small_rows), "terms",

time: 175 us -> 153 us (0.87)
  waiting for transfers between devices: 32.3 us -> 19.4 us
  starting transfers between devices: 76 us -> 64.6 us
    ppermute x9 -> x3, waiting for transfers between devices: 16.1 us -> 0.01 us  [over_clip(): lax.ppermute(pieces[b], 'clip', [(i, i ^ b) for i in range(size)])]
    ppermute x9 -> x3, starting transfers between devices: 11.4 us -> 2.81 us  [over_clip(): lax.ppermute(pieces[b], 'clip', [(i, i ^ b) for i in range(size)])]
    ppermute x21, starting transfers between devices: 40.2 us -> 32.2 us  [over_chips(): lax.ppermute(pieces[z], 'space', [(i, i ^ 2 * z) for i in range(2 * size)])]
    ppermute x0 -> x8, starting transfers between devices: none -> 7.43 us  [clip_swap(): lax.ppermute(values, 'clip', [(i, i ^ bit) for i in range(lax.axis_size('...]
    ppermute x21, waiting for transfers between devices: 7.88 us -> 12.9 us  [over_chips(): lax.ppermute(pieces[z], 'space', [(i, i ^ 2 * z) for i in range(2 * size)])]
    ppermute x4, starting transfers between devices: 9.75 us -> 6.33 us  [swap_neighbours(): lax.ppermute(to_core, 'space', core)]
    ppermute x11, waiting for transfers between devices: 6.79 us -> 4.74 us  [core_swap(): lax.ppermute(values, 'space', [(i, i ^ 1) for i in range(lax.axis_size('s...]
    pallas_call x26 -> x28, Pallas kernels: 49.2 us -> 50.8 us  [call(): pl.pallas_call(kernel, name=name, out_shape=[jax.ShapeDtypeStruct(s, d) f...]
  transfers between devices with their start and end apart: 49 -> 51, of which waited for: 15 -> 14; matrix products, arithmetic and copies ran while one was open for 3% -> 3% of each run, Pallas kernels for 21% -> 24%
where the time goes in v3:
time: 153 us
  starting transfers between devices  64.6 us (42%)
  Pallas kernels  59.1 us (39%)
  waiting for transfers between devices  19.4 us (13%)
  local copies, waits for them, and re-layouts  8.16 us (5%)
    pallas_call x28, Pallas kernels, call(): pl.pallas_call(kernel, name=name, out_shape=[jax.ShapeDtypeStruct(s, d) f...  50.8 us
    ppermute x21, starting transfers between devices, over_chips(): lax.ppermute(pieces[z], 'space', [(i, i ^ 2 * z) for i in range(2 * size)])  32.2 us
    ppermute x21, waiting for transfers between devices, over_chips(): lax.ppermute(pieces[z], 'space', [(i, i ^ 2 * z) for i in range(2 * size)])  12.9 us
    ppermute x11, starting transfers between devices, core_swap(): lax.ppermute(values, 'space', [(i, i ^ 1) for i in range(lax.axis_size('s...  12.6 us
    unnamed x32, local copies, waits for them, and re-layouts  8.16 us
    ppermute x8, starting transfers between devices, clip_swap(): lax.ppermute(values, 'clip', [(i, i ^ bit) for i in range(lax.axis_size('...  7.43 us
    ppermute x4, starting transfers between devices, swap_neighbours(): lax.ppermute(to_core, 'space', core)  6.33 us
    ppermute x11, waiting for transfers between devices, core_swap(): lax.ppermute(values, 'space', [(i, i ^ 1) for i in range(lax.axis_size('s...  4.74 us
  transfers between devices with their start and end apart: 51, of which 14 were waited for; matrix products, arithmetic and copies ran while one was open for 3% of the time, Pallas kernels for 24%

profile of v3, /device:TPU:0, one launch (start us, length us, event | category | flops | bytes accessed | tf_op | source)
XLA Modules:
  0.0 152.5 jit_solution(7339492323261050165)
XLA Ops:
  0.7 3.0 %copy.31.x_ref = bf16[4,2,14,14,1024]{4,3,2,1,0:T(8,128)(2,1)S(1)} copy(bf16[4,2,14,14,1024]{4,1,3,2,0:T(2,128)(2,1)} %param.16) | data formatting | bytes 6422528 | tf_op args[0]
  3.8 3.0 %first.1 = (f32[4,2,224,256]{3,2,1,0:T(8,128)S(1)}, bf16[4,224,256]{2,1,0:T(8,128)(2,1)S(1)}, bf16[4,224,256]{2,1,0:T(8,128)(2,1)S(1)}, f32[4,56,1024]{2,1,0:T(8,128)S(1)}) custom-call(s32[4]{0:T(128)S(1)} %copy-done.8, bf16[4,2,14,14,1024]{4,3,2,1,0:T(8,128)(2,1)S(1)} %copy.31.x_ref, bf16[1024,256]{1,0:T(8,128)(2,1)S(1)} %copy-done.4), custom_call_target="tpu_custom_call" | custom-call | bytes 18020000 | tf_op jit(solution)/shard_map/first/pallas_call | solution.py:787
  7.6 4.4 %collective-permute-start.1 = (bf16[4,224,256]{2,1,0:T(8,128)(2,1)S(1)}, bf16[4,224,256]{2,1,0:T(8,128)(2,1)S(1)}, u32[]{:S(2)}, u32[]{:S(2)}) collective-permute-start(bf16[4,224,256]{2,1,0:T(8,128)(2,1)S(1)} %get-tuple-element.145.oc_ref), channel_id=1, source_target_pairs={{0,1},{1,0},{2,3},{3,2},{4,5},{5,4},{6,7},{7,6},{8,9},{9,8},{10,11... | collective-permute-start | bytes 1376264 | tf_op jit(solution)/shard_map/ppermute | solution.py:817
  12.0 3.0 %mid_own.1.part_ref = f32[4,2,224,256]{3,2,1,0:T(8,128)S(1)} custom-call(bf16[4,224,256]{2,1,0:T(8,128)(2,1)S(1)} %get-tuple-element.144.oz_ref, bf16[4,224,256]{2,1,0:T(8,128)(2,1)S(1)} %get-tuple-element.145.oc_ref, f32[27,256]{1,0:T(8,128)S(1)} %get-tuple-element.146.taps_ref), custom_call_target="tpu_custom_call" | custom-call | bytes 17000000 | tf_op jit(solution)/shard_map/mid_own/pallas_call | solution.py:787
  15.1 6.1 %mid.1 = (f32[4,2,224,256]{3,2,1,0:T(8,128)S(1)}, bf16[4,2,224,256]{3,2,1,0:T(8,128)(2,1)S(1)}, bf16[224,256]{1,0:T(8,128)(2,1)S(1)}, f32[224,1024]{1,0:T(8,128)...) custom-call(s32[4]{0:T(128)S(1)} %copy-done.8, ...), custom_call_target="tpu_custom_call" | custom-call | bytes 29240000 | tf_op jit(solution)/shard_map/mid/pallas_call | solution.py:787
  21.3 3.0 %collective-permute-start.2 = (f32[2,1024]{1,0:T(2,128)S(1)}, f32[2,1024]{1,0:T(2,128)S(1)}, u32[]{:S(2)}, u32[]{:S(2)}) collective-permute-start(f32[2,1024]{1,0:T(2,128)S(1)} %get-tuple-element.147.one_ref), channel_id=1, source_target_pairs={{0,1},{1,0},{2,3},{3,2},{4,5},{5,4},{6,7},{7,6},{8,9},{9,8},{10,11... | collective-permute-start | bytes 24584 | tf_op jit(solution)/shard_map/ppermute | solution.py:835
  27.1 2.6 %collective-permute-start.4 = (f32[2,1024]{1,0:T(2,128)S(1)}, f32[2,1024]{1,0:T(2,128)S(1)}, u32[]{:S(2)}, u32[]{:S(2)}) collective-permute-start(f32[2,1024]{1,0:T(2,128)S(1)} %add.4), channel_id=1, source_target_pairs={{0,4},{1,5},{2,6},{3,7},{4,0},{5,1},{6,2},{7,3},{8,12},{9,13},{10,... | collective-permute-start | bytes 24584 | tf_op jit(solution)/shard_map/ppermute | solution.py:1000
  31.7 3.5 %collective-permute-done.5 = f32[2,1024]{1,0:T(2,128)S(1)} collective-permute-done((f32[2,1024]{1,0:T(2,128)S(1)}, f32[2,1024]{1,0:T(2,128)S(1)}, u32[]{:S(2)}, u32[]{:S(2)}) %collective-permute-start.5) | collective-permute-done | bytes 8224 | tf_op jit(solution)/shard_map/ppermute | solution.py:1000
  38.7 2.4 %late_mid.1 = (f32[4,56,512]{2,1,0:T(8,128)S(1)}, bf16[224,512]{1,0:T(8,128)(2,1)S(1)}, bf16[224,2048]{1,0:T(8,128)(2,1)S(1)}, f32[2,2048]{1,0:T(2,128)S(1)}) custom-call(s32[4]{0:T(128)S(1)} %copy-done.8, bf16[4,56,512]{2,1,0:T(8,128)(2,1)S(1)} %collective-permute-done.6.rz_ref, bf16[4,56,512]{2,1,0:T(8,128)(2,1)S(1)} %get-tuple-element.150.own_ref, ...), custom_call_target="tpu_custom_call" | custom-call | bytes 15980000 | tf_op jit(solution)/shard_map/late_mid/pallas_call | solution.py:787
  41.1 3.5 %collective-permute-start.8 = (f32[2,2048]{1,0:T(2,128)S(1)}, f32[2,2048]{1,0:T(2,128)S(1)}, u32[]{:S(2)}, u32[]{:S(2)}) collective-permute-start(f32[2,2048]{1,0:T(2,128)S(1)} %get-tuple-element.152.one_ref), channel_id=1, source_target_pairs={{0,1},{1,0},{2,3},{3,2},{4,5},{5,4},{6,7},{7,6},{8,9},{9,8},{10,11... | collective-permute-start | bytes 49160 | tf_op jit(solution)/shard_map/ppermute | solution.py:835
  53.5 2.9 %post.1 = (f32[2,2048]{1,0:T(2,128)S(1)}, f32[2,2048]{1,0:T(2,128)S(1)}, f32[4,2048]{1,0:T(4,128)S(1)}, f32[4,56,2048]{2,1,0:T(8,128)S(1)}, bf16[4,56,2048]{2,1,0:T(8,128)(2,1)S(1)}) custom-call(s32[4]{0:T(128)S(1)} %copy-done.8, f32[1,2,2048]{2,1,0:T(2,128)S(1)} %bitcast.51, f32[1,2,2048]{2,1,0:T(2,128)S(1)} %bitcast.67, f32[1,2,2048]{2,1,0:T(2,128)S(1)} %bitcast.68, ...), custom_call_target="tpu_custom_call" | custom-call | bytes 20400000 | tf_op jit(solution)/shard_map/post/pallas_call | solution.py:787
  58.2 2.4 %collective-permute-start.14 = (f32[2,2048]{1,0:T(2,128)S(1)}, f32[2,2048]{1,0:T(2,128)S(1)}, u32[]{:S(2)}, u32[]{:S(2)}) collective-permute-start(f32[2,2048]{1,0:T(2,128)S(1)} %add.6), channel_id=1, source_target_pairs={{0,4},{1,5},{2,6},{3,7},{4,0},{5,1},{6,2},{7,3},{8,12},{9,13},{10,... | collective-permute-start | bytes 49160 | tf_op jit(solution)/shard_map/ppermute | solution.py:1000
  64.4 4.1 %skip_sums.1 = (f32[224,1024]{1,0:T(8,128)S(1)}, bf16[2,2,32,2048]{3,2,1,0:T(8,128)(2,1)S(1)}, bf16[2,2,32,2048]{3,2,1,0:T(8,128)(2,1)S(1)}, bf16[2,2,32,2048]{3...) custom-call(bf16[224,1024]{1,0:T(8,128)(2,1)S(1)} %get-tuple-element.154.entry_ref.left_ref, ...), custom_call_target="tpu_custom_call" | custom-call | bytes 23800000 | tf_op jit(solution)/shard_map/skip_sums/pallas_call | solution.py:916
  77.1 2.3 %late_back.1 = (bf16[224,512]{1,0:T(8,128)(2,1)S(1)}, f32[4,56,1024]{2,1,0:T(8,128)S(1)}, f32[4,1024]{1,0:T(4,128)S(1)}) custom-call(s32[4]{0:T(128)S(1)} %copy-done.8, bf16[4,56,512]{2,1,0:T(8,128)(2,1)S(1)} %collective-permute-done.18.rz_ref, bf16[4,56,512]{2,1,0:T(8,128)(2,1)S(1)} %get-tuple-element.167.grad_ref.own_ref, ...), custom_call_target="tpu_custom_call" | custom-call | bytes 17000000 | tf_op jit(solution)/shard_map/late_back/pallas_call | solution.py:787
  79.4 3.8 %collective-permute-start.20 = (f32[4,1024]{1,0:T(4,128)S(1)}, f32[4,1024]{1,0:T(4,128)S(1)}, u32[]{:S(2)}, u32[]{:S(2)}) collective-permute-start(f32[4,1024]{1,0:T(4,128)S(1)} %get-tuple-element.171.one_ref.third_ref), channel_id=1, source_target_pairs={{0,1},{1,0},{2,3},{3,2},{4,5},{5,4},{6,7},{7,6},{8,9},{9,8},{10,11... | collective-permute-start | bytes 49160 | tf_op jit(solution)/shard_map/ppermute | solution.py:835
  92.7 4.0 %third_grad.1 = (bf16[4,224,256]{2,1,0:T(8,128)(2,1)S(1)}, bf16[4,224,256]{2,1,0:T(8,128)(2,1)S(1)}, bf16[256,1024]{1,0:T(8,128)(2,1)S(1)}, f32[4,400]{1,0:T(4,128)}) custom-call(s32[4]{0:T(128)S(1)} %copy-done.8, f32[1,4,1024]{2,1,0:T(4,128)S(1)} %bitcast.49, f32[1,4,1024]{2,1,0:T(4,128)S(1)} %bitcast.61, f32[1,4,1024]{2,1,0:T(4,128)S(1)} %bitcast.62, ...), custom_call_target="tpu_custom_call" | custom-call | bytes 22780000 | tf_op jit(solution)/shard_map/third_grad/pallas_call | solution.py:787
  99.0 5.3 %third_taps.1 = (f32[4,4,8,1792]{3,2,1,0:T(8,128)S(1)}, bf16[4,4,8,1792]{3,2,1,0:T(8,128)(2,1)S(1)}) custom-call(bf16[4,224,256]{2,1,0:T(8,128)(2,1)S(1)} %collective-permute-done.rz_ref, bf16[4,224,256]{2,1,0:T(8,128)(2,1)S(1)} %get-tuple-element.144.oz_ref, bf16[4,224,256]{2,1,0:T(8,128)(2,1)S(1)} %get-tuple-element.145.oc_ref, ...), custom_call_target="tpu_custom_call" | custom-call | bytes 26180000 | tf_op jit(solution)/shard_map/third_taps/pallas_call | solution.py:787
  107.8 9.1 %first_grad.1 = (bf16[4,448,256]{2,1,0:T(8,128)(2,1)S(1)}, f32[4,4,32,256]{3,2,1,0:T(8,128)S(1)}, bf16[4,4,32,256]{3,2,1,0:T(8,128)(2,1)S(1)}) custom-call(s32[4]{0:T(128)S(1)} %copy-done.8, bf16[4,224,256]{2,1,0:T(8,128)(2,1)S(1)} %collective-permute-done.29.rz_ref, bf16[4,224,256]{2,1,0:T(8,128)(2,1)S(1)} %get-tuple-element.198.gz_ref, ...), custom_call_target="tpu_custom_call" | custom-call | bytes 36380000 | tf_op jit(solution)/shard_map/first_grad/pallas_call | solution.py:787
  118.0 2.4 %collective-permute-start.43 = (bf16[32,2048]{1,0:T(8,128)(2,1)S(1)}, bf16[32,2048]{1,0:T(8,128)(2,1)S(1)}, u32[]{:S(2)}, u32[]{:S(2)}) collective-permute-start(bf16[32,2048]{1,0:T(8,128)(2,1)S(1)} %get-tuple-element.242), channel_id=1, source_target_pairs={{0,4},{1,5},{2,6},{3,7},{4,0},{5,1},{6,2},{7,3},{8,12},{9,13},{10,... | collective-permute-start | bytes 393224 | tf_op jit(solution)/shard_map/ppermute | solution.py:1000
  127.7 3.7 %collective-permute-done.44.refs_3_ = bf16[32,2048]{1,0:T(8,128)(2,1)S(1)} collective-permute-done((bf16[32,2048]{1,0:T(8,128)(2,1)S(1)}, bf16[32,2048]{1,0:T(8,128)(2,1)S(1)}, u32[]{:S(2)}, u32[]{:S(2)}) %collective-permute-start.44) | collective-permute-done | bytes 131104 | tf_op jit(solution)/shard_map/ppermute | solution.py:1000
  132.4 2.8 %collective-permute-start.48 = (bf16[24,2048]{1,0:T(8,128)(2,1)S(1)}, bf16[24,2048]{1,0:T(8,128)(2,1)S(1)}, u32[]{:S(2)}, u32[]{:S(2)}) collective-permute-start(bf16[24,2048]{1,0:T(8,128)(2,1)S(1)} %get-tuple-element.262), channel_id=1, source_target_pairs={{0,2},{1,3},{2,0},{3,1},{4,6},{5,7},{6,4},{7,5},{8,10},{9,11},{10,... | collective-permute-start | bytes 294920 | tf_op jit(solution)/shard_map/ppermute | solution.py:1000
  138.4 2.7 %clip_grad.1 = bf16[4,2,14,14,1024]{4,3,2,1,0:T(8,128)(2,1)S(1)} custom-call(bf16[4,448,256]{2,1,0:T(8,128)(2,1)S(1)} %get-tuple-element.213.grad_ref, bf16[1024,256]{1,0:T(8,128)(2,1)S(1)} %copy-done.4, f32[4,56,1024]{2,1,0:T(8,128)S(1)} %get-tuple-element.191.entry_grad_ref), custom_call_target="tpu_custom_call" | custom-call | bytes 18700000 | tf_op jit(solution)/shard_map/clip_grad/pallas_call | solution.py:787
  141.9 2.7 %collective-permute-start.46 = (bf16[8,2816]{1,0:T(8,128)(2,1)S(1)}, bf16[8,2816]{1,0:T(8,128)(2,1)S(1)}, u32[]{:S(2)}, u32[]{:S(2)}) collective-permute-start(bf16[8,2816]{1,0:T(8,128)(2,1)S(1)} %get-tuple-element.255), channel_id=1, source_target_pairs={{0,4},{1,5},{2,6},{3,7},{4,0},{5,1},{6,2},{7,3},{8,12},{9,13},{10,... | collective-permute-start | bytes 135176 | tf_op jit(solution)/shard_map/ppermute | solution.py:1000
  145.7 5.0 %copy.33 = bf16[4,2,14,14,1024]{4,1,3,2,0:T(2,128)(2,1)} copy(bf16[4,2,14,14,1024]{4,3,2,1,0:T(8,128)(2,1)S(1)} %clip_grad.1) | data formatting | bytes 6422528
  (141 shorter events, 63.5 us)
Async XLA Ops:
  6.8 8.3 %collective-permute-start = (bf16[4,224,256]{2,1,0:T(8,128)(2,1)S(1)}, bf16[4,224,256]{2,1,0:T(8,128)(2,1)S(1)}, u32[]{:S(2)}, u32[]{:S(2)}) collective-permute-start(bf16[4,224,256]{2,1,0:T(8,128)(2,1)S(1)} %get-tuple-element.144.oz_ref), channel_id=1, source_target_pairs={{1,2},{2,1},{3,4},{4,3},{5,6},{6,5},{9,10},{10,9},{11,12},{12,11},... | collective-permute-start | bytes 1376264 | tf_op jit(solution)/shard_map/ppermute | solution.py:817
  58.2 10.4 %collective-permute-start.13 = (f32[2,2048]{1,0:T(2,128)S(1)}, f32[2,2048]{1,0:T(2,128)S(1)}, u32[]{:S(2)}, u32[]{:S(2)}) collective-permute-start(f32[2,2048]{1,0:T(2,128)S(1)} %add.6), channel_id=1, source_target_pairs={{0,2},{1,3},{2,0},{3,1},{4,6},{5,7},{6,4},{7,5},{8,10},{9,11},{10,... | collective-permute-start | bytes 49160 | tf_op jit(solution)/shard_map/ppermute | solution.py:1000
  58.2 10.4 %collective-permute-start.14 = (f32[2,2048]{1,0:T(2,128)S(1)}, f32[2,2048]{1,0:T(2,128)S(1)}, u32[]{:S(2)}, u32[]{:S(2)}) collective-permute-start(f32[2,2048]{1,0:T(2,128)S(1)} %add.6), channel_id=1, source_target_pairs={{0,4},{1,5},{2,6},{3,7},{4,0},{5,1},{6,2},{7,3},{8,12},{9,13},{10,... | collective-permute-start | bytes 49160 | tf_op jit(solution)/shard_map/ppermute | solution.py:1000
  70.2 17.0 %collective-permute-start.28 = (bf16[224,2048]{1,0:T(8,128)(2,1)S(1)}, bf16[224,2048]{1,0:T(8,128)(2,1)S(1)}, u32[]{:S(2)}, u32[]{:S(2)}) collective-permute-start(bf16[224,2048]{1,0:T(8,128)(2,1)S(1)} %get-tuple-element.183.sum_ref), channel_id=1, source_target_pairs={{0,1},{1,0},{2,3},{3,2},{4,5},{5,4},{6,7},{7,6},{8,9},{9,8},{10,11... | collective-permute-start | bytes 2752520 | tf_op jit(solution)/shard_map/ppermute | solution.py:835
  70.3 21.1 %collective-permute-start.24 = (bf16[2,2,32,2048]{3,2,1,0:T(8,128)(2,1)S(1)}, bf16[2,2,32,2048]{3,2,1,0:T(8,128)(2,1)S(1)}, u32[]{:S(2)}, u32[]{:S(2)}) collective-permute-start(bf16[2,2,32,2048]{3,2,1,0:T(8,128)(2,1)S(1)} %get-tuple-element.178), channel_id=1, source_target_pairs={{0,8},{8,0},{16,24},{24,16},{1,9},{9,1},{17,25},{25,17},{2,10},{10... | collective-permute-start | bytes 1572872 | tf_op jit(solution)/shard_map/ppermute | solution.py:865
  71.8 19.6 %collective-permute-start.25 = (bf16[2,2,32,2048]{3,2,1,0:T(8,128)(2,1)S(1)}, bf16[2,2,32,2048]{3,2,1,0:T(8,128)(2,1)S(1)}, u32[]{:S(2)}, u32[]{:S(2)}) collective-permute-start(bf16[2,2,32,2048]{3,2,1,0:T(8,128)(2,1)S(1)} %get-tuple-element.180), channel_id=1, source_target_pairs={{0,16},{8,24},{16,0},{24,8},{1,17},{9,25},{17,1},{25,9},{2,18},{10... | collective-permute-start | bytes 1572872 | tf_op jit(solution)/shard_map/ppermute | solution.py:865
  97.3 10.4 %collective-permute-start.30 = (bf16[4,224,256]{2,1,0:T(8,128)(2,1)S(1)}, bf16[4,224,256]{2,1,0:T(8,128)(2,1)S(1)}, u32[]{:S(2)}, u32[]{:S(2)}) collective-permute-start(bf16[4,224,256]{2,1,0:T(8,128)(2,1)S(1)} %get-tuple-element.199.gc_ref), channel_id=1, source_target_pairs={{0,1},{1,0},{2,3},{3,2},{4,5},{5,4},{6,7},{7,6},{8,9},{9,8},{10,11... | collective-permute-start | bytes 1376264 | tf_op jit(solution)/shard_map/ppermute | solution.py:817
  98.0 8.3 %collective-permute-start.31 = (bf16[2,32,2048]{2,1,0:T(8,128)(2,1)S(1)}, bf16[2,32,2048]{2,1,0:T(8,128)(2,1)S(1)}, u32[]{:S(2)}, u32[]{:S(2)}) collective-permute-start(bf16[2,32,2048]{2,1,0:T(8,128)(2,1)S(1)} %get-tuple-element.204), channel_id=1, source_target_pairs={{0,16},{8,24},{16,0},{24,8},{1,17},{9,25},{17,1},{25,9},{2,18},{10... | collective-permute-start | bytes 786440 | tf_op jit(solution)/shard_map/ppermute | solution.py:865
  98.5 9.0 %collective-permute-start.32 = (bf16[2,32,2048]{2,1,0:T(8,128)(2,1)S(1)}, bf16[2,32,2048]{2,1,0:T(8,128)(2,1)S(1)}, u32[]{:S(2)}, u32[]{:S(2)}) collective-permute-start(bf16[2,32,2048]{2,1,0:T(8,128)(2,1)S(1)} %get-tuple-element.206), channel_id=1, source_target_pairs={{0,8},{8,0},{16,24},{24,16},{1,9},{9,1},{17,25},{25,17},{2,10},{10... | collective-permute-start | bytes 786440 | tf_op jit(solution)/shard_map/ppermute | solution.py:865
  104.3 18.7 %collective-permute-start.34 = (bf16[4,4,8,1792]{3,2,1,0:T(8,128)(2,1)S(1)}, bf16[4,4,8,1792]{3,2,1,0:T(8,128)(2,1)S(1)}, u32[]{:S(2)}, u32[]{:S(2)}) collective-permute-start(bf16[4,4,8,1792]{3,2,1,0:T(8,128)(2,1)S(1)} %get-tuple-element.217), channel_id=1, source_target_pairs={{0,1},{1,0},{2,3},{3,2},{4,5},{5,4},{6,7},{7,6},{8,9},{9,8},{10,11... | collective-permute-start | bytes 1376264 | tf_op jit(solution)/shard_map/ppermute | solution.py:835
  105.4 12.6 %collective-permute-start.38 = (bf16[2,2,24,2048]{3,2,1,0:T(8,128)(2,1)S(1)}, bf16[2,2,24,2048]{3,2,1,0:T(8,128)(2,1)S(1)}, u32[]{:S(2)}, u32[]{:S(2)}) collective-permute-start(bf16[2,2,24,2048]{3,2,1,0:T(8,128)(2,1)S(1)} %get-tuple-element.226), channel_id=1, source_target_pairs={{0,8},{8,0},{16,24},{24,16},{1,9},{9,1},{17,25},{25,17},{2,10},{10... | collective-permute-start | bytes 1179656 | tf_op jit(solution)/shard_map/ppermute | solution.py:865
  106.3 14.1 %collective-permute-start.39 = (bf16[2,2,24,2048]{3,2,1,0:T(8,128)(2,1)S(1)}, bf16[2,2,24,2048]{3,2,1,0:T(8,128)(2,1)S(1)}, u32[]{:S(2)}, u32[]{:S(2)}) collective-permute-start(bf16[2,2,24,2048]{3,2,1,0:T(8,128)(2,1)S(1)} %get-tuple-element.228), channel_id=1, source_target_pairs={{0,16},{8,24},{16,0},{24,8},{1,17},{9,25},{17,1},{25,9},{2,18},{10... | collective-permute-start | bytes 1179656 | tf_op jit(solution)/shard_map/ppermute | solution.py:865
  117.0 8.7 %collective-permute-start.42 = (bf16[32,2048]{1,0:T(8,128)(2,1)S(1)}, bf16[32,2048]{1,0:T(8,128)(2,1)S(1)}, u32[]{:S(2)}, u32[]{:S(2)}) collective-permute-start(bf16[32,2048]{1,0:T(8,128)(2,1)S(1)} %get-tuple-element.241), channel_id=1, source_target_pairs={{0,2},{1,3},{2,0},{3,1},{4,6},{5,7},{6,4},{7,5},{8,10},{9,11},{10,... | collective-permute-start | bytes 393224 | tf_op jit(solution)/shard_map/ppermute | solution.py:1000
  120.4 10.9 %collective-permute-start.44 = (bf16[32,2048]{1,0:T(8,128)(2,1)S(1)}, bf16[32,2048]{1,0:T(8,128)(2,1)S(1)}, u32[]{:S(2)}, u32[]{:S(2)}) collective-permute-start(bf16[32,2048]{1,0:T(8,128)(2,1)S(1)} %get-tuple-element.243), channel_id=1, source_target_pairs={{0,6},{1,7},{2,4},{3,5},{4,2},{5,3},{6,0},{7,1},{8,14},{9,15},{10,... | collective-permute-start | bytes 393224 | tf_op jit(solution)/shard_map/ppermute | solution.py:1000
  122.1 10.1 %collective-permute-start.40 = (bf16[2,24,2048]{2,1,0:T(8,128)(2,1)S(1)}, bf16[2,24,2048]{2,1,0:T(8,128)(2,1)S(1)}, u32[]{:S(2)}, u32[]{:S(2)}) collective-permute-start(bf16[2,24,2048]{2,1,0:T(8,128)(2,1)S(1)} %get-tuple-element.234), channel_id=1, source_target_pairs={{0,16},{8,24},{16,0},{24,8},{1,17},{9,25},{17,1},{25,9},{2,18},{10... | collective-permute-start | bytes 589832 | tf_op jit(solution)/shard_map/ppermute | solution.py:865
  123.0 9.2 %collective-permute-start.41 = (bf16[2,24,2048]{2,1,0:T(8,128)(2,1)S(1)}, bf16[2,24,2048]{2,1,0:T(8,128)(2,1)S(1)}, u32[]{:S(2)}, u32[]{:S(2)}) collective-permute-start(bf16[2,24,2048]{2,1,0:T(8,128)(2,1)S(1)} %get-tuple-element.236), channel_id=1, source_target_pairs={{0,8},{8,0},{16,24},{24,16},{1,9},{9,1},{17,25},{25,17},{2,10},{10... | collective-permute-start | bytes 589832 | tf_op jit(solution)/shard_map/ppermute | solution.py:865
  125.7 11.3 %collective-permute-start.35 = (bf16[4,8,2816]{2,1,0:T(8,128)(2,1)S(1)}, bf16[4,8,2816]{2,1,0:T(8,128)(2,1)S(1)}, u32[]{:S(2)}, u32[]{:S(2)}) collective-permute-start(bf16[4,8,2816]{2,1,0:T(8,128)(2,1)S(1)} %get-tuple-element.219), channel_id=1, source_target_pairs={{0,8},{8,0},{16,24},{24,16},{1,9},{9,1},{17,25},{25,17},{2,10},{10... | collective-permute-start | bytes 540680 | tf_op jit(solution)/shard_map/ppermute | solution.py:994
  126.2 14.9 %collective-permute-start.36 = (bf16[4,8,2816]{2,1,0:T(8,128)(2,1)S(1)}, bf16[4,8,2816]{2,1,0:T(8,128)(2,1)S(1)}, u32[]{:S(2)}, u32[]{:S(2)}) collective-permute-start(bf16[4,8,2816]{2,1,0:T(8,128)(2,1)S(1)} %get-tuple-element.220), channel_id=1, source_target_pairs={{0,16},{8,24},{16,0},{24,8},{1,17},{9,25},{17,1},{25,9},{2,18},{10... | collective-permute-start | bytes 540680 | tf_op jit(solution)/shard_map/ppermute | solution.py:994
  131.3 9.8 %collective-permute-start.37 = (bf16[4,8,2816]{2,1,0:T(8,128)(2,1)S(1)}, bf16[4,8,2816]{2,1,0:T(8,128)(2,1)S(1)}, u32[]{:S(2)}, u32[]{:S(2)}) collective-permute-start(bf16[4,8,2816]{2,1,0:T(8,128)(2,1)S(1)} %get-tuple-element.221), channel_id=1, source_target_pairs={{0,24},{8,16},{16,8},{24,0},{1,25},{9,17},{17,9},{25,1},{2,26},{10... | collective-permute-start | bytes 540680 | tf_op jit(solution)/shard_map/ppermute | solution.py:994
  132.4 12.2 %collective-permute-start.48 = (bf16[24,2048]{1,0:T(8,128)(2,1)S(1)}, bf16[24,2048]{1,0:T(8,128)(2,1)S(1)}, u32[]{:S(2)}, u32[]{:S(2)}) collective-permute-start(bf16[24,2048]{1,0:T(8,128)(2,1)S(1)} %get-tuple-element.262), channel_id=1, source_target_pairs={{0,2},{1,3},{2,0},{3,1},{4,6},{5,7},{6,4},{7,5},{8,10},{9,11},{10,... | collective-permute-start | bytes 294920 | tf_op jit(solution)/shard_map/ppermute | solution.py:1000
  135.2 15.5 %collective-permute-start.49 = (bf16[24,2048]{1,0:T(8,128)(2,1)S(1)}, bf16[24,2048]{1,0:T(8,128)(2,1)S(1)}, u32[]{:S(2)}, u32[]{:S(2)}) collective-permute-start(bf16[24,2048]{1,0:T(8,128)(2,1)S(1)} %get-tuple-element.263), channel_id=1, source_target_pairs={{0,4},{1,5},{2,6},{3,7},{4,0},{5,1},{6,2},{7,3},{8,12},{9,13},{10,... | collective-permute-start | bytes 294920 | tf_op jit(solution)/shard_map/ppermute | solution.py:1000
  137.0 13.7 %collective-permute-start.50 = (bf16[24,2048]{1,0:T(8,128)(2,1)S(1)}, bf16[24,2048]{1,0:T(8,128)(2,1)S(1)}, u32[]{:S(2)}, u32[]{:S(2)}) collective-permute-start(bf16[24,2048]{1,0:T(8,128)(2,1)S(1)} %get-tuple-element.264), channel_id=1, source_target_pairs={{0,6},{1,7},{2,4},{3,5},{4,2},{5,3},{6,0},{7,1},{8,14},{9,15},{10,... | collective-permute-start | bytes 294920 | tf_op jit(solution)/shard_map/ppermute | solution.py:1000
  141.2 10.3 %collective-permute-start.45 = (bf16[8,2816]{1,0:T(8,128)(2,1)S(1)}, bf16[8,2816]{1,0:T(8,128)(2,1)S(1)}, u32[]{:S(2)}, u32[]{:S(2)}) collective-permute-start(bf16[8,2816]{1,0:T(8,128)(2,1)S(1)} %get-tuple-element.254), channel_id=1, source_target_pairs={{0,2},{1,3},{2,0},{3,1},{4,6},{5,7},{6,4},{7,5},{8,10},{9,11},{10,... | collective-permute-start | bytes 135176 | tf_op jit(solution)/shard_map/ppermute | solution.py:1000
  141.9 9.7 %collective-permute-start.46 = (bf16[8,2816]{1,0:T(8,128)(2,1)S(1)}, bf16[8,2816]{1,0:T(8,128)(2,1)S(1)}, u32[]{:S(2)}, u32[]{:S(2)}) collective-permute-start(bf16[8,2816]{1,0:T(8,128)(2,1)S(1)} %get-tuple-element.255), channel_id=1, source_target_pairs={{0,4},{1,5},{2,6},{3,7},{4,0},{5,1},{6,2},{7,3},{8,12},{9,13},{10,... | collective-permute-start | bytes 135176 | tf_op jit(solution)/shard_map/ppermute | solution.py:1000
  (42 other events, 318.5 us)

commit v4 on v3

--- a/solution.py
+++ b/solution.py
@@ -1138,11 +1138,6 @@
         [],
     )
     received = group_parts(late_back)
-    logit_terms, bias_grad = call(
-        head_kernel, "head", w([after(pooled, received[0]), head, logit_grad]),
-        [((clips // 2, channels), f32, "w"), ((1, logit_grad.shape[1]), f32, "w")], [],
-    )
-    late_stats = after(late_stats, logit_terms)
     skip_rows = skip_grad.reshape(late_all, late_wide)
     if by_pairs:
         entry_other = core_swap(entry)
@@ -1166,6 +1161,11 @@
     late_gz, late_gc = swap_neighbours(late_mid_grad, late_mid_grad)
     if by_pairs:
         skip_pieces = first_phase(after(skip_pieces, late_mid_grad))
+    logit_terms, bias_grad = call(
+        head_kernel, "head", w([after(pooled, late_mid_grad), head, logit_grad]),
+        [((clips // 2, channels), f32, "w"), ((1, logit_grad.shape[1]), f32, "w")], [],
+    )
+    late_first = after(late_first, logit_terms)
     (late_taps_table,) = call(
         late_taps_kernel, "late_taps",
         [(late_z, "w"), (late_act, "w"), (late_c, "w"), (late_mid_grad, "w")],
@@ -1285,7 +1285,7 @@
         up_pieces = second_phase("up_down_phase", after(up_pieces, first_grad))
         clip_parts = call(
             pair_sum_kernel, "pair_sum",
-            w([keep, core_swap(send), keep_terms, core_swap(after(send_terms, third_gz))]),
+            w([after(keep, clip_grad), core_swap(send), keep_terms, core_swap(after(send_terms, third_gz))]),
             [((chips, deep, channels + extra + block // deep * inner), bf16, "w")] * clip_axis,
             [],
         )
@@ -1296,7 +1296,7 @@
         clip_parts = over_clip(clip_parts)
         up_pieces = over_chips(up_pieces)
         chip_parts = call(
-            functools.partial(chip_totals_kernel, clip_axis), "clip_sum", w(after(clip_parts, (up_pieces[0], clip_grad))),
+            functools.partial(chip_totals_kernel, clip_axis), "clip_sum", w(after(clip_parts, up_pieces[0])),
             [(clip_parts[0].shape[1:], bf16, "w")] * chips, [],
         )
         third_terms = [part[None] for part in over_chips(chip_parts)]

time: 153 us -> 150 us (0.980)
  waiting for transfers between devices: 19.4 us -> 15.9 us
    ppermute x21, waiting for transfers between devices: 12.9 us -> 9.54 us  [over_chips(): lax.ppermute(pieces[z], 'space', [(i, i ^ 2 * z) for i in range(2 * size)])]
    ppermute x21, starting transfers between devices: 32.2 us -> 34 us  [over_chips(): lax.ppermute(pieces[z], 'space', [(i, i ^ 2 * z) for i in range(2 * size)])]
    ppermute x11, starting transfers between devices: 12.6 us -> 10.9 us  [core_swap(): lax.ppermute(values, 'space', [(i, i ^ 1) for i in range(lax.axis_size('s...]
  transfers between devices with their start and end apart: 51 -> 51, of which waited for: 14 -> 14; matrix products, arithmetic and copies ran while one was open for 3% -> 3% of each run, Pallas kernels for 24% -> 25%
where the time goes in v4:
time: 150 us
  starting transfers between devices  65.1 us (43%)
  Pallas kernels  59.1 us (39%)
  waiting for transfers between devices  15.9 us (11%)
  local copies, waits for them, and re-layouts  8.16 us (5%)
    pallas_call x28, Pallas kernels, call(): pl.pallas_call(kernel, name=name, out_shape=[jax.ShapeDtypeStruct(s, d) f...  50.7 us
    ppermute x21, starting transfers between devices, over_chips(): lax.ppermute(pieces[z], 'space', [(i, i ^ 2 * z) for i in range(2 * size)])  34 us
    ppermute x11, starting transfers between devices, core_swap(): lax.ppermute(values, 'space', [(i, i ^ 1) for i in range(lax.axis_size('s...  10.9 us
    ppermute x21, waiting for transfers between devices, over_chips(): lax.ppermute(pieces[z], 'space', [(i, i ^ 2 * z) for i in range(2 * size)])  9.54 us
    unnamed x32, local copies, waits for them, and re-layouts  8.16 us
    ppermute x8, starting transfers between devices, clip_swap(): lax.ppermute(values, 'clip', [(i, i ^ bit) for i in range(lax.axis_size('...  7.44 us
    ppermute x4, starting transfers between devices, swap_neighbours(): lax.ppermute(to_core, 'space', core)  6.31 us
    ppermute x11, waiting for transfers between devices, core_swap(): lax.ppermute(values, 'space', [(i, i ^ 1) for i in range(lax.axis_size('s...  4.56 us
  transfers between devices with their start and end apart: 51, of which 14 were waited for; matrix products, arithmetic and copies ran while one was open for 3% of the time, Pallas kernels for 25%

profile of v4, /device:TPU:0, one launch (start us, length us, event | category | flops | bytes accessed | tf_op | source)
XLA Modules:
  0.0 149.5 jit_solution(3975217570731432654)
XLA Ops:
  0.7 3.0 %copy.31.x_ref = bf16[4,2,14,14,1024]{4,3,2,1,0:T(8,128)(2,1)S(1)} copy(bf16[4,2,14,14,1024]{4,1,3,2,0:T(2,128)(2,1)} %param.16) | data formatting | bytes 6422528 | tf_op args[0]
  3.8 3.0 %first.1 = (f32[4,2,224,256]{3,2,1,0:T(8,128)S(1)}, bf16[4,224,256]{2,1,0:T(8,128)(2,1)S(1)}, bf16[4,224,256]{2,1,0:T(8,128)(2,1)S(1)}, f32[4,56,1024]{2,1,0:T(8,128)S(1)}) custom-call(s32[4]{0:T(128)S(1)} %copy-done.8, bf16[4,2,14,14,1024]{4,3,2,1,0:T(8,128)(2,1)S(1)} %copy.31.x_ref, bf16[1024,256]{1,0:T(8,128)(2,1)S(1)} %copy-done.4), custom_call_target="tpu_custom_call" | custom-call | bytes 18020000 | tf_op jit(solution)/shard_map/first/pallas_call | solution.py:787
  7.6 4.4 %collective-permute-start.1 = (bf16[4,224,256]{2,1,0:T(8,128)(2,1)S(1)}, bf16[4,224,256]{2,1,0:T(8,128)(2,1)S(1)}, u32[]{:S(2)}, u32[]{:S(2)}) collective-permute-start(bf16[4,224,256]{2,1,0:T(8,128)(2,1)S(1)} %get-tuple-element.146.oc_ref), channel_id=1, source_target_pairs={{0,1},{1,0},{2,3},{3,2},{4,5},{5,4},{6,7},{7,6},{8,9},{9,8},{10,11... | collective-permute-start | bytes 1376264 | tf_op jit(solution)/shard_map/ppermute | solution.py:817
  12.0 3.0 %mid_own.1.part_ref = f32[4,2,224,256]{3,2,1,0:T(8,128)S(1)} custom-call(bf16[4,224,256]{2,1,0:T(8,128)(2,1)S(1)} %get-tuple-element.145.oz_ref, bf16[4,224,256]{2,1,0:T(8,128)(2,1)S(1)} %get-tuple-element.146.oc_ref, f32[27,256]{1,0:T(8,128)S(1)} %get-tuple-element.147.taps_ref), custom_call_target="tpu_custom_call" | custom-call | bytes 17000000 | tf_op jit(solution)/shard_map/mid_own/pallas_call | solution.py:787
  15.1 6.1 %mid.1 = (f32[4,2,224,256]{3,2,1,0:T(8,128)S(1)}, bf16[4,2,224,256]{3,2,1,0:T(8,128)(2,1)S(1)}, bf16[224,256]{1,0:T(8,128)(2,1)S(1)}, f32[224,1024]{1,0:T(8,128)...) custom-call(s32[4]{0:T(128)S(1)} %copy-done.8, ...), custom_call_target="tpu_custom_call" | custom-call | bytes 29240000 | tf_op jit(solution)/shard_map/mid/pallas_call | solution.py:787
  21.3 3.0 %collective-permute-start.2 = (f32[2,1024]{1,0:T(2,128)S(1)}, f32[2,1024]{1,0:T(2,128)S(1)}, u32[]{:S(2)}, u32[]{:S(2)}) collective-permute-start(f32[2,1024]{1,0:T(2,128)S(1)} %get-tuple-element.148.one_ref), channel_id=1, source_target_pairs={{0,1},{1,0},{2,3},{3,2},{4,5},{5,4},{6,7},{7,6},{8,9},{9,8},{10,11... | collective-permute-start | bytes 24584 | tf_op jit(solution)/shard_map/ppermute | solution.py:835
  27.1 2.6 %collective-permute-start.4 = (f32[2,1024]{1,0:T(2,128)S(1)}, f32[2,1024]{1,0:T(2,128)S(1)}, u32[]{:S(2)}, u32[]{:S(2)}) collective-permute-start(f32[2,1024]{1,0:T(2,128)S(1)} %add.4), channel_id=1, source_target_pairs={{0,4},{1,5},{2,6},{3,7},{4,0},{5,1},{6,2},{7,3},{8,12},{9,13},{10,... | collective-permute-start | bytes 24584 | tf_op jit(solution)/shard_map/ppermute | solution.py:1000
  31.7 3.5 %collective-permute-done.5 = f32[2,1024]{1,0:T(2,128)S(1)} collective-permute-done((f32[2,1024]{1,0:T(2,128)S(1)}, f32[2,1024]{1,0:T(2,128)S(1)}, u32[]{:S(2)}, u32[]{:S(2)}) %collective-permute-start.5) | collective-permute-done | bytes 8224 | tf_op jit(solution)/shard_map/ppermute | solution.py:1000
  38.5 2.4 %late_mid.1 = (f32[4,56,512]{2,1,0:T(8,128)S(1)}, bf16[224,512]{1,0:T(8,128)(2,1)S(1)}, bf16[224,2048]{1,0:T(8,128)(2,1)S(1)}, f32[2,2048]{1,0:T(2,128)S(1)}) custom-call(s32[4]{0:T(128)S(1)} %copy-done.8, bf16[4,56,512]{2,1,0:T(8,128)(2,1)S(1)} %collective-permute-done.6.rz_ref, bf16[4,56,512]{2,1,0:T(8,128)(2,1)S(1)} %get-tuple-element.151.own_ref, ...), custom_call_target="tpu_custom_call" | custom-call | bytes 15980000 | tf_op jit(solution)/shard_map/late_mid/pallas_call | solution.py:787
  40.9 3.6 %collective-permute-start.8 = (f32[2,2048]{1,0:T(2,128)S(1)}, f32[2,2048]{1,0:T(2,128)S(1)}, u32[]{:S(2)}, u32[]{:S(2)}) collective-permute-start(f32[2,2048]{1,0:T(2,128)S(1)} %get-tuple-element.153.one_ref), channel_id=1, source_target_pairs={{0,1},{1,0},{2,3},{3,2},{4,5},{5,4},{6,7},{7,6},{8,9},{9,8},{10,11... | collective-permute-start | bytes 49160 | tf_op jit(solution)/shard_map/ppermute | solution.py:835
  53.5 2.9 %post.1 = (f32[2,2048]{1,0:T(2,128)S(1)}, f32[2,2048]{1,0:T(2,128)S(1)}, f32[4,2048]{1,0:T(4,128)S(1)}, f32[4,56,2048]{2,1,0:T(8,128)S(1)}, bf16[4,56,2048]{2,1,0:T(8,128)(2,1)S(1)}) custom-call(s32[4]{0:T(128)S(1)} %copy-done.8, f32[1,2,2048]{2,1,0:T(2,128)S(1)} %bitcast.51, f32[1,2,2048]{2,1,0:T(2,128)S(1)} %bitcast.67, f32[1,2,2048]{2,1,0:T(2,128)S(1)} %bitcast.68, ...), custom_call_target="tpu_custom_call" | custom-call | bytes 20400000 | tf_op jit(solution)/shard_map/post/pallas_call | solution.py:787
  58.2 2.4 %collective-permute-start.14 = (f32[2,2048]{1,0:T(2,128)S(1)}, f32[2,2048]{1,0:T(2,128)S(1)}, u32[]{:S(2)}, u32[]{:S(2)}) collective-permute-start(f32[2,2048]{1,0:T(2,128)S(1)} %add.6), channel_id=1, source_target_pairs={{0,4},{1,5},{2,6},{3,7},{4,0},{5,1},{6,2},{7,3},{8,12},{9,13},{10,... | collective-permute-start | bytes 49160 | tf_op jit(solution)/shard_map/ppermute | solution.py:1000
  62.6 4.1 %skip_sums.1 = (f32[224,1024]{1,0:T(8,128)S(1)}, bf16[2,2,32,2048]{3,2,1,0:T(8,128)(2,1)S(1)}, bf16[2,2,32,2048]{3,2,1,0:T(8,128)(2,1)S(1)}, bf16[2,2,32,2048]{3...) custom-call(bf16[224,1024]{1,0:T(8,128)(2,1)S(1)} %get-tuple-element.155.entry_ref.left_ref, ...), custom_call_target="tpu_custom_call" | custom-call | bytes 23800000 | tf_op jit(solution)/shard_map/skip_sums/pallas_call | solution.py:916
  77.0 2.3 %late_back.1 = (bf16[224,512]{1,0:T(8,128)(2,1)S(1)}, f32[4,56,1024]{2,1,0:T(8,128)S(1)}, f32[4,1024]{1,0:T(4,128)S(1)}) custom-call(s32[4]{0:T(128)S(1)} %copy-done.8, bf16[4,56,512]{2,1,0:T(8,128)(2,1)S(1)} %collective-permute-done.18.rz_ref, bf16[4,56,512]{2,1,0:T(8,128)(2,1)S(1)} %get-tuple-element.164.grad_ref.own_ref, ...), custom_call_target="tpu_custom_call" | custom-call | bytes 17000000 | tf_op jit(solution)/shard_map/late_back/pallas_call | solution.py:787
  87.2 2.2 %up_down_sums.1 = (bf16[2,2,24,2048]{3,2,1,0:T(8,128)(2,1)S(1)}, bf16[2,2,24,2048]{3,2,1,0:T(8,128)(2,1)S(1)}, bf16[2,2,24,2048]{3,2,1,0:T(8,128)(2,1)S(1)}, bf16[2,2,24,2048]{3,2,1,0:T(8,128)(2,1)S(1)}) custom-call(bf16[224,512]{1,0:T(8,128)(2,1)S(1)} %get-tuple-element.182.act_ref, bf16[224,512]{1,0:T(8,128)(2,1)S(1)} %collective-permute-done.26.act_other_ref, ...), custom_call_target="tpu_custom_call" | custom-call | bytes 18700000 | tf_op jit(solution)/shard_map/up_down_sums/pallas_call | solution.py:974
  90.8 4.0 %third_grad.1 = (bf16[4,224,256]{2,1,0:T(8,128)(2,1)S(1)}, bf16[4,224,256]{2,1,0:T(8,128)(2,1)S(1)}, bf16[256,1024]{1,0:T(8,128)(2,1)S(1)}, f32[4,400]{1,0:T(4,128)}) custom-call(s32[4]{0:T(128)S(1)} %copy-done.8, f32[1,4,1024]{2,1,0:T(4,128)S(1)} %bitcast.49, f32[1,4,1024]{2,1,0:T(4,128)S(1)} %bitcast.61, f32[1,4,1024]{2,1,0:T(4,128)S(1)} %bitcast.62, ...), custom_call_target="tpu_custom_call" | custom-call | bytes 22780000 | tf_op jit(solution)/shard_map/third_grad/pallas_call | solution.py:787
  97.1 5.3 %third_taps.1 = (f32[4,4,8,1792]{3,2,1,0:T(8,128)S(1)}, bf16[4,4,8,1792]{3,2,1,0:T(8,128)(2,1)S(1)}) custom-call(bf16[4,224,256]{2,1,0:T(8,128)(2,1)S(1)} %collective-permute-done.rz_ref, bf16[4,224,256]{2,1,0:T(8,128)(2,1)S(1)} %get-tuple-element.145.oz_ref, bf16[4,224,256]{2,1,0:T(8,128)(2,1)S(1)} %get-tuple-element.146.oc_ref, ...), custom_call_target="tpu_custom_call" | custom-call | bytes 26180000 | tf_op jit(solution)/shard_map/third_taps/pallas_call | solution.py:787
  105.9 9.1 %first_grad.1 = (bf16[4,448,256]{2,1,0:T(8,128)(2,1)S(1)}, f32[4,4,32,256]{3,2,1,0:T(8,128)S(1)}, bf16[4,4,32,256]{3,2,1,0:T(8,128)(2,1)S(1)}) custom-call(s32[4]{0:T(128)S(1)} %copy-done.8, bf16[4,224,256]{2,1,0:T(8,128)(2,1)S(1)} %collective-permute-done.29.rz_ref, bf16[4,224,256]{2,1,0:T(8,128)(2,1)S(1)} %get-tuple-element.199.gz_ref, ...), custom_call_target="tpu_custom_call" | custom-call | bytes 36380000 | tf_op jit(solution)/shard_map/first_grad/pallas_call | solution.py:787
  116.2 2.4 %collective-permute-start.43 = (bf16[32,2048]{1,0:T(8,128)(2,1)S(1)}, bf16[32,2048]{1,0:T(8,128)(2,1)S(1)}, u32[]{:S(2)}, u32[]{:S(2)}) collective-permute-start(bf16[32,2048]{1,0:T(8,128)(2,1)S(1)} %get-tuple-element.244), channel_id=1, source_target_pairs={{0,4},{1,5},{2,6},{3,7},{4,0},{5,1},{6,2},{7,3},{8,12},{9,13},{10,... | collective-permute-start | bytes 393224 | tf_op jit(solution)/shard_map/ppermute | solution.py:1000
  121.8 2.7 %clip_grad.1 = bf16[4,2,14,14,1024]{4,3,2,1,0:T(8,128)(2,1)S(1)} custom-call(bf16[4,448,256]{2,1,0:T(8,128)(2,1)S(1)} %get-tuple-element.214.grad_ref, bf16[1024,256]{1,0:T(8,128)(2,1)S(1)} %copy-done.4, f32[4,56,1024]{2,1,0:T(8,128)S(1)} %get-tuple-element.192.entry_grad_ref), custom_call_target="tpu_custom_call" | custom-call | bytes 18700000 | tf_op jit(solution)/shard_map/clip_grad/pallas_call | solution.py:787
  130.5 2.8 %collective-permute-start.48 = (bf16[24,2048]{1,0:T(8,128)(2,1)S(1)}, bf16[24,2048]{1,0:T(8,128)(2,1)S(1)}, u32[]{:S(2)}, u32[]{:S(2)}) collective-permute-start(bf16[24,2048]{1,0:T(8,128)(2,1)S(1)} %get-tuple-element.264), channel_id=1, source_target_pairs={{0,2},{1,3},{2,0},{3,1},{4,6},{5,7},{6,4},{7,5},{8,10},{9,11},{10,... | collective-permute-start | bytes 294920 | tf_op jit(solution)/shard_map/ppermute | solution.py:1000
  136.6 2.7 %collective-permute-start.45 = (bf16[8,2816]{1,0:T(8,128)(2,1)S(1)}, bf16[8,2816]{1,0:T(8,128)(2,1)S(1)}, u32[]{:S(2)}, u32[]{:S(2)}) collective-permute-start(bf16[8,2816]{1,0:T(8,128)(2,1)S(1)} %get-tuple-element.256), channel_id=1, source_target_pairs={{0,2},{1,3},{2,0},{3,1},{4,6},{5,7},{6,4},{7,5},{8,10},{9,11},{10,... | collective-permute-start | bytes 135176 | tf_op jit(solution)/shard_map/ppermute | solution.py:1000
  139.3 3.4 %collective-permute-start.46 = (bf16[8,2816]{1,0:T(8,128)(2,1)S(1)}, bf16[8,2816]{1,0:T(8,128)(2,1)S(1)}, u32[]{:S(2)}, u32[]{:S(2)}) collective-permute-start(bf16[8,2816]{1,0:T(8,128)(2,1)S(1)} %get-tuple-element.257), channel_id=1, source_target_pairs={{0,4},{1,5},{2,6},{3,7},{4,0},{5,1},{6,2},{7,3},{8,12},{9,13},{10,... | collective-permute-start | bytes 135176 | tf_op jit(solution)/shard_map/ppermute | solution.py:1000
  142.7 5.0 %copy.33 = bf16[4,2,14,14,1024]{4,1,3,2,0:T(2,128)(2,1)} copy(bf16[4,2,14,14,1024]{4,3,2,1,0:T(8,128)(2,1)S(1)} %clip_grad.1) | data formatting | bytes 6422528
  (141 shorter events, 62.2 us)
Async XLA Ops:
  6.8 8.3 %collective-permute-start = (bf16[4,224,256]{2,1,0:T(8,128)(2,1)S(1)}, bf16[4,224,256]{2,1,0:T(8,128)(2,1)S(1)}, u32[]{:S(2)}, u32[]{:S(2)}) collective-permute-start(bf16[4,224,256]{2,1,0:T(8,128)(2,1)S(1)} %get-tuple-element.145.oz_ref), channel_id=1, source_target_pairs={{1,2},{2,1},{3,4},{4,3},{5,6},{6,5},{9,10},{10,9},{11,12},{12,11},... | collective-permute-start | bytes 1376264 | tf_op jit(solution)/shard_map/ppermute | solution.py:817
  58.2 8.5 %collective-permute-start.13 = (f32[2,2048]{1,0:T(2,128)S(1)}, f32[2,2048]{1,0:T(2,128)S(1)}, u32[]{:S(2)}, u32[]{:S(2)}) collective-permute-start(f32[2,2048]{1,0:T(2,128)S(1)} %add.6), channel_id=1, source_target_pairs={{0,2},{1,3},{2,0},{3,1},{4,6},{5,7},{6,4},{7,5},{8,10},{9,11},{10,... | collective-permute-start | bytes 49160 | tf_op jit(solution)/shard_map/ppermute | solution.py:1000
  58.2 8.5 %collective-permute-start.14 = (f32[2,2048]{1,0:T(2,128)S(1)}, f32[2,2048]{1,0:T(2,128)S(1)}, u32[]{:S(2)}, u32[]{:S(2)}) collective-permute-start(f32[2,2048]{1,0:T(2,128)S(1)} %add.6), channel_id=1, source_target_pairs={{0,4},{1,5},{2,6},{3,7},{4,0},{5,1},{6,2},{7,3},{8,12},{9,13},{10,... | collective-permute-start | bytes 49160 | tf_op jit(solution)/shard_map/ppermute | solution.py:1000
  68.3 16.9 %collective-permute-start.28 = (bf16[224,2048]{1,0:T(8,128)(2,1)S(1)}, bf16[224,2048]{1,0:T(8,128)(2,1)S(1)}, u32[]{:S(2)}, u32[]{:S(2)}) collective-permute-start(bf16[224,2048]{1,0:T(8,128)(2,1)S(1)} %get-tuple-element.184.sum_ref), channel_id=1, source_target_pairs={{0,1},{1,0},{2,3},{3,2},{4,5},{5,4},{6,7},{7,6},{8,9},{9,8},{10,11... | collective-permute-start | bytes 2752520 | tf_op jit(solution)/shard_map/ppermute | solution.py:835
  68.4 21.1 %collective-permute-start.24 = (bf16[2,2,32,2048]{3,2,1,0:T(8,128)(2,1)S(1)}, bf16[2,2,32,2048]{3,2,1,0:T(8,128)(2,1)S(1)}, u32[]{:S(2)}, u32[]{:S(2)}) collective-permute-start(bf16[2,2,32,2048]{3,2,1,0:T(8,128)(2,1)S(1)} %get-tuple-element.179), channel_id=1, source_target_pairs={{0,8},{8,0},{16,24},{24,16},{1,9},{9,1},{17,25},{25,17},{2,10},{10... | collective-permute-start | bytes 1572872 | tf_op jit(solution)/shard_map/ppermute | solution.py:865
  69.9 19.6 %collective-permute-start.25 = (bf16[2,2,32,2048]{3,2,1,0:T(8,128)(2,1)S(1)}, bf16[2,2,32,2048]{3,2,1,0:T(8,128)(2,1)S(1)}, u32[]{:S(2)}, u32[]{:S(2)}) collective-permute-start(bf16[2,2,32,2048]{3,2,1,0:T(8,128)(2,1)S(1)} %get-tuple-element.181), channel_id=1, source_target_pairs={{0,16},{8,24},{16,0},{24,8},{1,17},{9,25},{17,1},{25,9},{2,18},{10... | collective-permute-start | bytes 1572872 | tf_op jit(solution)/shard_map/ppermute | solution.py:865
  95.5 10.4 %collective-permute-start.30 = (bf16[4,224,256]{2,1,0:T(8,128)(2,1)S(1)}, bf16[4,224,256]{2,1,0:T(8,128)(2,1)S(1)}, u32[]{:S(2)}, u32[]{:S(2)}) collective-permute-start(bf16[4,224,256]{2,1,0:T(8,128)(2,1)S(1)} %get-tuple-element.200.gc_ref), channel_id=1, source_target_pairs={{0,1},{1,0},{2,3},{3,2},{4,5},{5,4},{6,7},{7,6},{8,9},{9,8},{10,11... | collective-permute-start | bytes 1376264 | tf_op jit(solution)/shard_map/ppermute | solution.py:817
  96.1 8.3 %collective-permute-start.31 = (bf16[2,32,2048]{2,1,0:T(8,128)(2,1)S(1)}, bf16[2,32,2048]{2,1,0:T(8,128)(2,1)S(1)}, u32[]{:S(2)}, u32[]{:S(2)}) collective-permute-start(bf16[2,32,2048]{2,1,0:T(8,128)(2,1)S(1)} %get-tuple-element.205), channel_id=1, source_target_pairs={{0,16},{8,24},{16,0},{24,8},{1,17},{9,25},{17,1},{25,9},{2,18},{10... | collective-permute-start | bytes 786440 | tf_op jit(solution)/shard_map/ppermute | solution.py:865
  96.6 9.0 %collective-permute-start.32 = (bf16[2,32,2048]{2,1,0:T(8,128)(2,1)S(1)}, bf16[2,32,2048]{2,1,0:T(8,128)(2,1)S(1)}, u32[]{:S(2)}, u32[]{:S(2)}) collective-permute-start(bf16[2,32,2048]{2,1,0:T(8,128)(2,1)S(1)} %get-tuple-element.207), channel_id=1, source_target_pairs={{0,8},{8,0},{16,24},{24,16},{1,9},{9,1},{17,25},{25,17},{2,10},{10... | collective-permute-start | bytes 786440 | tf_op jit(solution)/shard_map/ppermute | solution.py:865
  102.4 18.7 %collective-permute-start.34 = (bf16[4,4,8,1792]{3,2,1,0:T(8,128)(2,1)S(1)}, bf16[4,4,8,1792]{3,2,1,0:T(8,128)(2,1)S(1)}, u32[]{:S(2)}, u32[]{:S(2)}) collective-permute-start(bf16[4,4,8,1792]{3,2,1,0:T(8,128)(2,1)S(1)} %get-tuple-element.219), channel_id=1, source_target_pairs={{0,1},{1,0},{2,3},{3,2},{4,5},{5,4},{6,7},{7,6},{8,9},{9,8},{10,11... | collective-permute-start | bytes 1376264 | tf_op jit(solution)/shard_map/ppermute | solution.py:835
  103.5 12.6 %collective-permute-start.38 = (bf16[2,2,24,2048]{3,2,1,0:T(8,128)(2,1)S(1)}, bf16[2,2,24,2048]{3,2,1,0:T(8,128)(2,1)S(1)}, u32[]{:S(2)}, u32[]{:S(2)}) collective-permute-start(bf16[2,2,24,2048]{3,2,1,0:T(8,128)(2,1)S(1)} %get-tuple-element.228), channel_id=1, source_target_pairs={{0,8},{8,0},{16,24},{24,16},{1,9},{9,1},{17,25},{25,17},{2,10},{10... | collective-permute-start | bytes 1179656 | tf_op jit(solution)/shard_map/ppermute | solution.py:865
  104.4 14.2 %collective-permute-start.39 = (bf16[2,2,24,2048]{3,2,1,0:T(8,128)(2,1)S(1)}, bf16[2,2,24,2048]{3,2,1,0:T(8,128)(2,1)S(1)}, u32[]{:S(2)}, u32[]{:S(2)}) collective-permute-start(bf16[2,2,24,2048]{3,2,1,0:T(8,128)(2,1)S(1)} %get-tuple-element.230), channel_id=1, source_target_pairs={{0,16},{8,24},{16,0},{24,8},{1,17},{9,25},{17,1},{25,9},{2,18},{10... | collective-permute-start | bytes 1179656 | tf_op jit(solution)/shard_map/ppermute | solution.py:865
  115.1 9.6 %collective-permute-start.42 = (bf16[32,2048]{1,0:T(8,128)(2,1)S(1)}, bf16[32,2048]{1,0:T(8,128)(2,1)S(1)}, u32[]{:S(2)}, u32[]{:S(2)}) collective-permute-start(bf16[32,2048]{1,0:T(8,128)(2,1)S(1)} %get-tuple-element.243), channel_id=1, source_target_pairs={{0,2},{1,3},{2,0},{3,1},{4,6},{5,7},{6,4},{7,5},{8,10},{9,11},{10,... | collective-permute-start | bytes 393224 | tf_op jit(solution)/shard_map/ppermute | solution.py:1000
  116.2 9.9 %collective-permute-start.43 = (bf16[32,2048]{1,0:T(8,128)(2,1)S(1)}, bf16[32,2048]{1,0:T(8,128)(2,1)S(1)}, u32[]{:S(2)}, u32[]{:S(2)}) collective-permute-start(bf16[32,2048]{1,0:T(8,128)(2,1)S(1)} %get-tuple-element.244), channel_id=1, source_target_pairs={{0,4},{1,5},{2,6},{3,7},{4,0},{5,1},{6,2},{7,3},{8,12},{9,13},{10,... | collective-permute-start | bytes 393224 | tf_op jit(solution)/shard_map/ppermute | solution.py:1000
  118.5 10.9 %collective-permute-start.44 = (bf16[32,2048]{1,0:T(8,128)(2,1)S(1)}, bf16[32,2048]{1,0:T(8,128)(2,1)S(1)}, u32[]{:S(2)}, u32[]{:S(2)}) collective-permute-start(bf16[32,2048]{1,0:T(8,128)(2,1)S(1)} %get-tuple-element.245), channel_id=1, source_target_pairs={{0,6},{1,7},{2,4},{3,5},{4,2},{5,3},{6,0},{7,1},{8,14},{9,15},{10,... | collective-permute-start | bytes 393224 | tf_op jit(solution)/shard_map/ppermute | solution.py:1000
  120.2 10.1 %collective-permute-start.40 = (bf16[2,24,2048]{2,1,0:T(8,128)(2,1)S(1)}, bf16[2,24,2048]{2,1,0:T(8,128)(2,1)S(1)}, u32[]{:S(2)}, u32[]{:S(2)}) collective-permute-start(bf16[2,24,2048]{2,1,0:T(8,128)(2,1)S(1)} %get-tuple-element.236), channel_id=1, source_target_pairs={{0,16},{8,24},{16,0},{24,8},{1,17},{9,25},{17,1},{25,9},{2,18},{10... | collective-permute-start | bytes 589832 | tf_op jit(solution)/shard_map/ppermute | solution.py:865
  121.1 9.2 %collective-permute-start.41 = (bf16[2,24,2048]{2,1,0:T(8,128)(2,1)S(1)}, bf16[2,24,2048]{2,1,0:T(8,128)(2,1)S(1)}, u32[]{:S(2)}, u32[]{:S(2)}) collective-permute-start(bf16[2,24,2048]{2,1,0:T(8,128)(2,1)S(1)} %get-tuple-element.238), channel_id=1, source_target_pairs={{0,8},{8,0},{16,24},{24,16},{1,9},{9,1},{17,25},{25,17},{2,10},{10... | collective-permute-start | bytes 589832 | tf_op jit(solution)/shard_map/ppermute | solution.py:865
  124.7 10.4 %collective-permute-start.35 = (bf16[4,8,2816]{2,1,0:T(8,128)(2,1)S(1)}, bf16[4,8,2816]{2,1,0:T(8,128)(2,1)S(1)}, u32[]{:S(2)}, u32[]{:S(2)}) collective-permute-start(bf16[4,8,2816]{2,1,0:T(8,128)(2,1)S(1)} %get-tuple-element.221), channel_id=1, source_target_pairs={{0,8},{8,0},{16,24},{24,16},{1,9},{9,1},{17,25},{25,17},{2,10},{10... | collective-permute-start | bytes 540680 | tf_op jit(solution)/shard_map/ppermute | solution.py:994
  126.1 10.4 %collective-permute-start.36 = (bf16[4,8,2816]{2,1,0:T(8,128)(2,1)S(1)}, bf16[4,8,2816]{2,1,0:T(8,128)(2,1)S(1)}, u32[]{:S(2)}, u32[]{:S(2)}) collective-permute-start(bf16[4,8,2816]{2,1,0:T(8,128)(2,1)S(1)} %get-tuple-element.222), channel_id=1, source_target_pairs={{0,16},{8,24},{16,0},{24,8},{1,17},{9,25},{17,1},{25,9},{2,18},{10... | collective-permute-start | bytes 540680 | tf_op jit(solution)/shard_map/ppermute | solution.py:994
  130.5 12.2 %collective-permute-start.48 = (bf16[24,2048]{1,0:T(8,128)(2,1)S(1)}, bf16[24,2048]{1,0:T(8,128)(2,1)S(1)}, u32[]{:S(2)}, u32[]{:S(2)}) collective-permute-start(bf16[24,2048]{1,0:T(8,128)(2,1)S(1)} %get-tuple-element.264), channel_id=1, source_target_pairs={{0,2},{1,3},{2,0},{3,1},{4,6},{5,7},{6,4},{7,5},{8,10},{9,11},{10,... | collective-permute-start | bytes 294920 | tf_op jit(solution)/shard_map/ppermute | solution.py:1000
  133.3 14.4 %collective-permute-start.49 = (bf16[24,2048]{1,0:T(8,128)(2,1)S(1)}, bf16[24,2048]{1,0:T(8,128)(2,1)S(1)}, u32[]{:S(2)}, u32[]{:S(2)}) collective-permute-start(bf16[24,2048]{1,0:T(8,128)(2,1)S(1)} %get-tuple-element.265), channel_id=1, source_target_pairs={{0,4},{1,5},{2,6},{3,7},{4,0},{5,1},{6,2},{7,3},{8,12},{9,13},{10,... | collective-permute-start | bytes 294920 | tf_op jit(solution)/shard_map/ppermute | solution.py:1000
  135.1 12.6 %collective-permute-start.50 = (bf16[24,2048]{1,0:T(8,128)(2,1)S(1)}, bf16[24,2048]{1,0:T(8,128)(2,1)S(1)}, u32[]{:S(2)}, u32[]{:S(2)}) collective-permute-start(bf16[24,2048]{1,0:T(8,128)(2,1)S(1)} %get-tuple-element.266), channel_id=1, source_target_pairs={{0,6},{1,7},{2,4},{3,5},{4,2},{5,3},{6,0},{7,1},{8,14},{9,15},{10,... | collective-permute-start | bytes 294920 | tf_op jit(solution)/shard_map/ppermute | solution.py:1000
  136.6 11.9 %collective-permute-start.45 = (bf16[8,2816]{1,0:T(8,128)(2,1)S(1)}, bf16[8,2816]{1,0:T(8,128)(2,1)S(1)}, u32[]{:S(2)}, u32[]{:S(2)}) collective-permute-start(bf16[8,2816]{1,0:T(8,128)(2,1)S(1)} %get-tuple-element.256), channel_id=1, source_target_pairs={{0,2},{1,3},{2,0},{3,1},{4,6},{5,7},{6,4},{7,5},{8,10},{9,11},{10,... | collective-permute-start | bytes 135176 | tf_op jit(solution)/shard_map/ppermute | solution.py:1000
  139.3 9.2 %collective-permute-start.46 = (bf16[8,2816]{1,0:T(8,128)(2,1)S(1)}, bf16[8,2816]{1,0:T(8,128)(2,1)S(1)}, u32[]{:S(2)}, u32[]{:S(2)}) collective-permute-start(bf16[8,2816]{1,0:T(8,128)(2,1)S(1)} %get-tuple-element.257), channel_id=1, source_target_pairs={{0,4},{1,5},{2,6},{3,7},{4,0},{5,1},{6,2},{7,3},{8,12},{9,13},{10,... | collective-permute-start | bytes 135176 | tf_op jit(solution)/shard_map/ppermute | solution.py:1000
  (42 other events, 312.5 us)

commit v5 on v4

--- a/solution.py
+++ b/solution.py
@@ -217,7 +217,7 @@
             )
             return 0
 
-        lax.fori_loop(0, rows // chunk, step, 0)
+        lax.fori_loop(0, rows // chunk, step, 0, unroll=True)
 
 
 def mid_kernel(
@@ -253,7 +253,7 @@
             put_lanes(acts, slot * rows + start, act)
             return 0
 
-        lax.fori_loop(0, rows // chunk, step, 0)
+        lax.fori_loop(0, rows // chunk, step, 0, unroll=True)
         act = act_ref[0, slot]
         mask = frame_mask(counts_ref, k, frame_of(slot))
         gram[...] += t_dot(act, act) * mask
@@ -513,7 +513,7 @@
                 count,
                 chunk,
             )
-            totals = lax.fori_loop(0, steps, step, totals)
+            totals = lax.fori_loop(0, steps, step, totals, unroll=True)
         for i in range(27):
             total[i, :, cols] = totals[i]
 
@@ -645,7 +645,7 @@
             grad_ref[0, pl.ds(pl.multiple_of(slot * rows + start, chunk), chunk), :] = grad.astype(bf16)
             return 0
 
-        lax.fori_loop(0, rows // chunk, step, 0)
+        lax.fori_loop(0, rows // chunk, step, 0, unroll=True)
     product[...] += t_dot(grad_ref[0], xpad[...])
 
     @pl.when(k == pl.num_programs(0) - 1)

time: 150 us -> 147 us (0.980)
  Pallas kernels: 59.1 us -> 55.6 us
    pallas_call x28, Pallas kernels: 50.7 us -> 47.2 us  [call(): pl.pallas_call(kernel, name=name, out_shape=[jax.ShapeDtypeStruct(s, d) f...]
  transfers between devices with their start and end apart: 51 -> 51, of which waited for: 14 -> 14; matrix products, arithmetic and copies ran while one was open for 3% -> 3% of each run, Pallas kernels for 25% -> 24%
where the time goes in v5:
time: 147 us
  starting transfers between devices  65.8 us (45%)
  Pallas kernels  55.6 us (38%)
  waiting for transfers between devices  16.3 us (11%)
  local copies, waits for them, and re-layouts  8.16 us (6%)
    pallas_call x28, Pallas kernels, call(): pl.pallas_call(kernel, name=name, out_shape=[jax.ShapeDtypeStruct(s, d) f...  47.2 us
    ppermute x21, starting transfers between devices, over_chips(): lax.ppermute(pieces[z], 'space', [(i, i ^ 2 * z) for i in range(2 * size)])  33.6 us
    ppermute x11, starting transfers between devices, core_swap(): lax.ppermute(values, 'space', [(i, i ^ 1) for i in range(lax.axis_size('s...  11.5 us
    ppermute x21, waiting for transfers between devices, over_chips(): lax.ppermute(pieces[z], 'space', [(i, i ^ 2 * z) for i in range(2 * size)])  9.73 us
    unnamed x32, local copies, waits for them, and re-layouts  8.16 us
    ppermute x8, starting transfers between devices, clip_swap(): lax.ppermute(values, 'clip', [(i, i ^ bit) for i in range(lax.axis_size('...  7.3 us
    ppermute x4, starting transfers between devices, swap_neighbours(): lax.ppermute(to_core, 'space', core)  6.31 us
    ppermute x11, waiting for transfers between devices, core_swap(): lax.ppermute(values, 'space', [(i, i ^ 1) for i in range(lax.axis_size('s...  4.52 us
  transfers between devices with their start and end apart: 51, of which 14 were waited for; matrix products, arithmetic and copies ran while one was open for 3% of the time, Pallas kernels for 24%

profile of v5, /device:TPU:0, one launch (start us, length us, event | category | flops | bytes accessed | tf_op | source)
XLA Modules:
  0.0 147.0 jit_solution(7072744267310634960)
XLA Ops:
  0.7 3.0 %copy.31.x_ref = bf16[4,2,14,14,1024]{4,3,2,1,0:T(8,128)(2,1)S(1)} copy(bf16[4,2,14,14,1024]{4,1,3,2,0:T(2,128)(2,1)} %param.16) | data formatting | bytes 6422528 | tf_op args[0]
  3.8 3.0 %first.1 = (f32[4,2,224,256]{3,2,1,0:T(8,128)S(1)}, bf16[4,224,256]{2,1,0:T(8,128)(2,1)S(1)}, bf16[4,224,256]{2,1,0:T(8,128)(2,1)S(1)}, f32[4,56,1024]{2,1,0:T(8,128)S(1)}) custom-call(s32[4]{0:T(128)S(1)} %copy-done.8, bf16[4,2,14,14,1024]{4,3,2,1,0:T(8,128)(2,1)S(1)} %copy.31.x_ref, bf16[1024,256]{1,0:T(8,128)(2,1)S(1)} %copy-done.4), custom_call_target="tpu_custom_call" | custom-call | bytes 18020000 | tf_op jit(solution)/shard_map/first/pallas_call | solution.py:787
  7.6 4.4 %collective-permute-start.1 = (bf16[4,224,256]{2,1,0:T(8,128)(2,1)S(1)}, bf16[4,224,256]{2,1,0:T(8,128)(2,1)S(1)}, u32[]{:S(2)}, u32[]{:S(2)}) collective-permute-start(bf16[4,224,256]{2,1,0:T(8,128)(2,1)S(1)} %get-tuple-element.146.oc_ref), channel_id=1, source_target_pairs={{0,1},{1,0},{2,3},{3,2},{4,5},{5,4},{6,7},{7,6},{8,9},{9,8},{10,11... | collective-permute-start | bytes 1376264 | tf_op jit(solution)/shard_map/ppermute | solution.py:817
  12.0 2.5 %mid_own.1.part_ref = f32[4,2,224,256]{3,2,1,0:T(8,128)S(1)} custom-call(bf16[4,224,256]{2,1,0:T(8,128)(2,1)S(1)} %get-tuple-element.145.oz_ref, bf16[4,224,256]{2,1,0:T(8,128)(2,1)S(1)} %get-tuple-element.146.oc_ref, f32[27,256]{1,0:T(8,128)S(1)} %get-tuple-element.147.taps_ref), custom_call_target="tpu_custom_call" | custom-call | bytes 17000000 | tf_op jit(solution)/shard_map/mid_own/pallas_call | solution.py:787
  14.7 4.6 %mid.1 = (f32[4,2,224,256]{3,2,1,0:T(8,128)S(1)}, bf16[4,2,224,256]{3,2,1,0:T(8,128)(2,1)S(1)}, bf16[224,256]{1,0:T(8,128)(2,1)S(1)}, f32[224,1024]{1,0:T(8,128)...) custom-call(s32[4]{0:T(128)S(1)} %copy-done.8, ...), custom_call_target="tpu_custom_call" | custom-call | bytes 29240000 | tf_op jit(solution)/shard_map/mid/pallas_call | solution.py:787
  19.3 3.5 %collective-permute-start.2 = (f32[2,1024]{1,0:T(2,128)S(1)}, f32[2,1024]{1,0:T(2,128)S(1)}, u32[]{:S(2)}, u32[]{:S(2)}) collective-permute-start(f32[2,1024]{1,0:T(2,128)S(1)} %get-tuple-element.148.one_ref), channel_id=1, source_target_pairs={{0,1},{1,0},{2,3},{3,2},{4,5},{5,4},{6,7},{7,6},{8,9},{9,8},{10,11... | collective-permute-start | bytes 24584 | tf_op jit(solution)/shard_map/ppermute | solution.py:835
  25.6 2.6 %collective-permute-start.4 = (f32[2,1024]{1,0:T(2,128)S(1)}, f32[2,1024]{1,0:T(2,128)S(1)}, u32[]{:S(2)}, u32[]{:S(2)}) collective-permute-start(f32[2,1024]{1,0:T(2,128)S(1)} %add.4), channel_id=1, source_target_pairs={{0,4},{1,5},{2,6},{3,7},{4,0},{5,1},{6,2},{7,3},{8,12},{9,13},{10,... | collective-permute-start | bytes 24584 | tf_op jit(solution)/shard_map/ppermute | solution.py:1000
  30.1 3.5 %collective-permute-done.5 = f32[2,1024]{1,0:T(2,128)S(1)} collective-permute-done((f32[2,1024]{1,0:T(2,128)S(1)}, f32[2,1024]{1,0:T(2,128)S(1)}, u32[]{:S(2)}, u32[]{:S(2)}) %collective-permute-start.5) | collective-permute-done | bytes 8224 | tf_op jit(solution)/shard_map/ppermute | solution.py:1000
  37.1 2.4 %late_mid.1 = (f32[4,56,512]{2,1,0:T(8,128)S(1)}, bf16[224,512]{1,0:T(8,128)(2,1)S(1)}, bf16[224,2048]{1,0:T(8,128)(2,1)S(1)}, f32[2,2048]{1,0:T(2,128)S(1)}) custom-call(s32[4]{0:T(128)S(1)} %copy-done.8, bf16[4,56,512]{2,1,0:T(8,128)(2,1)S(1)} %collective-permute-done.6.rz_ref, bf16[4,56,512]{2,1,0:T(8,128)(2,1)S(1)} %get-tuple-element.151.own_ref, ...), custom_call_target="tpu_custom_call" | custom-call | bytes 15980000 | tf_op jit(solution)/shard_map/late_mid/pallas_call | solution.py:787
  39.6 3.5 %collective-permute-start.8 = (f32[2,2048]{1,0:T(2,128)S(1)}, f32[2,2048]{1,0:T(2,128)S(1)}, u32[]{:S(2)}, u32[]{:S(2)}) collective-permute-start(f32[2,2048]{1,0:T(2,128)S(1)} %get-tuple-element.153.one_ref), channel_id=1, source_target_pairs={{0,1},{1,0},{2,3},{3,2},{4,5},{5,4},{6,7},{7,6},{8,9},{9,8},{10,11... | collective-permute-start | bytes 49160 | tf_op jit(solution)/shard_map/ppermute | solution.py:835
  51.9 2.9 %post.1 = (f32[2,2048]{1,0:T(2,128)S(1)}, f32[2,2048]{1,0:T(2,128)S(1)}, f32[4,2048]{1,0:T(4,128)S(1)}, f32[4,56,2048]{2,1,0:T(8,128)S(1)}, bf16[4,56,2048]{2,1,0:T(8,128)(2,1)S(1)}) custom-call(s32[4]{0:T(128)S(1)} %copy-done.8, f32[1,2,2048]{2,1,0:T(2,128)S(1)} %bitcast.51, f32[1,2,2048]{2,1,0:T(2,128)S(1)} %bitcast.67, f32[1,2,2048]{2,1,0:T(2,128)S(1)} %bitcast.68, ...), custom_call_target="tpu_custom_call" | custom-call | bytes 20400000 | tf_op jit(solution)/shard_map/post/pallas_call | solution.py:787
  56.6 2.4 %collective-permute-start.14 = (f32[2,2048]{1,0:T(2,128)S(1)}, f32[2,2048]{1,0:T(2,128)S(1)}, u32[]{:S(2)}, u32[]{:S(2)}) collective-permute-start(f32[2,2048]{1,0:T(2,128)S(1)} %add.6), channel_id=1, source_target_pairs={{0,4},{1,5},{2,6},{3,7},{4,0},{5,1},{6,2},{7,3},{8,12},{9,13},{10,... | collective-permute-start | bytes 49160 | tf_op jit(solution)/shard_map/ppermute | solution.py:1000
  61.0 4.1 %skip_sums.1 = (f32[224,1024]{1,0:T(8,128)S(1)}, bf16[2,2,32,2048]{3,2,1,0:T(8,128)(2,1)S(1)}, bf16[2,2,32,2048]{3,2,1,0:T(8,128)(2,1)S(1)}, bf16[2,2,32,2048]{3...) custom-call(bf16[224,1024]{1,0:T(8,128)(2,1)S(1)} %get-tuple-element.155.entry_ref.left_ref, ...), custom_call_target="tpu_custom_call" | custom-call | bytes 23800000 | tf_op jit(solution)/shard_map/skip_sums/pallas_call | solution.py:916
  75.5 2.3 %late_back.1 = (bf16[224,512]{1,0:T(8,128)(2,1)S(1)}, f32[4,56,1024]{2,1,0:T(8,128)S(1)}, f32[4,1024]{1,0:T(4,128)S(1)}) custom-call(s32[4]{0:T(128)S(1)} %copy-done.8, bf16[4,56,512]{2,1,0:T(8,128)(2,1)S(1)} %collective-permute-done.18.rz_ref, bf16[4,56,512]{2,1,0:T(8,128)(2,1)S(1)} %get-tuple-element.164.grad_ref.own_ref, ...), custom_call_target="tpu_custom_call" | custom-call | bytes 17000000 | tf_op jit(solution)/shard_map/late_back/pallas_call | solution.py:787
  85.7 2.2 %up_down_sums.1 = (bf16[2,2,24,2048]{3,2,1,0:T(8,128)(2,1)S(1)}, bf16[2,2,24,2048]{3,2,1,0:T(8,128)(2,1)S(1)}, bf16[2,2,24,2048]{3,2,1,0:T(8,128)(2,1)S(1)}, bf16[2,2,24,2048]{3,2,1,0:T(8,128)(2,1)S(1)}) custom-call(bf16[224,512]{1,0:T(8,128)(2,1)S(1)} %get-tuple-element.182.act_ref, bf16[224,512]{1,0:T(8,128)(2,1)S(1)} %collective-permute-done.26.act_other_ref, ...), custom_call_target="tpu_custom_call" | custom-call | bytes 18700000 | tf_op jit(solution)/shard_map/up_down_sums/pallas_call | solution.py:974
  89.2 4.0 %third_grad.1 = (bf16[4,224,256]{2,1,0:T(8,128)(2,1)S(1)}, bf16[4,224,256]{2,1,0:T(8,128)(2,1)S(1)}, bf16[256,1024]{1,0:T(8,128)(2,1)S(1)}, f32[4,400]{1,0:T(4,128)}) custom-call(s32[4]{0:T(128)S(1)} %copy-done.8, f32[1,4,1024]{2,1,0:T(4,128)S(1)} %bitcast.49, f32[1,4,1024]{2,1,0:T(4,128)S(1)} %bitcast.61, f32[1,4,1024]{2,1,0:T(4,128)S(1)} %bitcast.62, ...), custom_call_target="tpu_custom_call" | custom-call | bytes 22780000 | tf_op jit(solution)/shard_map/third_grad/pallas_call | solution.py:787
  95.9 4.6 %third_taps.1 = (f32[4,4,8,1792]{3,2,1,0:T(8,128)S(1)}, bf16[4,4,8,1792]{3,2,1,0:T(8,128)(2,1)S(1)}) custom-call(bf16[4,224,256]{2,1,0:T(8,128)(2,1)S(1)} %collective-permute-done.rz_ref, bf16[4,224,256]{2,1,0:T(8,128)(2,1)S(1)} %get-tuple-element.145.oz_ref, bf16[4,224,256]{2,1,0:T(8,128)(2,1)S(1)} %get-tuple-element.146.oc_ref, ...), custom_call_target="tpu_custom_call" | custom-call | bytes 26180000 | tf_op jit(solution)/shard_map/third_taps/pallas_call | solution.py:787
  103.9 8.2 %first_grad.1 = (bf16[4,448,256]{2,1,0:T(8,128)(2,1)S(1)}, f32[4,4,32,256]{3,2,1,0:T(8,128)S(1)}, bf16[4,4,32,256]{3,2,1,0:T(8,128)(2,1)S(1)}) custom-call(s32[4]{0:T(128)S(1)} %copy-done.8, bf16[4,224,256]{2,1,0:T(8,128)(2,1)S(1)} %collective-permute-done.29.rz_ref, bf16[4,224,256]{2,1,0:T(8,128)(2,1)S(1)} %get-tuple-element.199.gz_ref, ...), custom_call_target="tpu_custom_call" | custom-call | bytes 36380000 | tf_op jit(solution)/shard_map/first_grad/pallas_call | solution.py:787
  113.7 2.3 %collective-permute-start.43 = (bf16[32,2048]{1,0:T(8,128)(2,1)S(1)}, bf16[32,2048]{1,0:T(8,128)(2,1)S(1)}, u32[]{:S(2)}, u32[]{:S(2)}) collective-permute-start(bf16[32,2048]{1,0:T(8,128)(2,1)S(1)} %get-tuple-element.244), channel_id=1, source_target_pairs={{0,4},{1,5},{2,6},{3,7},{4,0},{5,1},{6,2},{7,3},{8,12},{9,13},{10,... | collective-permute-start | bytes 393224 | tf_op jit(solution)/shard_map/ppermute | solution.py:1000
  119.5 2.7 %clip_grad.1 = bf16[4,2,14,14,1024]{4,3,2,1,0:T(8,128)(2,1)S(1)} custom-call(bf16[4,448,256]{2,1,0:T(8,128)(2,1)S(1)} %get-tuple-element.214.grad_ref, bf16[1024,256]{1,0:T(8,128)(2,1)S(1)} %copy-done.4, f32[4,56,1024]{2,1,0:T(8,128)S(1)} %get-tuple-element.192.entry_grad_ref), custom_call_target="tpu_custom_call" | custom-call | bytes 18700000 | tf_op jit(solution)/shard_map/clip_grad/pallas_call | solution.py:787
  124.5 2.2 %collective-permute-done.44.refs_3_ = bf16[32,2048]{1,0:T(8,128)(2,1)S(1)} collective-permute-done((bf16[32,2048]{1,0:T(8,128)(2,1)S(1)}, bf16[32,2048]{1,0:T(8,128)(2,1)S(1)}, u32[]{:S(2)}, u32[]{:S(2)}) %collective-permute-start.44) | collective-permute-done | bytes 131104 | tf_op jit(solution)/shard_map/ppermute | solution.py:1000
  128.3 2.6 %collective-permute-start.48 = (bf16[24,2048]{1,0:T(8,128)(2,1)S(1)}, bf16[24,2048]{1,0:T(8,128)(2,1)S(1)}, u32[]{:S(2)}, u32[]{:S(2)}) collective-permute-start(bf16[24,2048]{1,0:T(8,128)(2,1)S(1)} %get-tuple-element.264), channel_id=1, source_target_pairs={{0,2},{1,3},{2,0},{3,1},{4,6},{5,7},{6,4},{7,5},{8,10},{9,11},{10,... | collective-permute-start | bytes 294920 | tf_op jit(solution)/shard_map/ppermute | solution.py:1000
  136.6 3.4 %collective-permute-start.46 = (bf16[8,2816]{1,0:T(8,128)(2,1)S(1)}, bf16[8,2816]{1,0:T(8,128)(2,1)S(1)}, u32[]{:S(2)}, u32[]{:S(2)}) collective-permute-start(bf16[8,2816]{1,0:T(8,128)(2,1)S(1)} %get-tuple-element.257), channel_id=1, source_target_pairs={{0,4},{1,5},{2,6},{3,7},{4,0},{5,1},{6,2},{7,3},{8,12},{9,13},{10,... | collective-permute-start | bytes 135176 | tf_op jit(solution)/shard_map/ppermute | solution.py:1000
  140.0 5.0 %copy.33 = bf16[4,2,14,14,1024]{4,1,3,2,0:T(2,128)(2,1)} copy(bf16[4,2,14,14,1024]{4,3,2,1,0:T(8,128)(2,1)S(1)} %clip_grad.1) | data formatting | bytes 6422528
  (141 shorter events, 63.8 us)
Async XLA Ops:
  6.8 7.9 %collective-permute-start = (bf16[4,224,256]{2,1,0:T(8,128)(2,1)S(1)}, bf16[4,224,256]{2,1,0:T(8,128)(2,1)S(1)}, u32[]{:S(2)}, u32[]{:S(2)}) collective-permute-start(bf16[4,224,256]{2,1,0:T(8,128)(2,1)S(1)} %get-tuple-element.145.oz_ref), channel_id=1, source_target_pairs={{1,2},{2,1},{3,4},{4,3},{5,6},{6,5},{9,10},{10,9},{11,12},{12,11},... | collective-permute-start | bytes 1376264 | tf_op jit(solution)/shard_map/ppermute | solution.py:817
  56.6 8.5 %collective-permute-start.13 = (f32[2,2048]{1,0:T(2,128)S(1)}, f32[2,2048]{1,0:T(2,128)S(1)}, u32[]{:S(2)}, u32[]{:S(2)}) collective-permute-start(f32[2,2048]{1,0:T(2,128)S(1)} %add.6), channel_id=1, source_target_pairs={{0,2},{1,3},{2,0},{3,1},{4,6},{5,7},{6,4},{7,5},{8,10},{9,11},{10,... | collective-permute-start | bytes 49160 | tf_op jit(solution)/shard_map/ppermute | solution.py:1000
  56.6 8.5 %collective-permute-start.14 = (f32[2,2048]{1,0:T(2,128)S(1)}, f32[2,2048]{1,0:T(2,128)S(1)}, u32[]{:S(2)}, u32[]{:S(2)}) collective-permute-start(f32[2,2048]{1,0:T(2,128)S(1)} %add.6), channel_id=1, source_target_pairs={{0,4},{1,5},{2,6},{3,7},{4,0},{5,1},{6,2},{7,3},{8,12},{9,13},{10,... | collective-permute-start | bytes 49160 | tf_op jit(solution)/shard_map/ppermute | solution.py:1000
  66.7 16.9 %collective-permute-start.28 = (bf16[224,2048]{1,0:T(8,128)(2,1)S(1)}, bf16[224,2048]{1,0:T(8,128)(2,1)S(1)}, u32[]{:S(2)}, u32[]{:S(2)}) collective-permute-start(bf16[224,2048]{1,0:T(8,128)(2,1)S(1)} %get-tuple-element.184.sum_ref), channel_id=1, source_target_pairs={{0,1},{1,0},{2,3},{3,2},{4,5},{5,4},{6,7},{7,6},{8,9},{9,8},{10,11... | collective-permute-start | bytes 2752520 | tf_op jit(solution)/shard_map/ppermute | solution.py:835
  66.8 21.1 %collective-permute-start.24 = (bf16[2,2,32,2048]{3,2,1,0:T(8,128)(2,1)S(1)}, bf16[2,2,32,2048]{3,2,1,0:T(8,128)(2,1)S(1)}, u32[]{:S(2)}, u32[]{:S(2)}) collective-permute-start(bf16[2,2,32,2048]{3,2,1,0:T(8,128)(2,1)S(1)} %get-tuple-element.179), channel_id=1, source_target_pairs={{0,8},{8,0},{16,24},{24,16},{1,9},{9,1},{17,25},{25,17},{2,10},{10... | collective-permute-start | bytes 1572872 | tf_op jit(solution)/shard_map/ppermute | solution.py:865
  68.4 19.6 %collective-permute-start.25 = (bf16[2,2,32,2048]{3,2,1,0:T(8,128)(2,1)S(1)}, bf16[2,2,32,2048]{3,2,1,0:T(8,128)(2,1)S(1)}, u32[]{:S(2)}, u32[]{:S(2)}) collective-permute-start(bf16[2,2,32,2048]{3,2,1,0:T(8,128)(2,1)S(1)} %get-tuple-element.181), channel_id=1, source_target_pairs={{0,16},{8,24},{16,0},{24,8},{1,17},{9,25},{17,1},{25,9},{2,18},{10... | collective-permute-start | bytes 1572872 | tf_op jit(solution)/shard_map/ppermute | solution.py:865
  94.2 9.8 %collective-permute-start.30 = (bf16[4,224,256]{2,1,0:T(8,128)(2,1)S(1)}, bf16[4,224,256]{2,1,0:T(8,128)(2,1)S(1)}, u32[]{:S(2)}, u32[]{:S(2)}) collective-permute-start(bf16[4,224,256]{2,1,0:T(8,128)(2,1)S(1)} %get-tuple-element.200.gc_ref), channel_id=1, source_target_pairs={{0,1},{1,0},{2,3},{3,2},{4,5},{5,4},{6,7},{7,6},{8,9},{9,8},{10,11... | collective-permute-start | bytes 1376264 | tf_op jit(solution)/shard_map/ppermute | solution.py:817
  94.8 8.3 %collective-permute-start.31 = (bf16[2,32,2048]{2,1,0:T(8,128)(2,1)S(1)}, bf16[2,32,2048]{2,1,0:T(8,128)(2,1)S(1)}, u32[]{:S(2)}, u32[]{:S(2)}) collective-permute-start(bf16[2,32,2048]{2,1,0:T(8,128)(2,1)S(1)} %get-tuple-element.205), channel_id=1, source_target_pairs={{0,16},{8,24},{16,0},{24,8},{1,17},{9,25},{17,1},{25,9},{2,18},{10... | collective-permute-start | bytes 786440 | tf_op jit(solution)/shard_map/ppermute | solution.py:865
  95.3 8.3 %collective-permute-start.32 = (bf16[2,32,2048]{2,1,0:T(8,128)(2,1)S(1)}, bf16[2,32,2048]{2,1,0:T(8,128)(2,1)S(1)}, u32[]{:S(2)}, u32[]{:S(2)}) collective-permute-start(bf16[2,32,2048]{2,1,0:T(8,128)(2,1)S(1)} %get-tuple-element.207), channel_id=1, source_target_pairs={{0,8},{8,0},{16,24},{24,16},{1,9},{9,1},{17,25},{25,17},{2,10},{10... | collective-permute-start | bytes 786440 | tf_op jit(solution)/shard_map/ppermute | solution.py:865
  100.5 18.4 %collective-permute-start.34 = (bf16[4,4,8,1792]{3,2,1,0:T(8,128)(2,1)S(1)}, bf16[4,4,8,1792]{3,2,1,0:T(8,128)(2,1)S(1)}, u32[]{:S(2)}, u32[]{:S(2)}) collective-permute-start(bf16[4,4,8,1792]{3,2,1,0:T(8,128)(2,1)S(1)} %get-tuple-element.219), channel_id=1, source_target_pairs={{0,1},{1,0},{2,3},{3,2},{4,5},{5,4},{6,7},{7,6},{8,9},{9,8},{10,11... | collective-permute-start | bytes 1376264 | tf_op jit(solution)/shard_map/ppermute | solution.py:835
  102.0 11.7 %collective-permute-start.38 = (bf16[2,2,24,2048]{3,2,1,0:T(8,128)(2,1)S(1)}, bf16[2,2,24,2048]{3,2,1,0:T(8,128)(2,1)S(1)}, u32[]{:S(2)}, u32[]{:S(2)}) collective-permute-start(bf16[2,2,24,2048]{3,2,1,0:T(8,128)(2,1)S(1)} %get-tuple-element.228), channel_id=1, source_target_pairs={{0,8},{8,0},{16,24},{24,16},{1,9},{9,1},{17,25},{25,17},{2,10},{10... | collective-permute-start | bytes 1179656 | tf_op jit(solution)/shard_map/ppermute | solution.py:865
  103.1 12.9 %collective-permute-start.39 = (bf16[2,2,24,2048]{3,2,1,0:T(8,128)(2,1)S(1)}, bf16[2,2,24,2048]{3,2,1,0:T(8,128)(2,1)S(1)}, u32[]{:S(2)}, u32[]{:S(2)}) collective-permute-start(bf16[2,2,24,2048]{3,2,1,0:T(8,128)(2,1)S(1)} %get-tuple-element.230), channel_id=1, source_target_pairs={{0,16},{8,24},{16,0},{24,8},{1,17},{9,25},{17,1},{25,9},{2,18},{10... | collective-permute-start | bytes 1179656 | tf_op jit(solution)/shard_map/ppermute | solution.py:865
  112.3 10.1 %collective-permute-start.42 = (bf16[32,2048]{1,0:T(8,128)(2,1)S(1)}, bf16[32,2048]{1,0:T(8,128)(2,1)S(1)}, u32[]{:S(2)}, u32[]{:S(2)}) collective-permute-start(bf16[32,2048]{1,0:T(8,128)(2,1)S(1)} %get-tuple-element.243), channel_id=1, source_target_pairs={{0,2},{1,3},{2,0},{3,1},{4,6},{5,7},{6,4},{7,5},{8,10},{9,11},{10,... | collective-permute-start | bytes 393224 | tf_op jit(solution)/shard_map/ppermute | solution.py:1000
  113.7 10.3 %collective-permute-start.43 = (bf16[32,2048]{1,0:T(8,128)(2,1)S(1)}, bf16[32,2048]{1,0:T(8,128)(2,1)S(1)}, u32[]{:S(2)}, u32[]{:S(2)}) collective-permute-start(bf16[32,2048]{1,0:T(8,128)(2,1)S(1)} %get-tuple-element.244), channel_id=1, source_target_pairs={{0,4},{1,5},{2,6},{3,7},{4,0},{5,1},{6,2},{7,3},{8,12},{9,13},{10,... | collective-permute-start | bytes 393224 | tf_op jit(solution)/shard_map/ppermute | solution.py:1000
  116.0 10.7 %collective-permute-start.44 = (bf16[32,2048]{1,0:T(8,128)(2,1)S(1)}, bf16[32,2048]{1,0:T(8,128)(2,1)S(1)}, u32[]{:S(2)}, u32[]{:S(2)}) collective-permute-start(bf16[32,2048]{1,0:T(8,128)(2,1)S(1)} %get-tuple-element.245), channel_id=1, source_target_pairs={{0,6},{1,7},{2,4},{3,5},{4,2},{5,3},{6,0},{7,1},{8,14},{9,15},{10,... | collective-permute-start | bytes 393224 | tf_op jit(solution)/shard_map/ppermute | solution.py:1000
  117.4 10.7 %collective-permute-start.40 = (bf16[2,24,2048]{2,1,0:T(8,128)(2,1)S(1)}, bf16[2,24,2048]{2,1,0:T(8,128)(2,1)S(1)}, u32[]{:S(2)}, u32[]{:S(2)}) collective-permute-start(bf16[2,24,2048]{2,1,0:T(8,128)(2,1)S(1)} %get-tuple-element.236), channel_id=1, source_target_pairs={{0,16},{8,24},{16,0},{24,8},{1,17},{9,25},{17,1},{25,9},{2,18},{10... | collective-permute-start | bytes 589832 | tf_op jit(solution)/shard_map/ppermute | solution.py:865
  118.9 9.2 %collective-permute-start.41 = (bf16[2,24,2048]{2,1,0:T(8,128)(2,1)S(1)}, bf16[2,24,2048]{2,1,0:T(8,128)(2,1)S(1)}, u32[]{:S(2)}, u32[]{:S(2)}) collective-permute-start(bf16[2,24,2048]{2,1,0:T(8,128)(2,1)S(1)} %get-tuple-element.238), channel_id=1, source_target_pairs={{0,8},{8,0},{16,24},{24,16},{1,9},{9,1},{17,25},{25,17},{2,10},{10... | collective-permute-start | bytes 589832 | tf_op jit(solution)/shard_map/ppermute | solution.py:865
  122.4 10.6 %collective-permute-start.35 = (bf16[4,8,2816]{2,1,0:T(8,128)(2,1)S(1)}, bf16[4,8,2816]{2,1,0:T(8,128)(2,1)S(1)}, u32[]{:S(2)}, u32[]{:S(2)}) collective-permute-start(bf16[4,8,2816]{2,1,0:T(8,128)(2,1)S(1)} %get-tuple-element.221), channel_id=1, source_target_pairs={{0,8},{8,0},{16,24},{24,16},{1,9},{9,1},{17,25},{25,17},{2,10},{10... | collective-permute-start | bytes 540680 | tf_op jit(solution)/shard_map/ppermute | solution.py:994
  123.9 10.4 %collective-permute-start.36 = (bf16[4,8,2816]{2,1,0:T(8,128)(2,1)S(1)}, bf16[4,8,2816]{2,1,0:T(8,128)(2,1)S(1)}, u32[]{:S(2)}, u32[]{:S(2)}) collective-permute-start(bf16[4,8,2816]{2,1,0:T(8,128)(2,1)S(1)} %get-tuple-element.222), channel_id=1, source_target_pairs={{0,16},{8,24},{16,0},{24,8},{1,17},{9,25},{17,1},{25,9},{2,18},{10... | collective-permute-start | bytes 540680 | tf_op jit(solution)/shard_map/ppermute | solution.py:994
  128.3 11.6 %collective-permute-start.48 = (bf16[24,2048]{1,0:T(8,128)(2,1)S(1)}, bf16[24,2048]{1,0:T(8,128)(2,1)S(1)}, u32[]{:S(2)}, u32[]{:S(2)}) collective-permute-start(bf16[24,2048]{1,0:T(8,128)(2,1)S(1)} %get-tuple-element.264), channel_id=1, source_target_pairs={{0,2},{1,3},{2,0},{3,1},{4,6},{5,7},{6,4},{7,5},{8,10},{9,11},{10,... | collective-permute-start | bytes 294920 | tf_op jit(solution)/shard_map/ppermute | solution.py:1000
  130.9 14.1 %collective-permute-start.49 = (bf16[24,2048]{1,0:T(8,128)(2,1)S(1)}, bf16[24,2048]{1,0:T(8,128)(2,1)S(1)}, u32[]{:S(2)}, u32[]{:S(2)}) collective-permute-start(bf16[24,2048]{1,0:T(8,128)(2,1)S(1)} %get-tuple-element.265), channel_id=1, source_target_pairs={{0,4},{1,5},{2,6},{3,7},{4,0},{5,1},{6,2},{7,3},{8,12},{9,13},{10,... | collective-permute-start | bytes 294920 | tf_op jit(solution)/shard_map/ppermute | solution.py:1000
  132.9 12.1 %collective-permute-start.50 = (bf16[24,2048]{1,0:T(8,128)(2,1)S(1)}, bf16[24,2048]{1,0:T(8,128)(2,1)S(1)}, u32[]{:S(2)}, u32[]{:S(2)}) collective-permute-start(bf16[24,2048]{1,0:T(8,128)(2,1)S(1)} %get-tuple-element.266), channel_id=1, source_target_pairs={{0,6},{1,7},{2,4},{3,5},{4,2},{5,3},{6,0},{7,1},{8,14},{9,15},{10,... | collective-permute-start | bytes 294920 | tf_op jit(solution)/shard_map/ppermute | solution.py:1000
  134.4 11.4 %collective-permute-start.45 = (bf16[8,2816]{1,0:T(8,128)(2,1)S(1)}, bf16[8,2816]{1,0:T(8,128)(2,1)S(1)}, u32[]{:S(2)}, u32[]{:S(2)}) collective-permute-start(bf16[8,2816]{1,0:T(8,128)(2,1)S(1)} %get-tuple-element.256), channel_id=1, source_target_pairs={{0,2},{1,3},{2,0},{3,1},{4,6},{5,7},{6,4},{7,5},{8,10},{9,11},{10,... | collective-permute-start | bytes 135176 | tf_op jit(solution)/shard_map/ppermute | solution.py:1000
  136.6 9.5 %collective-permute-start.46 = (bf16[8,2816]{1,0:T(8,128)(2,1)S(1)}, bf16[8,2816]{1,0:T(8,128)(2,1)S(1)}, u32[]{:S(2)}, u32[]{:S(2)}) collective-permute-start(bf16[8,2816]{1,0:T(8,128)(2,1)S(1)} %get-tuple-element.257), channel_id=1, source_target_pairs={{0,4},{1,5},{2,6},{3,7},{4,0},{5,1},{6,2},{7,3},{8,12},{9,13},{10,... | collective-permute-start | bytes 135176 | tf_op jit(solution)/shard_map/ppermute | solution.py:1000
  (42 other events, 308.5 us)
